TPU v7x, 128 devices: a whole 4x4x4 slice. The times are simulated.
128 devices in a mesh: tx: 8 (over z, x_lo), ty: 4 (over y), mem: 4 (over x_hi, core).
Axes of the slice: x: 4 (x_hi: 2, x_lo: 2; x = x_hi * 2 + x_lo), y: 4, z: 4, core: 2. Of those that a mesh axis runs over, the one named last changes fastest.
Arguments:
- alpha: float32 [64, 128, 2560], P('tx', 'ty', 'mem'), may hold values from -6 to 6
- lv_sqrt: float32 [32, 32], replicated, may hold values from -1 to 1
- ens_pert: bfloat16 [80, 32, 256, 512], P('mem', None, 'tx', 'ty'), may hold values from -0.625 to 0.625
- bg_sigma: float32 [32, 256, 512], P(None, 'tx', 'ty'), may hold values from 0.1 to 1
- static_ctrl: float32 [32, 256, 512], P(None, 'tx', 'ty'), may hold values from -6 to 6
- obs_owner: int32 [1048576, 1], P(('tx', 'ty', 'mem')), may hold values from 0 to 31; in each aligned block of 8192 rows (0 to 8191, 8192 to 16383, ...) at most 512 rows name the same one
- obs_column: int32 [1048576], P(('tx', 'ty', 'mem')), may hold values from 0 to 3966, as said below
- obs_level: int32 [1048576], P(('tx', 'ty', 'mem')), may hold values from 0 to 30
- obs_frac: float32 [3, 1048576], P(None, ('tx', 'ty', 'mem')), may hold values from 0 to 1
- innovation: float32 [1048576], P(('tx', 'ty', 'mem')), may hold values from -6 to 6
- obs_rinv: float32 [1048576], P(('tx', 'ty', 'mem')), may hold values from 0.5 to 8
- obs_count: int32 [128], P(('tx', 'ty', 'mem')), may hold values from 4096 to 8192, as said below
Outputs:
- grad_alpha: float32 [64, 128, 2560], P('tx', 'ty', 'mem')
- grad_static: float32 [32, 256, 512], P(None, 'tx', 'ty')
- departures: float32 [1048576], P(('tx', 'ty', 'mem'))
Inputs may be any that keep to these rules, and one draw needn't show every extreme that they name: `obs_owner`: tile number (tx index) * 4 + (ty index). Among one device's 8192 rows no tile is named more than 512 times, a bound that some block reaches. `obs_column`: i * 128 + j with i < 31 and j < 127. `obs_count`: the live slots of a device are its first ones; some device has all 8192 live and some half of them.
All inputs are finite; a program needn't handle non-finite values.
Results may differ from a plain program's by a relative error of at most 0.0003.
Values sent between devices are 32-bit elements; how exact they have to be, the bound alone decides.
A program may use at most 128 MiB of HBM per device.

v0:
```python
import math

import jax
import jax.numpy as jnp
from jax import lax
from jax.sharding import PartitionSpec as P

RATIO = 4
NSTEP = 4


NU = 0.2


def with_halo(value, sides, width):
    for axis, dim in sides:
        count, length = (lax.axis_size(axis), value.shape[dim])
        up = [(i, (i + 1) % count) for i in range(count)]
        down = [(j, i) for i, j in up]
        last = lax.slice_in_dim(value, length - width, length, axis=dim)
        first = lax.slice_in_dim(value, 0, width, axis=dim)
        before = lax.ppermute(last, axis, up)
        after = lax.ppermute(first, axis, down)
        value = jnp.concatenate([before, value, after], axis=dim)
    return value


def passed_along(value, axis, by):
    count = lax.axis_size(axis)
    return lax.ppermute(value, axis, [(i, (i + by) % count) for i in range(count)])


def diffusion_step(padded):
    center = padded[1:-1, 1:-1]
    near = padded[2:, 1:-1] + padded[:-2, 1:-1] + padded[1:-1, 2:] + padded[1:-1, :-2]
    return center + NU * (near - 4.0 * center)


def diffuse(field):
    for repeat in range(NSTEP):
        padded = with_halo(field, (("tx", 0), ("ty", 1)), 1)
        field = diffusion_step(padded)
    return field


def interpolation_matrix(fine_count, coarse_count):
    index = jnp.arange(fine_count, dtype=jnp.int32)
    lower = index // RATIO
    frac = (index % RATIO).astype(jnp.float32) / RATIO
    target = jnp.arange(coarse_count + 1, dtype=jnp.int32)
    low_part = jnp.where(target[None, :] == lower[:, None], 1.0 - frac[:, None], 0.0)
    high_part = jnp.where(target[None, :] == lower[:, None] + 1, frac[:, None], 0.0)
    return low_part + high_part


def slot_targets(dest, live, groups, capacity):
    onehot = (
        (dest[:, None] == jnp.arange(groups, dtype=jnp.int32)[None, :]) & live[:, None]
    ).astype(jnp.int32)
    rank = jnp.sum((jnp.cumsum(onehot, 0) - onehot) * onehot, 1)
    return jnp.where(live, dest * capacity + rank, groups * capacity)


def stencil(field, incoming):
    highest = lax.Precision.HIGHEST
    level_count, fine_x, fine_y = field.shape
    plane = fine_x * fine_y
    row_count = level_count * fine_x
    matrix = field.reshape(row_count, fine_y)
    width = incoming.shape[1]
    block = math.gcd(width, 2048)
    blocks = incoming.reshape(6, width // block, block).transpose(1, 0, 2)
    row_ids = jnp.arange(row_count, dtype=jnp.int32)[None, :]
    col_ids = jnp.arange(fine_y, dtype=jnp.int32)[None, :]

    def one_block(adjoint_total, item):
        base = item[5].astype(jnp.int32)
        level = base // plane
        column = base % plane
        across = column // fine_y
        along = (column % fine_y)[:, None]
        start = (level * fine_x + across)[:, None]
        frac_x = item[0][:, None]
        frac_y = item[1][:, None]
        frac_l = item[2][:, None]
        row_pick = jnp.where(row_ids == start, (1.0 - frac_x) * (1.0 - frac_l), 0.0)
        row_pick = row_pick + jnp.where(row_ids == start + 1, frac_x * (1.0 - frac_l), 0.0)
        row_pick = row_pick + jnp.where(row_ids == start + fine_x, (1.0 - frac_x) * frac_l, 0.0)
        row_pick = row_pick + jnp.where(row_ids == start + fine_x + 1, frac_x * frac_l, 0.0)
        col_pick = jnp.where(col_ids == along, 1.0 - frac_y, 0.0) + jnp.where(
            col_ids == along + 1, frac_y, 0.0
        )
        picked = jnp.dot(row_pick, matrix, precision=highest, preferred_element_type=jnp.float32)
        hx = jnp.sum(picked * col_pick, 1)
        departure = hx - item[3]
        weighted = item[4] * departure
        spread = weighted[:, None] * col_pick
        adjoint_block = jnp.einsum("nr,nc->rc", row_pick, spread, precision=highest)
        return (adjoint_total + adjoint_block, departure)

    adjoint_rows, departures = lax.scan(
        one_block, jnp.zeros((row_count, fine_y), jnp.float32), blocks
    )
    return (departures.reshape(width), adjoint_rows.reshape(level_count, fine_x, fine_y))


def per_device(
    alpha,
    lv_sqrt,
    ens_pert,
    bg_sigma,
    static_ctrl,
    obs_owner,
    obs_column,
    obs_level,
    obs_frac,
    innovation,
    obs_rinv,
    obs_count,
):
    highest = lax.Precision.HIGHEST
    coarse_x, coarse_y, channel_count = alpha.shape
    members, levels, fine_x, fine_y = ens_pert.shape
    plane = fine_x * fine_y
    alpha_four = alpha.reshape(coarse_x, coarse_y, members, levels)
    vert = jnp.einsum("xykm,lm->xykl", alpha_four, lv_sqrt, precision=highest).reshape(
        coarse_x, coarse_y, channel_count
    )
    smooth = diffuse(vert)
    row_next = passed_along(smooth[0:1], "tx", -1)
    extended = jnp.concatenate([smooth, row_next], 0)
    col_next = passed_along(extended[:, 0:1], "ty", -1)
    extended = jnp.concatenate([extended, col_next], 1)
    matrix_x = interpolation_matrix(fine_x, coarse_x)
    matrix_y = interpolation_matrix(fine_y, coarse_y)
    partial_x = jnp.einsum("xa,abc->xbc", matrix_x, extended, precision=highest)
    fine_grid = jnp.einsum("yb,xbc->cxy", matrix_y, partial_x, precision=highest)
    fine_grid = fine_grid.reshape(members, levels, fine_x, fine_y)
    partial_sum = jnp.sum(fine_grid * ens_pert.astype(jnp.float32), 0)
    tiles_x = lax.axis_size("tx")
    tiles_y = lax.axis_size("ty")
    tiles = tiles_x * tiles_y
    slots = obs_owner.shape[0]
    capacity = 2 * slots // tiles
    owner = obs_owner[:, 0]
    live = jnp.arange(slots, dtype=jnp.int32) < obs_count[0]
    increment = lax.psum(partial_sum, "mem") + bg_sigma * static_ctrl
    width = tiles * capacity
    target = slot_targets(owner, live, tiles, capacity)
    base = (obs_level * plane + obs_column).astype(jnp.float32)
    packed = jnp.stack([obs_frac[0], obs_frac[1], obs_frac[2], innovation, obs_rinv, base], 0)
    outgoing = jnp.zeros((6, width), jnp.float32).at[:, target].set(packed, mode="drop")
    incoming = lax.all_to_all(outgoing, ("tx", "ty"), split_axis=1, concat_axis=1, tiled=True)
    departure, adjoint_part = stencil(increment, incoming)
    returned = lax.all_to_all(departure, ("tx", "ty"), split_axis=0, concat_axis=0, tiled=True)
    departures = jnp.where(live, returned[jnp.minimum(target, width - 1)], 0.0)
    adjoint_grid_values = lax.psum(adjoint_part, "mem")
    grad_static = static_ctrl + bg_sigma * adjoint_grid_values
    scaled = (ens_pert.astype(jnp.float32) * adjoint_grid_values[None]).reshape(
        channel_count, fine_x, fine_y
    )
    back_y = jnp.einsum("yb,cxy->xbc", matrix_y, scaled, precision=highest)
    back_ext = jnp.einsum("xa,xbc->abc", matrix_x, back_y, precision=highest)
    row_in = passed_along(back_ext[-1:], "tx", 1)
    folded = back_ext[:-1].at[0:1].add(row_in)
    col_in = passed_along(folded[:, -1:], "ty", 1)
    folded = folded[:, :-1].at[:, 0:1].add(col_in)
    smooth_back = diffuse(folded).reshape(coarse_x, coarse_y, members, levels)
    mixed = jnp.einsum("xykl,lm->xykm", smooth_back, lv_sqrt, precision=highest)
    grad_alpha = alpha + mixed.reshape(coarse_x, coarse_y, channel_count)
    return (grad_alpha, grad_static, departures)


def solution(mesh):
    placed = (
        P("tx", "ty", "mem"),
        P(),
        P("mem", None, "tx", "ty"),
        P(None, "tx", "ty"),
        P(None, "tx", "ty"),
        P(("tx", "ty", "mem"), None),
        P(("tx", "ty", "mem")),
        P(("tx", "ty", "mem")),
        P(None, ("tx", "ty", "mem")),
        P(("tx", "ty", "mem")),
        P(("tx", "ty", "mem")),
        P(("tx", "ty", "mem")),
    )
    return jax.shard_map(
        per_device,
        mesh=mesh,
        in_specs=placed,
        out_specs=(P("tx", "ty", "mem"), P(None, "tx", "ty"), P(("tx", "ty", "mem"))),
        check_vma=False,
    )
```

profile of v0, /device:TPU:0, one launch (start us, length us, event | category | flops | bytes accessed | tf_op | source)
XLA Modules:
  0.0 646.2 jit_solution(5828478584702400166)
XLA Ops:
  7.2 3.2 reshape.437
  10.5 4.2 fusion.48
  17.2 3.6 collective-permute-start
  22.6 18.7 %reduce-window.6 = s32[32,64,128]{2,1,0:T(8,128)} reduce-window(s32[32,64,128]{2,1,0:T(8,128)} %fusion.61, s32[]{:T(128)} %constant.248.clone.1), window={size=1x1x128 pad=0_0x0_0x127_0}, to_apply=%region_0.1 | reduce-window | flops 33292288 | bytes 2097156 | tf_op jit(solution)/shard_map/reduce-window
  41.2 2.1 slice_reduce_fusion
  43.6 2.5 broadcast_add_fusion.4
  46.1 3.2 copy.64
  49.3 2.2 reshape.465
  51.6 3.1 collective-permute-start.2
  56.4 3.5 collective-permute-done.3
  60.5 4.6 collective-permute-start.4
  73.6 4.1 collective-permute-start.8
  77.8 2.3 collective-permute-done.9
  86.3 4.1 collective-permute-start.12
  90.4 2.3 collective-permute-done.13
  98.6 4.3 collective-permute-start.16
  105.9 3.2 collective-permute-done.17
  109.1 2.3 fusion.50
  111.4 16.8 %fusion.44 = f32[32,640,128]{2,1,0:T(8,128)S(1)} fusion(f32[32,33,640]{2,0,1:T(8,128)S(1)} %fusion.50, f32[128]{0:T(128)S(1)} %get-tuple-element.297, s32[128]{0:T(128)S(1)} %get-tuple-element.296, f32[128]{0:T(128)S(1)} %get-tuple-element.298, s32[128]{0:T(128)S(1)} %get-tuple-element.295), kind=kOutput, calls=%fused_computation.84 | convolution fusion | flops 1038111360 | bytes 13191168 | tf_op jit(solution)/shard_map/yb,xbc->cxy/dot_general | solution.py:137
  128.3 9.7 %fusion.41 = f32[32,32,128]{2,1,0:T(8,128)} fusion(bf16[20,32,32,128]{3,2,1,0:T(8,128)(2,1)} %param.20, f32[20,32,32,128]{3,1,0,2:T(8,128)S(1)} %bitcast.112), kind=kLoop, calls=%fused_computation.80 | loop fusion | flops 7733248 | bytes 16252928 | tf_op jit(solution)/shard_map/reduce_sum | solution.py:139
  138.2 2.7 copy.37
  140.9 24.6 %scatter_custom_fusion = f32[6,16384]{0,1:T(8,128)} fusion(s32[8192]{0:T(1024)S(1)} %bitcast.134, f32[8192,6]{1,0:T(8,128)} %copy.37, f32[]{:T(128)} %constant.254.clone.1), kind=kCustom, calls=%fused_computation.81 | custom fusion | bytes 393728 | tf_op jit(solution)/shard_map/scatter | solution.py:152
  165.5 6.0 copy.38
  171.6 7.6 %all-to-all-start = ((f32[6,32,512]{2,0,1:T(8,128)}), f32[6,32,512]{2,0,1:T(8,128)S(1)}, u32[]{:S(2)}, u32[]{:S(2)}) async-start(f32[6,32,512]{2,0,1:T(8,128)} %copy.38), calls=%async_computation | async-start | bytes 1048576 | tf_op jit(solution)/shard_map/all_to_all | solution.py:153
  179.2 9.9 %all-to-all-done = f32[6,32,512]{2,0,1:T(8,128)S(1)} async-done(((f32[6,32,512]{2,0,1:T(8,128)}), f32[6,32,512]{2,0,1:T(8,128)S(1)}, u32[]{:S(2)}, u32[]{:S(2)}) %all-to-all-start) | async-done | bytes 393248 | tf_op jit(solution)/shard_map/all_to_all | solution.py:153
  190.8 252.3 %while.19 = (s32[]{:T(128)}, f32[1024,128]{1,0:T(8,128)S(1)}, f32[8,2048]{1,0:T(8,128)S(1)}, f32[8,6,2048]{2,0,1:T(8,128)S(1)}, f32[1024,128]{1,0:T(8,128)S(1)},...) while((s32[]{:T(128)}, f32[1024,128]{1,0:T(8,128)S(1)}, ...), condition=%wide.region_8.9_spmd.clone.clone, body=%wide.region_6.8_spmd.clone.clone.sunk | while | flops 6492368896 | bytes 2080995 | solution.py:101
  191.1 14.0 %fusion.165 = f32[2048]{0:T(1024)S(1)} fusion(f32[1024,128]{1,0:T(8,128)S(1)} %get-tuple-element.394, f32[2048]{0:T(1024)S(1)} %get-tuple-element.351, s32[2048]{0:T(1024)S(1)} %get-tuple-element.354, f32[2048]{0:T(1024)S(1)} %get-tuple-element.355, s32[2048]{0:T(1024)S(1)} %get-tuple-element.356, f32[2048]{0:T(1024)S(1)} %get-tuple-element.357, ...), kind=kOutput, calls=%fused_computation.33.clone.1 | convolution fusion | flops 3246127104 | bytes 630784 | tf_op jit(solution)/shard_map/while/body/eval_jaxpr/dot_general | solution.py:93
  205.4 17.0 %fusion.166 = f32[1024,128]{1,0:T(8,128)S(1)} fusion(f32[2048]{0:T(1024)S(1)} %get-tuple-element.351, s32[2048]{0:T(1024)S(1)} %get-tuple-element.354, f32[2048]{0:T(1024)S(1)} %get-tuple-element.355, s32[2048]{0:T(1024)S(1)} %get-tuple-element.356, f32[2048]{0:T(1024)S(1)} %get-tuple-element.357, s32[2048]{0:T(1024)S(1)} %get-tuple-element.358, ...), kind=kOutput, calls=%fused_computation.32.clone.1 | convolution fusion | flops 3246129152 | bytes 1155073 | tf_op jit(solution)/shard_map/while/body/eval_jaxpr/nr,nc->rc/dot_general | solution.py:98
  222.6 14.0 %fusion.165 = f32[2048]{0:T(1024)S(1)} fusion(f32[1024,128]{1,0:T(8,128)S(1)} %get-tuple-element.394, f32[2048]{0:T(1024)S(1)} %get-tuple-element.351, s32[2048]{0:T(1024)S(1)} %get-tuple-element.354, f32[2048]{0:T(1024)S(1)} %get-tuple-element.355, s32[2048]{0:T(1024)S(1)} %get-tuple-element.356, f32[2048]{0:T(1024)S(1)} %get-tuple-element.357, ...), kind=kOutput, calls=%fused_computation.33.clone.1 | convolution fusion | flops 3246127104 | bytes 630784 | tf_op jit(solution)/shard_map/while/body/eval_jaxpr/dot_general | solution.py:93
  236.9 17.0 %fusion.166 = f32[1024,128]{1,0:T(8,128)S(1)} fusion(f32[2048]{0:T(1024)S(1)} %get-tuple-element.351, s32[2048]{0:T(1024)S(1)} %get-tuple-element.354, f32[2048]{0:T(1024)S(1)} %get-tuple-element.355, s32[2048]{0:T(1024)S(1)} %get-tuple-element.356, f32[2048]{0:T(1024)S(1)} %get-tuple-element.357, s32[2048]{0:T(1024)S(1)} %get-tuple-element.358, ...), kind=kOutput, calls=%fused_computation.32.clone.1 | convolution fusion | flops 3246129152 | bytes 1155073 | tf_op jit(solution)/shard_map/while/body/eval_jaxpr/nr,nc->rc/dot_general | solution.py:98
  254.0 14.0 %fusion.165 = f32[2048]{0:T(1024)S(1)} fusion(f32[1024,128]{1,0:T(8,128)S(1)} %get-tuple-element.394, f32[2048]{0:T(1024)S(1)} %get-tuple-element.351, s32[2048]{0:T(1024)S(1)} %get-tuple-element.354, f32[2048]{0:T(1024)S(1)} %get-tuple-element.355, s32[2048]{0:T(1024)S(1)} %get-tuple-element.356, f32[2048]{0:T(1024)S(1)} %get-tuple-element.357, ...), kind=kOutput, calls=%fused_computation.33.clone.1 | convolution fusion | flops 3246127104 | bytes 630784 | tf_op jit(solution)/shard_map/while/body/eval_jaxpr/dot_general | solution.py:93
  268.3 17.0 %fusion.166 = f32[1024,128]{1,0:T(8,128)S(1)} fusion(f32[2048]{0:T(1024)S(1)} %get-tuple-element.351, s32[2048]{0:T(1024)S(1)} %get-tuple-element.354, f32[2048]{0:T(1024)S(1)} %get-tuple-element.355, s32[2048]{0:T(1024)S(1)} %get-tuple-element.356, f32[2048]{0:T(1024)S(1)} %get-tuple-element.357, s32[2048]{0:T(1024)S(1)} %get-tuple-element.358, ...), kind=kOutput, calls=%fused_computation.32.clone.1 | convolution fusion | flops 3246129152 | bytes 1155073 | tf_op jit(solution)/shard_map/while/body/eval_jaxpr/nr,nc->rc/dot_general | solution.py:98
  285.5 14.0 %fusion.165 = f32[2048]{0:T(1024)S(1)} fusion(f32[1024,128]{1,0:T(8,128)S(1)} %get-tuple-element.394, f32[2048]{0:T(1024)S(1)} %get-tuple-element.351, s32[2048]{0:T(1024)S(1)} %get-tuple-element.354, f32[2048]{0:T(1024)S(1)} %get-tuple-element.355, s32[2048]{0:T(1024)S(1)} %get-tuple-element.356, f32[2048]{0:T(1024)S(1)} %get-tuple-element.357, ...), kind=kOutput, calls=%fused_computation.33.clone.1 | convolution fusion | flops 3246127104 | bytes 630784 | tf_op jit(solution)/shard_map/while/body/eval_jaxpr/dot_general | solution.py:93
  299.8 17.0 %fusion.166 = f32[1024,128]{1,0:T(8,128)S(1)} fusion(f32[2048]{0:T(1024)S(1)} %get-tuple-element.351, s32[2048]{0:T(1024)S(1)} %get-tuple-element.354, f32[2048]{0:T(1024)S(1)} %get-tuple-element.355, s32[2048]{0:T(1024)S(1)} %get-tuple-element.356, f32[2048]{0:T(1024)S(1)} %get-tuple-element.357, s32[2048]{0:T(1024)S(1)} %get-tuple-element.358, ...), kind=kOutput, calls=%fused_computation.32.clone.1 | convolution fusion | flops 3246129152 | bytes 1155073 | tf_op jit(solution)/shard_map/while/body/eval_jaxpr/nr,nc->rc/dot_general | solution.py:98
  317.0 14.0 %fusion.165 = f32[2048]{0:T(1024)S(1)} fusion(f32[1024,128]{1,0:T(8,128)S(1)} %get-tuple-element.394, f32[2048]{0:T(1024)S(1)} %get-tuple-element.351, s32[2048]{0:T(1024)S(1)} %get-tuple-element.354, f32[2048]{0:T(1024)S(1)} %get-tuple-element.355, s32[2048]{0:T(1024)S(1)} %get-tuple-element.356, f32[2048]{0:T(1024)S(1)} %get-tuple-element.357, ...), kind=kOutput, calls=%fused_computation.33.clone.1 | convolution fusion | flops 3246127104 | bytes 630784 | tf_op jit(solution)/shard_map/while/body/eval_jaxpr/dot_general | solution.py:93
  331.3 17.0 %fusion.166 = f32[1024,128]{1,0:T(8,128)S(1)} fusion(f32[2048]{0:T(1024)S(1)} %get-tuple-element.351, s32[2048]{0:T(1024)S(1)} %get-tuple-element.354, f32[2048]{0:T(1024)S(1)} %get-tuple-element.355, s32[2048]{0:T(1024)S(1)} %get-tuple-element.356, f32[2048]{0:T(1024)S(1)} %get-tuple-element.357, s32[2048]{0:T(1024)S(1)} %get-tuple-element.358, ...), kind=kOutput, calls=%fused_computation.32.clone.1 | convolution fusion | flops 3246129152 | bytes 1155073 | tf_op jit(solution)/shard_map/while/body/eval_jaxpr/nr,nc->rc/dot_general | solution.py:98
  348.4 14.0 %fusion.165 = f32[2048]{0:T(1024)S(1)} fusion(f32[1024,128]{1,0:T(8,128)S(1)} %get-tuple-element.394, f32[2048]{0:T(1024)S(1)} %get-tuple-element.351, s32[2048]{0:T(1024)S(1)} %get-tuple-element.354, f32[2048]{0:T(1024)S(1)} %get-tuple-element.355, s32[2048]{0:T(1024)S(1)} %get-tuple-element.356, f32[2048]{0:T(1024)S(1)} %get-tuple-element.357, ...), kind=kOutput, calls=%fused_computation.33.clone.1 | convolution fusion | flops 3246127104 | bytes 630784 | tf_op jit(solution)/shard_map/while/body/eval_jaxpr/dot_general | solution.py:93
  362.7 17.0 %fusion.166 = f32[1024,128]{1,0:T(8,128)S(1)} fusion(f32[2048]{0:T(1024)S(1)} %get-tuple-element.351, s32[2048]{0:T(1024)S(1)} %get-tuple-element.354, f32[2048]{0:T(1024)S(1)} %get-tuple-element.355, s32[2048]{0:T(1024)S(1)} %get-tuple-element.356, f32[2048]{0:T(1024)S(1)} %get-tuple-element.357, s32[2048]{0:T(1024)S(1)} %get-tuple-element.358, ...), kind=kOutput, calls=%fused_computation.32.clone.1 | convolution fusion | flops 3246129152 | bytes 1155073 | tf_op jit(solution)/shard_map/while/body/eval_jaxpr/nr,nc->rc/dot_general | solution.py:98
  379.9 14.0 %fusion.165 = f32[2048]{0:T(1024)S(1)} fusion(f32[1024,128]{1,0:T(8,128)S(1)} %get-tuple-element.394, f32[2048]{0:T(1024)S(1)} %get-tuple-element.351, s32[2048]{0:T(1024)S(1)} %get-tuple-element.354, f32[2048]{0:T(1024)S(1)} %get-tuple-element.355, s32[2048]{0:T(1024)S(1)} %get-tuple-element.356, f32[2048]{0:T(1024)S(1)} %get-tuple-element.357, ...), kind=kOutput, calls=%fused_computation.33.clone.1 | convolution fusion | flops 3246127104 | bytes 630784 | tf_op jit(solution)/shard_map/while/body/eval_jaxpr/dot_general | solution.py:93
  394.2 17.0 %fusion.166 = f32[1024,128]{1,0:T(8,128)S(1)} fusion(f32[2048]{0:T(1024)S(1)} %get-tuple-element.351, s32[2048]{0:T(1024)S(1)} %get-tuple-element.354, f32[2048]{0:T(1024)S(1)} %get-tuple-element.355, s32[2048]{0:T(1024)S(1)} %get-tuple-element.356, f32[2048]{0:T(1024)S(1)} %get-tuple-element.357, s32[2048]{0:T(1024)S(1)} %get-tuple-element.358, ...), kind=kOutput, calls=%fused_computation.32.clone.1 | convolution fusion | flops 3246129152 | bytes 1155073 | tf_op jit(solution)/shard_map/while/body/eval_jaxpr/nr,nc->rc/dot_general | solution.py:98
  411.4 14.0 %fusion.165 = f32[2048]{0:T(1024)S(1)} fusion(f32[1024,128]{1,0:T(8,128)S(1)} %get-tuple-element.394, f32[2048]{0:T(1024)S(1)} %get-tuple-element.351, s32[2048]{0:T(1024)S(1)} %get-tuple-element.354, f32[2048]{0:T(1024)S(1)} %get-tuple-element.355, s32[2048]{0:T(1024)S(1)} %get-tuple-element.356, f32[2048]{0:T(1024)S(1)} %get-tuple-element.357, ...), kind=kOutput, calls=%fused_computation.33.clone.1 | convolution fusion | flops 3246127104 | bytes 630784 | tf_op jit(solution)/shard_map/while/body/eval_jaxpr/dot_general | solution.py:93
  425.6 17.0 %fusion.166 = f32[1024,128]{1,0:T(8,128)S(1)} fusion(f32[2048]{0:T(1024)S(1)} %get-tuple-element.351, s32[2048]{0:T(1024)S(1)} %get-tuple-element.354, f32[2048]{0:T(1024)S(1)} %get-tuple-element.355, s32[2048]{0:T(1024)S(1)} %get-tuple-element.356, f32[2048]{0:T(1024)S(1)} %get-tuple-element.357, s32[2048]{0:T(1024)S(1)} %get-tuple-element.358, ...), kind=kOutput, calls=%fused_computation.32.clone.1 | convolution fusion | flops 3246129152 | bytes 1155073 | tf_op jit(solution)/shard_map/while/body/eval_jaxpr/nr,nc->rc/dot_general | solution.py:98
  443.9 39.9 %all-reduce.5.cloned.1.call-done = f32[32,32,128]{2,1,0:T(8,128)} async-done(((f32[32,32,128]{2,1,0:T(8,128)}), f32[32,32,128]{2,1,0:T(8,128)}) %all-reduce.5.cloned.1.call-update) | async-done | bytes 524304 | tf_op jit(solution)/shard_map/psum | solution.py:157
  483.8 4.1 convert_multiply_fusion
  487.9 11.0 %convolution_bitcast_fusion = f32[32,33,640]{1,0,2:T(8,128)} fusion(f32[640,32,128]{2,1,0:T(8,128)S(1)} %bitcast.113, f32[128]{0:T(128)S(1)} %get-tuple-element.297, s32[128]{0:T(128)S(1)} %get-tuple-element.296, f32[128]{0:T(128)S(1)} %get-tuple-element.298, s32[128]{0:T(128)S(1)} %get-tuple-element.295), kind=kOutput, calls=%fused_computation.83 | convolution fusion | flops 1038111360 | bytes 13191168 | tf_op jit(solution)/shard_map/yb,cxy->xbc/dot_general | solution.py:162
  498.9 8.5 %copy.54 = f32[32,33,640]{2,0,1:T(8,128)S(1)} copy(f32[32,33,640]{1,0,2:T(8,128)} %convolution_bitcast_fusion) | data formatting | bytes 5406720 | tf_op jit(solution)/shard_map/yb,cxy->xbc/transpose | solution.py:162
  509.6 6.2 collective-permute-done.18
  515.9 2.9 scatter-add.6
  520.4 3.5 collective-permute-done.19
  524.1 4.1 collective-permute-start.20
  528.2 2.4 collective-permute-done.21
  534.7 2.7 collective-permute-done.23
  538.7 3.8 collective-permute-start.24
  542.5 2.2 collective-permute-done.25
  551.1 4.0 collective-permute-start.28
  555.8 3.9 all-to-all-start.1
  559.7 3.0 collective-permute-start.30
  562.8 5.4 all-to-all-done.1
  568.2 45.5 %gather_fusion = f32[8192]{0:T(1024)S(1)} fusion(f32[16384]{0:T(1024)S(1)} %bitcast.111, s32[8192]{0:T(1024)S(1)} %broadcast_clamp_fusion), kind=kCustom, calls=%fused_computation | custom fusion | bytes 98304 | tf_op jit(solution)/shard_map/gather | solution.py:156
  614.9 3.5 collective-permute-start.32
  625.0 2.3 collective-permute-done.35
  628.6 2.1 reshape.464
  630.7 4.2 fusion.46
  634.9 2.2 reshape.444
  (196 shorter events, 62.4 us)
Async XLA Ops:
  7.2 3.3 copy-start
  7.2 14.2 %copy-start.6 = (s32[8192,1]{0,1:T(1,128)S(1)}, s32[8192,1]{0,1:T(1,128)}, u32[]{:S(2)}) copy-start(s32[8192,1]{0,1:T(1,128)} %param.23) | copy-start | bytes 98308
  7.2 182.4 %all-reduce.3.cloned.1.call-start = ((), (), s32[]{:S(2)}) async-start(), calls=%async_computation.2 | async-start | bytes 1048576 | tf_op jit(solution)/shard_map/psum | solution.py:147
  15.1 36.4 %collective-permute-start.1 = (f32[1,32,640]{2,0,1:T(1,128)S(1)}, f32[1,32,640]{2,0,1:T(1,128)S(1)}, u32[]{:S(2)}, u32[]{:S(2)}) collective-permute-start(f32[1,32,640]{2,0,1:T(1,128)S(1)} %slice.445), channel_id=1, source_target_pairs={{0,16},{16,32},{32,48},{48,64},{64,80},{80,96},{96,112},{112,0},{1... | collective-permute-start | bytes 245768 | tf_op jit(solution)/shard_map/ppermute | solution.py:22
  17.2 34.4 %collective-permute-start = (f32[1,32,640]{2,0,1:T(1,128)S(1)}, f32[1,32,640]{2,0,1:T(1,128)S(1)}, u32[]{:S(2)}, u32[]{:S(2)}) collective-permute-start(f32[1,32,640]{2,0,1:T(1,128)S(1)} %slice.444), channel_id=1, source_target_pairs={{16,0},{32,16},{48,32},{64,48},{80,64},{96,80},{112,96},{0,112},{1... | collective-permute-start | bytes 245768 | tf_op jit(solution)/shard_map/ppermute | solution.py:23
  46.1 36.1 %copy-start.8 = (s32[8192]{0:T(1024)S(1)}, s32[8192]{0:T(1024)}, u32[]{:S(2)}) copy-start(s32[8192]{0:T(1024)} %param.24) | copy-start | bytes 98308
  46.1 36.1 %copy-start.9 = (s32[8192]{0:T(1024)S(1)}, s32[8192]{0:T(1024)}, u32[]{:S(2)}) copy-start(s32[8192]{0:T(1024)} %param.25) | copy-start | bytes 98308
  51.6 4.8 collective-permute-start.2
  54.7 5.2 collective-permute-start.3
  60.5 6.7 %collective-permute-start.5 = (f32[1,32,640]{2,0,1:T(1,128)S(1)}, f32[1,32,640]{2,0,1:T(1,128)S(1)}, u32[]{:S(2)}, u32[]{:S(2)}) collective-permute-start(f32[1,32,640]{2,0,1:T(1,128)S(1)} %get-tuple-element.289), channel_id=1, source_target_pairs={{0,16},{16,32},{32,48},{48,64},{64,80},{80,96},{96,112},{112,0},{1... | collective-permute-start | bytes 245768 | tf_op jit(solution)/shard_map/ppermute | solution.py:22
  60.5 6.6 %collective-permute-start.4 = (f32[1,32,640]{2,0,1:T(1,128)S(1)}, f32[1,32,640]{2,0,1:T(1,128)S(1)}, u32[]{:S(2)}, u32[]{:S(2)}) collective-permute-start(f32[1,32,640]{2,0,1:T(1,128)S(1)} %get-tuple-element.290), channel_id=1, source_target_pairs={{16,0},{32,16},{48,32},{64,48},{80,64},{96,80},{112,96},{0,112},{1... | collective-permute-start | bytes 245768 | tf_op jit(solution)/shard_map/ppermute | solution.py:23
  67.2 4.1 collective-permute-start.6
  67.3 5.3 collective-permute-start.7
  73.1 7.0 %collective-permute-start.9 = (f32[1,32,640]{2,0,1:T(1,128)S(1)}, f32[1,32,640]{2,0,1:T(1,128)S(1)}, u32[]{:S(2)}, u32[]{:S(2)}) collective-permute-start(f32[1,32,640]{2,0,1:T(1,128)S(1)} %get-tuple-element.287), channel_id=1, source_target_pairs={{0,16},{16,32},{32,48},{48,64},{64,80},{80,96},{96,112},{112,0},{1... | collective-permute-start | bytes 245768 | tf_op jit(solution)/shard_map/ppermute | solution.py:22
  73.6 6.4 collective-permute-start.8
  80.1 4.1 collective-permute-start.10
  80.2 5.3 collective-permute-start.11
  86.0 6.7 %collective-permute-start.13 = (f32[1,32,640]{2,0,1:T(1,128)S(1)}, f32[1,32,640]{2,0,1:T(1,128)S(1)}, u32[]{:S(2)}, u32[]{:S(2)}) collective-permute-start(f32[1,32,640]{2,0,1:T(1,128)S(1)} %get-tuple-element.285), channel_id=1, source_target_pairs={{0,16},{16,32},{32,48},{48,64},{64,80},{80,96},{96,112},{112,0},{1... | collective-permute-start | bytes 245768 | tf_op jit(solution)/shard_map/ppermute | solution.py:22
  86.3 6.4 collective-permute-start.12
  92.7 4.1 collective-permute-start.14
  92.9 5.2 collective-permute-start.15
  98.6 6.3 collective-permute-start.16
  104.9 4.2 collective-permute-start.17
  128.2 9.8 %copy-start.7 = (f32[3,8192]{1,0:T(4,128)S(1)}, f32[3,8192]{1,0:T(4,128)}, u32[]{:S(2)}) copy-start(f32[3,8192]{1,0:T(4,128)} %param.26) | copy-start | bytes 294916
  128.2 9.8 %copy-start.10 = (f32[8192]{0:T(1024)S(1)}, f32[8192]{0:T(1024)}, u32[]{:S(2)}) copy-start(f32[8192]{0:T(1024)} %param.28) | copy-start | bytes 98308
  128.2 9.8 %copy-start.11 = (f32[8192]{0:T(1024)S(1)}, f32[8192]{0:T(1024)}, u32[]{:S(2)}) copy-start(f32[8192]{0:T(1024)} %param.27) | copy-start | bytes 98308
  140.9 48.7 %copy-start.2 = (f32[32,32,128]{2,1,0:T(8,128)S(1)}, f32[32,32,128]{2,1,0:T(8,128)}, u32[]{:S(2)}) copy-start(f32[32,32,128]{2,1,0:T(8,128)} %param.21) | copy-start | bytes 1572868
  140.9 48.7 %copy-start.3 = (f32[32,32,128]{2,1,0:T(8,128)S(1)}, f32[32,32,128]{2,1,0:T(8,128)}, u32[]{:S(2)}) copy-start(f32[32,32,128]{2,1,0:T(8,128)} %param.22) | copy-start | bytes 1572868
  171.6 17.6 %all-to-all-start = ((f32[6,32,512]{2,0,1:T(8,128)}), f32[6,32,512]{2,0,1:T(8,128)S(1)}, u32[]{:S(2)}, u32[]{:S(2)}) async-start(f32[6,32,512]{2,0,1:T(8,128)} %copy.38), calls=%async_computation | async-start | bytes 1048576 | tf_op jit(solution)/shard_map/all_to_all | solution.py:153
  179.2 304.7 %all-reduce.5.cloned.1.call-start = ((), (), s32[]{:S(2)}) async-start(), calls=%async_computation.3 | async-start | bytes 1048576 | tf_op jit(solution)/shard_map/psum | solution.py:157
  443.1 0.8 copy-start.5
  508.9 6.9 %collective-permute-start.18 = (f32[1,33,640]{2,0,1:T(1,128)S(1)}, f32[1,33,640]{2,0,1:T(1,128)S(1)}, u32[]{:S(2)}, u32[]{:S(2)}) collective-permute-start(f32[1,33,640]{2,0,1:T(1,128)S(1)} %slice.461), channel_id=1, source_target_pairs={{0,16},{16,32},{32,48},{48,64},{64,80},{80,96},{96,112},{112,0},{1... | collective-permute-start | bytes 253448 | tf_op jit(solution)/shard_map/ppermute | solution.py:30
  518.8 5.1 collective-permute-start.19
  524.0 6.6 %collective-permute-start.21 = (f32[1,32,640]{2,0,1:T(1,128)S(1)}, f32[1,32,640]{2,0,1:T(1,128)S(1)}, u32[]{:S(2)}, u32[]{:S(2)}) collective-permute-start(f32[1,32,640]{2,0,1:T(1,128)S(1)} %get-tuple-element.283), channel_id=1, source_target_pairs={{0,16},{16,32},{32,48},{48,64},{64,80},{80,96},{96,112},{112,0},{1... | collective-permute-start | bytes 245768 | tf_op jit(solution)/shard_map/ppermute | solution.py:22
  524.1 6.5 %collective-permute-start.20 = (f32[1,32,640]{2,0,1:T(1,128)S(1)}, f32[1,32,640]{2,0,1:T(1,128)S(1)}, u32[]{:S(2)}, u32[]{:S(2)}) collective-permute-start(f32[1,32,640]{2,0,1:T(1,128)S(1)} %get-tuple-element.284), channel_id=1, source_target_pairs={{16,0},{32,16},{48,32},{64,48},{80,64},{96,80},{112,96},{0,112},{1... | collective-permute-start | bytes 245768 | tf_op jit(solution)/shard_map/ppermute | solution.py:23
  530.6 4.1 collective-permute-start.22
  532.2 5.2 collective-permute-start.23
  538.0 6.6 %collective-permute-start.25 = (f32[1,32,640]{2,0,1:T(1,128)S(1)}, f32[1,32,640]{2,0,1:T(1,128)S(1)}, u32[]{:S(2)}, u32[]{:S(2)}) collective-permute-start(f32[1,32,640]{2,0,1:T(1,128)S(1)} %get-tuple-element.281), channel_id=1, source_target_pairs={{0,16},{16,32},{32,48},{48,64},{64,80},{80,96},{96,112},{112,0},{1... | collective-permute-start | bytes 245768 | tf_op jit(solution)/shard_map/ppermute | solution.py:22
  538.7 6.0 collective-permute-start.24
  544.6 4.1 collective-permute-start.26
  544.7 5.3 collective-permute-start.27
  550.6 9.1 %collective-permute-start.29 = (f32[1,32,640]{2,0,1:T(1,128)S(1)}, f32[1,32,640]{2,0,1:T(1,128)S(1)}, u32[]{:S(2)}, u32[]{:S(2)}) collective-permute-start(f32[1,32,640]{2,0,1:T(1,128)S(1)} %get-tuple-element.279), channel_id=1, source_target_pairs={{0,16},{16,32},{32,48},{48,64},{64,80},{80,96},{96,112},{112,0},{1... | collective-permute-start | bytes 245768 | tf_op jit(solution)/shard_map/ppermute | solution.py:22
  551.1 8.6 %collective-permute-start.28 = (f32[1,32,640]{2,0,1:T(1,128)S(1)}, f32[1,32,640]{2,0,1:T(1,128)S(1)}, u32[]{:S(2)}, u32[]{:S(2)}) collective-permute-start(f32[1,32,640]{2,0,1:T(1,128)S(1)} %get-tuple-element.280), channel_id=1, source_target_pairs={{16,0},{32,16},{48,32},{64,48},{80,64},{96,80},{112,96},{0,112},{1... | collective-permute-start | bytes 245768 | tf_op jit(solution)/shard_map/ppermute | solution.py:23
  555.8 12.3 %all-to-all-start.1 = ((f32[32,512,1]{1,2,0:T(1,128)}), f32[32,512,1]{1,2,0:T(1,128)S(1)}, u32[]{:S(2)}, u32[]{:S(2)}) async-start(f32[32,512,1]{1,2,0:T(1,128)} %all_to_all.16), calls=%async_computation.1 | async-start | bytes 131072 | tf_op jit(solution)/shard_map/all_to_all | solution.py:155
  559.7 54.0 %collective-permute-start.30 = (f32[10,1,640]{2,0,1:T(8,128)S(1)}, f32[10,1,640]{2,0,1:T(8,128)S(1)}, u32[]{:S(2)}, u32[]{:S(2)}) collective-permute-start(f32[10,1,640]{2,0,1:T(8,128)S(1)} %get-tuple-element.263), channel_id=1, source_target_pairs={{4,0},{8,4},{12,8},{0,12},{5,1},{9,5},{13,9},{1,13},{6,2},{10,6},{... | collective-permute-start | bytes 76808 | tf_op jit(solution)/shard_map/ppermute | solution.py:23
  562.8 50.9 %collective-permute-start.31 = (f32[10,1,640]{2,0,1:T(8,128)S(1)}, f32[10,1,640]{2,0,1:T(8,128)S(1)}, u32[]{:S(2)}, u32[]{:S(2)}) collective-permute-start(f32[10,1,640]{2,0,1:T(8,128)S(1)} %get-tuple-element.264), channel_id=1, source_target_pairs={{0,4},{4,8},{8,12},{12,0},{1,5},{5,9},{9,13},{13,1},{2,6},{6,10},{... | collective-permute-start | bytes 76808 | tf_op jit(solution)/shard_map/ppermute | solution.py:22
  568.2 54.9 %copy-start.1 = (f32[32,32,128]{2,1,0:T(8,128)S(1)}, f32[32,32,128]{2,1,0:T(8,128)}, u32[]{:S(2)}) copy-start(f32[32,32,128]{2,1,0:T(8,128)} %all-reduce.5.cloned.1.call-done) | copy-start | bytes 1572868
  568.2 54.9 %copy-start.4 = (f32[32,32,128]{2,1,0:T(8,128)S(1)}, f32[32,32,128]{2,1,0:T(8,128)}, u32[]{:S(2)}) copy-start(f32[32,32,128]{2,1,0:T(8,128)} %param.22) | copy-start | bytes 1572868
  614.3 6.6 %collective-permute-start.33 = (f32[1,32,640]{2,0,1:T(1,128)S(1)}, f32[1,32,640]{2,0,1:T(1,128)S(1)}, u32[]{:S(2)}, u32[]{:S(2)}) collective-permute-start(f32[1,32,640]{2,0,1:T(1,128)S(1)} %get-tuple-element.277), channel_id=1, source_target_pairs={{0,16},{16,32},{32,48},{48,64},{64,80},{80,96},{96,112},{112,0},{1... | collective-permute-start | bytes 245768 | tf_op jit(solution)/shard_map/ppermute | solution.py:22
  614.9 5.9 collective-permute-start.32
  620.9 4.1 collective-permute-start.34
  622.1 5.2 collective-permute-start.35
Sparse Core Ops, SparseCore 0:
  138.1 42.5 all-reduce.2
  444.0 39.7 all-reduce.4
where the time goes:
time: 657 us; the launch traced here: 646 us
  matrix products  288 us (44%)
  local copies, waits for them, and re-layouts  111 us (17%)
  waiting for transfers between devices  108 us (16%)
  starting transfers between devices  73.8 us (11%)
  other arithmetic  48.9 us (7%)
  between operations  15.5 us (2%)
    dot_general x8, matrix products, one_block(): adjoint_block = jnp.einsum('nr,nc->rc', row_pick, spread, precision=highest)  136 us
    dot_general x8, matrix products, one_block(): jnp.dot(row_pick, matrix, precision=highest, preferred_element_type=jnp.f...  112 us
    gather x1, local copies, waits for them, and re-layouts, per_device(): departures = jnp.where(live, returned[jnp.minimum(target, width - 1)], 0.0)  45.5 us
    ppermute x16, starting transfers between devices, with_halo(): after = lax.ppermute(first, axis, down)  41 us
    psum x1, waiting for transfers between devices, per_device(): adjoint_grid_values = lax.psum(adjoint_part, 'mem')  39.9 us
    ppermute x16, waiting for transfers between devices, with_halo(): before = lax.ppermute(last, axis, up)  24.8 us
    scatter x1, local copies, waits for them, and re-layouts, per_device(): jnp.zeros((6, width), jnp.float32).at[:, target].set(packed, mode='drop')  24.6 us
    another operation x3, other arithmetic  21.4 us
  transfers between devices with their start and end apart: 40, of which 26 were waited for; matrix products, arithmetic and copies ran while one was open for 18% of the time, Pallas kernels for 0%

commit v1 on v0

v1 whole, which is shorter than its diff:
```python
import functools
import numpy as np
import jax
import jax.numpy as jnp
from jax import lax
from jax.experimental import pallas as pl
from jax.experimental.pallas import tpu as pltpu
from jax.sharding import PartitionSpec as P

F32 = jnp.float32
BF16 = jnp.bfloat16
NU = 0.2
RATIO = 4
VMEM_LIMIT = 56 * 1024 * 1024
NN = (((1,), (0,)), ((), ()))
NT = (((1,), (1,)), ((), ()))
TN = (((0,), (0,)), ((), ()))


def mm(a, b, dims=NN):
    return lax.dot_general(a, b, dims, preferred_element_type=F32)


def split(v):
    hi = v.astype(BF16)
    return hi, (v - hi.astype(F32)).astype(BF16)


def iota(shape, dim):
    return lax.broadcasted_iota(jnp.int32, shape, dim)


def route_kernel(cnt_ref, owner_ref, col_ref, lev_ref, frac_ref, inn_ref, rinv_ref, out_ref, tgt_ref, acc_ref):
    rows, wide = owner_ref.shape
    groups = 32
    place = iota((rows, wide), 0) * wide + iota((rows, wide), 1)
    live = place < cnt_ref[0]
    owner = jnp.where(live, owner_ref[...], groups)
    same = iota((rows, groups, wide), 1) == owner[:, None, :]
    onehot = jnp.where(same, 1.0, 0.0).astype(BF16).reshape(rows * groups, wide)
    before = jnp.where(iota((wide, wide), 0) < iota((wide, wide), 1), 1.0, 0.0).astype(BF16)
    inside = mm(onehot, before).reshape(rows, groups, wide)
    totals = mm(onehot, jnp.ones((wide, wide), BF16)).reshape(rows, groups, wide)
    running = jnp.zeros((groups, wide), F32)
    ranks = []
    for c in range(rows):
        ranks.append(jnp.sum(jnp.where(same[c], inside[c] + running, 0.0), 0, keepdims=True))
        running = running + totals[c]
    rank = jnp.concatenate(ranks, 0).astype(jnp.int32)
    low = rank % 128
    part = rank // 128
    tgt_ref[...] = jnp.where(live, owner * 512 + rank, -1)
    high = jnp.where(live, part * groups + owner, -1)
    base = (lev_ref[...] * 4096 + col_ref[...]).astype(F32)
    values = [frac_ref[0], frac_ref[1], frac_ref[2], inn_ref[...], rinv_ref[...], base]
    terms = []
    for v in values:
        terms.extend(split(v))
    acc_ref[...] = jnp.zeros_like(acc_ref)
    for c in range(rows):
        hit = jnp.where(iota((128, wide), 0) == high[c:c + 1], 1.0, 0.0).astype(BF16)
        lane = jnp.where(iota((128, wide), 0) == low[c:c + 1], 1.0, 0.0).astype(BF16)
        stack = jnp.concatenate([lane * t[c:c + 1] for t in terms], 0)
        acc_ref[...] += mm(hit, stack, NT)
    for ch in range(6):
        full = acc_ref[:, 256 * ch:256 * ch + 128] + acc_ref[:, 256 * ch + 128:256 * ch + 256]
        for q in range(4):
            out_ref[:, ch * 4 + q, :] = full[q * groups:(q + 1) * groups]


def route(cnt, owner, col, lev, frac, inn, rinv):
    slots = owner.shape[0]
    shape = (slots // 256, 256)
    return pl.pallas_call(
        route_kernel,
        out_shape=(jax.ShapeDtypeStruct((32, 24, 128), F32), jax.ShapeDtypeStruct(shape, jnp.int32)),
        in_specs=[pl.BlockSpec(memory_space=pltpu.SMEM)] + [pl.BlockSpec(memory_space=pltpu.VMEM)] * 6,
        out_specs=(pl.BlockSpec(memory_space=pltpu.VMEM),) * 2,
        scratch_shapes=[pltpu.VMEM((128, 1536), F32)],
        compiler_params=pltpu.CompilerParams(vmem_limit_bytes=VMEM_LIMIT),
        cost_estimate=pl.CostEstimate(flops=4_000_000_000, bytes_accessed=1_000_000, transcendentals=0),
        name="route",
    )(cnt, owner.reshape(shape), col.reshape(shape), lev.reshape(shape), frac.reshape((3,) + shape), inn.reshape(shape), rinv.reshape(shape))


def unroute_kernel(tgt_ref, ret_ref, out_ref):
    rows, wide = tgt_ref.shape
    ret = ret_ref[...].T
    hi, lo = split(ret)
    table = jnp.concatenate([hi, lo], 0)
    for c in range(rows):
        tgt = tgt_ref[c:c + 1]
        hit = jnp.where(iota((128, wide), 0) == tgt // 128, 1.0, 0.0).astype(BF16)
        picked = mm(table, hit)
        picked = picked[:128] + picked[128:]
        out_ref[c:c + 1] = jnp.sum(jnp.where((iota((128, wide), 0) == tgt % 128) & (tgt >= 0), picked, 0.0), 0, keepdims=True)


def unroute(tgt, ret):
    return pl.pallas_call(
        unroute_kernel,
        out_shape=jax.ShapeDtypeStruct(tgt.shape, F32),
        in_specs=[pl.BlockSpec(memory_space=pltpu.VMEM)] * 2,
        out_specs=pl.BlockSpec(memory_space=pltpu.VMEM),
        compiler_params=pltpu.CompilerParams(vmem_limit_bytes=VMEM_LIMIT),
        cost_estimate=pl.CostEstimate(flops=600_000_000, bytes_accessed=200_000, transcendentals=0),
        name="unroute",
    )(tgt, ret)


def tent(position, count):
    return jnp.maximum(1.0 - jnp.abs(position - iota((count, 128), 0).astype(F32)), 0.0)


def stencil_kernel(inc_ref, obs_ref, dep_ref, adj_ref, table_ref, acc_ref, ahi_ref, alo_ref):
    turned = inc_ref[...].T
    hi, lo = split(turned)
    table_ref[0:128] = hi
    table_ref[128:256] = lo
    acc_ref[...] = jnp.zeros_like(acc_ref)

    def one_source(s, carry):
        cols = []
        for q in range(4):
            get = lambda ch: obs_ref[s, ch * 4 + q:ch * 4 + q + 1, :]
            base = get(5).astype(jnp.int32)
            pos_l = (base // 4096).astype(F32) + get(2)
            pos_x = ((base // 128) % 32).astype(F32) + get(0)
            pos_y = (base % 128).astype(F32) + get(1)
            in_l, in_x = tent(pos_l, 32), tent(pos_x, 32)
            cols.append(tent(pos_y, 128))
            for l in range(32):
                hi, lo = split(in_l[l:l + 1] * in_x)
                ahi_ref[l * 32:(l + 1) * 32, q * 128:(q + 1) * 128] = hi
                alo_ref[l * 32:(l + 1) * 32, q * 128:(q + 1) * 128] = lo
        both = mm(table_ref[...], ahi_ref[...])
        picked = both[:128] + both[128:] + mm(table_ref[0:128], alo_ref[...])
        shi, slo = [], []
        for q in range(4):
            dep = jnp.sum(picked[:, q * 128:(q + 1) * 128] * cols[q], 0, keepdims=True) - obs_ref[s, 12 + q:13 + q, :]
            dep_ref[s, q:q + 1, :] = dep
            hi, lo = split(cols[q] * (dep * obs_ref[s, 16 + q:17 + q, :]))
            shi.append(hi)
            slo.append(lo)
        shi = jnp.concatenate(shi, 1)
        slo = jnp.concatenate(slo, 1)
        acc_ref[...] += mm(ahi_ref[...], shi, NT) + mm(ahi_ref[...], slo, NT) + mm(alo_ref[...], shi, NT)
        return carry

    lax.fori_loop(0, obs_ref.shape[0], one_source, 0)
    adj_ref[...] = acc_ref[...]


def stencil(inc, obs):
    return pl.pallas_call(
        stencil_kernel,
        out_shape=(jax.ShapeDtypeStruct((32, 4, 128), F32), jax.ShapeDtypeStruct((1024, 128), F32)),
        in_specs=[pl.BlockSpec(memory_space=pltpu.VMEM)] * 2,
        out_specs=(pl.BlockSpec(memory_space=pltpu.VMEM),) * 2,
        scratch_shapes=[
            pltpu.VMEM((256, 1024), BF16),
            pltpu.VMEM((1024, 128), F32),
            pltpu.VMEM((1024, 512), BF16),
            pltpu.VMEM((1024, 512), BF16),
        ],
        compiler_params=pltpu.CompilerParams(vmem_limit_bytes=VMEM_LIMIT),
        name="stencil",
    )(inc, obs)


def line_weights(fine, coarse):
    out = np.zeros((fine, coarse), np.float32)
    for f in range(fine):
        out[f, f // RATIO] += 1.0 - (f % RATIO) / RATIO
        out[f, f // RATIO + 1] += (f % RATIO) / RATIO
    return out


def tables():
    along = line_weights(128, 40)
    across = line_weights(32, 16)
    spread_y = np.concatenate([along.T, along.T], 0)
    gather_y = np.concatenate([along.T, along.T], 1)
    eye = np.eye(8, dtype=np.float32)
    block = np.kron(eye, across)
    spread_x = np.concatenate([block, block], 1)
    gather_x = np.concatenate([block.T, block.T], 1)
    return [jnp.asarray(t, BF16) for t in (spread_y, gather_y, spread_x, gather_x)]


def diffuse_rows(field, first, last):
    near = field[first - 1:last - 1] + field[first + 1:last + 1]
    mid = field[first:last]
    near = near + pltpu.roll(mid, 1, 1) + pltpu.roll(mid, 47, 1)
    return mid + NU * (near - 4.0 * mid)


def three(a, b_ref):
    hi, lo = split(a)
    return mm(jnp.concatenate([hi, lo, hi], 1), b_ref[...])


def forward_kernel(ext_ref, pert_ref, mix_ref, sy_ref, sx_ref, inc_ref, turn_ref):
    g = pl.program_id(0)

    @pl.when(g == 0)
    def _():
        inc_ref[...] = jnp.zeros_like(inc_ref)
        turn_ref[...] = jnp.zeros_like(turn_ref)

    field = ext_ref[...]
    for step in range(4):
        field = diffuse_rows(field, 1, field.shape[0] - 1)
    field = field[:, 8:48].reshape(9 * 40, 128)
    field = three(field, mix_ref).reshape(9, 40, 128)
    for a in range(9):
        hi, lo = split(field[a])
        turn_ref[:, a, :] = mm(jnp.concatenate([hi, lo], 0), sy_ref[...], TN)
    for i in range(16):
        hi, lo = split(turn_ref[8 * i:8 * i + 8].reshape(128, 128))
        fine = mm(sx_ref[...], jnp.concatenate([hi, lo], 0)).reshape(8, 32, 128)
        l0 = i % 4 * 8
        inc_ref[l0:l0 + 8] += fine * pert_ref[i // 4, l0:l0 + 8].astype(F32)


def forward(ext, pert, mix, sy, sx):
    whole = lambda a: pl.BlockSpec(a.shape, lambda g: (0,) * a.ndim)
    return pl.pallas_call(
        forward_kernel,
        grid=(5,),
        out_shape=jax.ShapeDtypeStruct((32, 32, 128), F32),
        in_specs=[
            pl.BlockSpec((17, 48, 128), lambda g: (0, 0, g)),
            pl.BlockSpec((4, 32, 32, 128), lambda g: (g, 0, 0, 0)),
            whole(mix), whole(sy), whole(sx),
        ],
        out_specs=pl.BlockSpec((32, 32, 128), lambda g: (0, 0, 0)),
        scratch_shapes=[pltpu.VMEM((128, 16, 128), F32)],
        compiler_params=pltpu.CompilerParams(vmem_limit_bytes=VMEM_LIMIT),
        name="forward",
    )(ext, pert, mix, sy, sx)


def backward_kernel(adj_ref, pert_ref, mix_ref, gy_ref, gx_ref, out_ref, turn_ref, grid_ref):
    for i in range(16):
        l0 = i % 4 * 8
        fine = adj_ref[l0:l0 + 8] * pert_ref[i // 4, l0:l0 + 8].astype(F32)
        hi, lo = split(fine.reshape(256, 128))
        turn_ref[8 * i:8 * i + 8] = mm(gx_ref[...], jnp.concatenate([hi, lo], 0)).reshape(8, 16, 128)
    rows = []
    for a in range(9):
        hi, lo = split(turn_ref[:, a, :])
        rows.append(mm(gy_ref[...], jnp.concatenate([hi, lo], 1), NT))
    field = three(jnp.concatenate(rows, 0), mix_ref).reshape(9, 40, 128)
    field = jnp.concatenate([jnp.zeros((9, 8, 128), F32), field], 1)
    for step in range(4):
        two = jnp.zeros((2, 48, 128), F32)
        field = jnp.concatenate([two, field, two], 0)
        field = diffuse_rows(field, 1, field.shape[0] - 1)
    out_ref[...] = field


def backward(adj, pert, mix, gy, gx):
    whole = lambda a: pl.BlockSpec(a.shape, lambda g: (0,) * a.ndim)
    return pl.pallas_call(
        backward_kernel,
        grid=(5,),
        out_shape=jax.ShapeDtypeStruct((17, 48, 640), F32),
        in_specs=[
            whole(adj),
            pl.BlockSpec((4, 32, 32, 128), lambda g: (g, 0, 0, 0)),
            whole(mix), whole(gy), whole(gx),
        ],
        out_specs=pl.BlockSpec((17, 48, 128), lambda g: (0, 0, g)),
        scratch_shapes=[pltpu.VMEM((128, 16, 128), F32), pltpu.VMEM((17, 48, 128), F32)],
        compiler_params=pltpu.CompilerParams(vmem_limit_bytes=VMEM_LIMIT),
        name="backward",
    )(adj, pert, mix, gy, gx)


def mixing(lv):
    eye = jnp.eye(4, dtype=F32)
    def stacked(m):
        hi, lo = split(jnp.kron(eye, m))
        return jnp.concatenate([hi, hi, lo], 0)
    return stacked(lv.T), stacked(lv)


def shifted(value, axis, by):
    count = lax.axis_size(axis)
    return lax.ppermute(value, axis, [(i, (i + by) % count) for i in range(count)])


def per_device(alpha, lv_sqrt, ens_pert, bg_sigma, static_ctrl, obs_owner, obs_column, obs_level, obs_frac, innovation, obs_rinv, obs_count):
    mix_forward, mix_backward = mixing(lv_sqrt)
    spread_y, gather_y, spread_x, gather_x = tables()
    above = shifted(alpha[4:], "tx", 1)
    below = shifted(alpha[:5], "tx", -1)
    outgoing, target = route(obs_count, obs_owner[:, 0], obs_column, obs_level, obs_frac, innovation, obs_rinv)
    incoming = lax.all_to_all(outgoing, ("tx", "ty"), split_axis=0, concat_axis=0, tiled=True)
    tall = jnp.concatenate([above, alpha, below], 0)
    left = shifted(tall[:, 24:], "ty", 1)
    right = shifted(tall[:, :8], "ty", -1)
    ext = jnp.concatenate([left, tall, right], 1)
    partial = forward(ext, ens_pert, mix_forward, spread_y, spread_x)
    increment = lax.psum(partial, "mem") + bg_sigma * static_ctrl
    departure, adjoint = stencil(increment.reshape(1024, 128), incoming)
    returned = lax.all_to_all(departure, ("tx", "ty"), split_axis=0, concat_axis=0, tiled=True)
    adjoint = lax.psum(adjoint, "mem").reshape(32, 32, 128)
    grad_static = static_ctrl + bg_sigma * adjoint
    back = backward(adjoint, ens_pert, mix_backward, gather_y, gather_x)
    departures = unroute(target, returned.reshape(128, 128)).reshape(-1)
    above = shifted(back[12:], "tx", 1)
    below = shifted(back[:4], "tx", -1)
    tall = back[4:12].at[:5].add(above).at[4:].add(below)
    left = shifted(tall[:, 40:45], "ty", 1)
    right = shifted(tall[:, 4:8], "ty", -1)
    center = tall[:, 8:40].at[:, :5].add(left).at[:, 28:].add(right)
    return alpha + center, grad_static, departures


def solution(mesh):
    placed = (
        P("tx", "ty", "mem"),
        P(),
        P("mem", None, "tx", "ty"),
        P(None, "tx", "ty"),
        P(None, "tx", "ty"),
        P(("tx", "ty", "mem"), None),
        P(("tx", "ty", "mem")),
        P(("tx", "ty", "mem")),
        P(None, ("tx", "ty", "mem")),
        P(("tx", "ty", "mem")),
        P(("tx", "ty", "mem")),
        P(("tx", "ty", "mem")),
    )
    return jax.shard_map(
        per_device,
        mesh=mesh,
        in_specs=placed,
        out_specs=(P("tx", "ty", "mem"), P(None, "tx", "ty"), P(("tx", "ty", "mem"))),
        check_vma=False,
    )
```

time: 657 us -> 274 us (0.42); the launches traced: 646 us -> 273 us
  matrix products: 288 us -> 0 us
  Pallas kernels: 0 us -> 104 us
  local copies, waits for them, and re-layouts: 111 us -> 11.8 us
  starting transfers between devices: 73.8 us -> 25 us
  other arithmetic: 48.9 us -> 8.82 us
  blocking collectives: 0 us -> 28.1 us
  waiting for transfers between devices: 108 us -> 81.1 us
    dot_general x22 -> x0, matrix products: 288 us -> none  [the longest x8 136 us: one_block(): adjoint_block = jnp.einsum('nr,nc->rc', row_pick, spread, precision=highest)]
    pallas_call x0 -> x5, Pallas kernels: none -> 104 us  [the longest x1 61.5 us: stencil(): pl.pallas_call(stencil_kernel, out_shape=(jax.ShapeDtypeStruct((32, 4, 12...]
    ppermute x36 -> x8, starting transfers between devices: 62.3 us -> 16.1 us  [shifted(): lax.ppermute(value, axis, [(i, (i + by) % count) for i in range(count)])]
    gather x1 -> x0, local copies, waits for them, and re-layouts: 45.5 us -> none  [per_device(): departures = jnp.where(live, returned[jnp.minimum(target, width - 1)], 0.0)]
    ppermute x36 -> x8, waiting for transfers between devices: 52.3 us -> 21.8 us  [shifted(): lax.ppermute(value, axis, [(i, (i + by) % count) for i in range(count)])]
    all_to_all x0 -> x1, blocking collectives: none -> 28.1 us  [per_device(): lax.all_to_all(departure, ('tx', 'ty'), split_axis=0, concat_axis=0, tile...]
    scatter x1 -> x0, local copies, waits for them, and re-layouts: 24.6 us -> none  [per_device(): jnp.zeros((6, width), jnp.float32).at[:, target].set(packed, mode='drop')]
    another operation x4 -> x0, other arithmetic: 21.6 us -> none
  transfers between devices with their start and end apart: 40 -> 11, of which waited for: 26 -> 6; matrix products, arithmetic and copies ran while one was open for 18% -> 5% of each run, Pallas kernels for 0% -> 5%
where the time goes in v1:
time: 274 us; the launch traced here: 273 us
  Pallas kernels  104 us (38%)
  waiting for transfers between devices  81.1 us (30%)
  blocking collectives  28.1 us (10%)
  starting transfers between devices  25 us (9%)
  between operations  14.9 us (5%)
  local copies, waits for them, and re-layouts  11.8 us (4%)
  other arithmetic  8.82 us (3%)
    pallas_call x1, Pallas kernels, stencil(): pl.pallas_call(stencil_kernel, out_shape=(jax.ShapeDtypeStruct((32, 4, 12...  61.5 us
    psum x1, waiting for transfers between devices, per_device(): adjoint = lax.psum(adjoint, 'mem').reshape(32, 32, 128)  40.8 us
    all_to_all x1, blocking collectives, per_device(): lax.all_to_all(departure, ('tx', 'ty'), split_axis=0, concat_axis=0, tile...  28.1 us
    ppermute x8, waiting for transfers between devices, shifted(): lax.ppermute(value, axis, [(i, (i + by) % count) for i in range(count)])  21.8 us
    psum x1, waiting for transfers between devices, per_device(): increment = lax.psum(partial, 'mem') + bg_sigma * static_ctrl  18.5 us
    pallas_call x1, Pallas kernels, backward(): pl.pallas_call(backward_kernel, grid=(5,), out_shape=jax.ShapeDtypeStruct...  16.1 us
    ppermute x8, starting transfers between devices, shifted(): lax.ppermute(value, axis, [(i, (i + by) % count) for i in range(count)])  16.1 us
    pallas_call x1, Pallas kernels, forward(): pl.pallas_call(forward_kernel, grid=(5,), out_shape=jax.ShapeDtypeStruct(...  11.7 us
  transfers between devices with their start and end apart: 11, of which 6 were waited for; matrix products, arithmetic and copies ran while one was open for 5% of the time, Pallas kernels for 5%

profile of v1, /device:TPU:0, one launch (start us, length us, event | category | flops | bytes accessed | tf_op | source)
XLA Modules:
  0.0 273.3 jit_solution(17211309727392510715)
XLA Ops:
  7.2 0.0 copy-start.1
  7.2 0.0 all-reduce.3.cloned.1.call-start
  7.2 1.1 slice.128
  8.3 1.6 collective-permute-start
  9.9 1.0 slice.129
  11.0 3.6 %collective-permute-start.1 = (f32[5,32,640]{2,1,0:T(8,128)S(1)}, f32[5,32,640]{2,1,0:T(8,128)S(1)}, u32[]{:S(2)}, u32[]{:S(2)}) collective-permute-start(f32[5,32,640]{2,1,0:T(8,128)S(1)} %slice.129), channel_id=1, source_target_pairs={{0,112},{16,0},{32,16},{48,32},{64,48},{80,64},{96,80},{112,96},{1... | collective-permute-start | bytes 1228808 | tf_op jit(solution)/shard_map/ppermute | solution.py:291
  14.5 0.0 copy-done.7
  14.5 0.1 copy.19
  14.6 7.3 %collective-permute-done = f32[4,32,640]{2,1,0:T(8,128)S(1)} collective-permute-done((f32[4,32,640]{2,1,0:T(8,128)S(1)}, f32[4,32,640]{2,1,0:T(8,128)S(1)}, u32[]{:S(2)}, u32[]{:S(2)}) %collective-permute-start) | collective-permute-done | bytes 327712 | tf_op jit(solution)/shard_map/ppermute | solution.py:291
  22.0 6.0 %collective-permute-done.1 = f32[5,32,640]{2,1,0:T(8,128)S(1)} collective-permute-done((f32[5,32,640]{2,1,0:T(8,128)S(1)}, f32[5,32,640]{2,1,0:T(8,128)S(1)}, u32[]{:S(2)}, u32[]{:S(2)}) %collective-permute-start.1) | collective-permute-done | bytes 409632 | tf_op jit(solution)/shard_map/ppermute | solution.py:291
  28.1 1.6 collective-permute-start.2
  29.8 1.7 collective-permute-start.3
  31.4 0.1 broadcast_multiply_fusion
  31.6 0.2 mul.50
  31.7 0.6 pad_maximum_fusion.1.mix_ref
  32.4 6.2 %collective-permute-done.2 = f32[17,8,640]{2,1,0:T(8,128)} collective-permute-done((f32[17,8,640]{2,1,0:T(8,128)S(1)}, f32[17,8,640]{2,1,0:T(8,128)}, u32[]{:S(2)}, u32[]{:S(2)}) %collective-permute-start.2) | collective-permute-done | bytes 348192 | tf_op jit(solution)/shard_map/ppermute | solution.py:291
  38.6 0.0 collective-permute-done.3
  38.6 2.6 pad_maximum_fusion.ext_ref
  41.2 0.0 copy-start.12
  41.2 0.0 copy-start.13
  41.2 11.7 %forward.1 = f32[32,32,128]{2,1,0:T(8,128)} custom-call(f32[17,48,640]{2,1,0:T(8,128)} %pad_maximum_fusion.ext_ref, bf16[20,32,32,128]{3,2,1,0:T(8,128)(2,1)} %pert_ref.3, bf16[384,128]{1,0:T(8,128)(2,1)} %pad_maximum_fusion.1.mix_ref, bf16[80,128]{1,0:T(8,128)(2,1)} %constant.116.clone.sy_ref, bf16[256,256]{1,0:T(8,128)(2,1)} %constant.118.clone.sx_ref), custom_call_target="tpu_custom_call" | custom-call | tf_op jit(solution)/shard_map/forward/pallas_call | solution.py:228
  52.9 0.0 all-reduce.3.cloned.1.call-update
  53.0 0.7 copy.23
  53.6 0.5 broadcast.79
  54.1 0.7 reduce.11
  54.8 0.6 reshape_squeeze.3.owner_ref
  55.5 0.6 reshape.170.col_ref
  56.1 0.6 reshape.171.lev_ref
  56.7 0.6 reshape.173.inn_ref
  57.3 0.6 reshape.174.rinv_ref
  58.6 0.0 copy-start.3
  58.6 0.0 copy-start.4
  58.6 10.9 %route.1 = (f32[32,24,128]{2,1,0:T(8,128)}, s32[32,256]{1,0:T(8,128)}) custom-call(s32[1]{0:T(128)S(6)} %copy.32.cnt_ref, s32[32,256]{1,0:T(8,128)} %reshape_squeeze.3.owner_ref, s32[32,256]{1,0:T(8,128)} %reshape.170.col_ref, s32[32,256]{1,0:T(8,128)} %reshape.171.lev_ref, f32[3,32,256]{2,1,0:T(8,128)} %bitcast.14, f32[32,256]{1,0:T(8,128)} %reshape.173.inn_ref, ...), custom_call_target="tpu_custom_call" | custom-call | flops 4000000000 | bytes 1000000 | tf_op jit(solution)/shard_map/route/pallas_call | solution.py:74
  69.5 8.6 %all-to-all-start = ((f32[32,24,128]{2,1,0:T(8,128)}), f32[32,24,128]{2,1,0:T(8,128)S(1)}, u32[]{:S(2)}, u32[]{:S(2)}) async-start(f32[32,24,128]{2,1,0:T(8,128)} %get-tuple-element.55), calls=%async_computation | async-start | bytes 786432 | tf_op jit(solution)/shard_map/all_to_all | solution.py:300
  78.1 0.2 all-reduce.5.cloned.1.call-start
  78.4 18.5 %all-reduce.3.cloned.1.call-done = f32[32,32,128]{2,1,0:T(8,128)} async-done(((f32[32,32,128]{2,1,0:T(8,128)}), f32[32,32,128]{2,1,0:T(8,128)}) %all-reduce.3.cloned.1.call-update) | async-done | bytes 524304 | tf_op jit(solution)/shard_map/psum | solution.py:306
  96.9 2.0 multiply_add_fusion.1
  98.8 0.0 all-to-all-done.obs_ref
  98.8 0.8 copy-done.5
  99.6 61.5 %stencil.1 = (f32[32,4,128]{2,1,0:T(4,128)}, f32[1024,128]{1,0:T(8,128)}) custom-call(f32[1024,128]{1,0:T(8,128)} %bitcast.11, f32[32,24,128]{2,1,0:T(8,128)} %copy-done.5), custom_call_target="tpu_custom_call" | custom-call | tf_op jit(solution)/shard_map/stencil/pallas_call | solution.py:155
  161.0 0.0 all-reduce.5.cloned.1.call-update
  161.1 0.2 mul.54
  161.3 0.6 pad_maximum_fusion.2.mix_ref
  161.9 40.8 %all-reduce.5.cloned.1.call-done.adj_ref = f32[32,32,128]{2,1,0:T(8,128)} async-done(((f32[32,32,128]{2,1,0:T(8,128)}), f32[32,32,128]{2,1,0:T(8,128)}) %all-reduce.5.cloned.1.call-update) | async-done | bytes 524304 | tf_op jit(solution)/shard_map/psum | solution.py:309
  202.8 16.1 %backward.1 = f32[17,48,640]{2,1,0:T(8,128)} custom-call(f32[32,32,128]{2,1,0:T(8,128)} %all-reduce.5.cloned.1.call-done.adj_ref, bf16[20,32,32,128]{3,2,1,0:T(8,128)(2,1)} %pert_ref.3, bf16[384,128]{1,0:T(8,128)(2,1)} %pad_maximum_fusion.2.mix_ref, bf16[40,256]{1,0:T(8,128)(2,1)} %constant.117.clone.gy_ref, bf16[128,512]{1,0:T(8,128)(2,1)} %constant.119.clone.gx_ref), custom_call_target="tpu_custom_call" | custom-call | tf_op jit(solution)/shard_map/backward/pallas_call | solution.py:265
  218.8 1.1 slice.146
  220.0 0.6 collective-permute-start.4
  220.6 1.1 slice.148
  221.7 3.6 %collective-permute-start.5 = (f32[4,48,640]{2,1,0:T(8,128)S(1)}, f32[4,48,640]{2,1,0:T(8,128)S(1)}, u32[]{:S(2)}, u32[]{:S(2)}) collective-permute-start(f32[4,48,640]{2,1,0:T(8,128)S(1)} %slice.148), channel_id=1, source_target_pairs={{0,112},{16,0},{32,16},{48,32},{64,48},{80,64},{96,80},{112,96},{1... | collective-permute-start | bytes 1474568 | tf_op jit(solution)/shard_map/ppermute | solution.py:291
  225.3 28.1 %all_to_all.10 = f32[32,4,128]{2,1,0:T(4,128)} all-to-all(f32[32,4,128]{2,1,0:T(4,128)S(1)} %copy-done.8), channel_id=1, replica_groups=mesh['tx'=8,'ty'=4,'mem'=4] {'tx','ty'}, dimensions={0} | all-to-all | bytes 131072 | tf_op jit(solution)/shard_map/all_to_all | solution.py:308
  253.4 3.4 %unroute.1 = f32[32,256]{1,0:T(8,128)} custom-call(s32[32,256]{1,0:T(8,128)} %get-tuple-element.57.tgt_ref, f32[128,128]{1,0:T(8,128)} %bitcast.16), custom_call_target="tpu_custom_call" | custom-call | flops 600000000 | bytes 200000 | tf_op jit(solution)/shard_map/unroute/pallas_call | solution.py:100
  256.8 1.5 copy.21
  258.3 0.0 collective-permute-done.4
  258.3 0.1 fusion
  258.4 0.0 collective-permute-done.5
  258.4 0.1 fusion.1
  258.5 0.7 collective-permute-start.6
  259.3 0.1 copy-done.2
  259.3 0.9 multiply_add_fusion
  260.4 2.6 collective-permute-start.7
  262.9 2.2 collective-permute-done.6
  265.2 0.3 scatter-add.16
  265.5 0.0 collective-permute-done.7
  265.5 0.9 add.46
  (34 shorter events, 0.4 us)
Async XLA Ops:
  7.2 14.8 %copy-start.1 = (f32[8,32,640]{2,1,0:T(8,128)S(1)}, f32[8,32,640]{2,1,0:T(8,128)}, u32[]{:S(2)}) copy-start(f32[8,32,640]{2,1,0:T(8,128)} %param.24) | copy-start | bytes 1966084
  7.2 7.3 %copy-start.7 = (f32[32,32]{1,0:T(8,128)S(1)}, f32[32,32]{1,0:T(8,128)}, u32[]{:S(2)}) copy-start(f32[32,32]{1,0:T(8,128)} %param.25) | copy-start | bytes 12292
  7.2 89.7 %all-reduce.3.cloned.1.call-start = ((), (), s32[]{:S(2)}) async-start(), calls=%async_computation.2 | async-start | bytes 1048576 | tf_op jit(solution)/shard_map/psum | solution.py:306
  8.3 13.7 %collective-permute-start = (f32[4,32,640]{2,1,0:T(8,128)S(1)}, f32[4,32,640]{2,1,0:T(8,128)S(1)}, u32[]{:S(2)}, u32[]{:S(2)}) collective-permute-start(f32[4,32,640]{2,1,0:T(8,128)S(1)} %slice.128), channel_id=1, source_target_pairs={{0,16},{16,32},{32,48},{48,64},{64,80},{80,96},{96,112},{112,0},{1... | collective-permute-start | bytes 983048 | tf_op jit(solution)/shard_map/ppermute | solution.py:291
  11.0 17.1 %collective-permute-start.1 = (f32[5,32,640]{2,1,0:T(8,128)S(1)}, f32[5,32,640]{2,1,0:T(8,128)S(1)}, u32[]{:S(2)}, u32[]{:S(2)}) collective-permute-start(f32[5,32,640]{2,1,0:T(8,128)S(1)} %slice.129), channel_id=1, source_target_pairs={{0,112},{16,0},{32,16},{48,32},{64,48},{80,64},{96,80},{112,96},{1... | collective-permute-start | bytes 1228808 | tf_op jit(solution)/shard_map/ppermute | solution.py:291
  28.1 10.5 %collective-permute-start.2 = (f32[17,8,640]{2,1,0:T(8,128)S(1)}, f32[17,8,640]{2,1,0:T(8,128)}, u32[]{:S(2)}, u32[]{:S(2)}) collective-permute-start(f32[17,8,640]{2,1,0:T(8,128)S(1)} %get-tuple-element.63), channel_id=1, source_target_pairs={{0,4},{4,8},{8,12},{12,0},{1,5},{5,9},{9,13},{13,1},{2,6},{6,10},{... | collective-permute-start | bytes 1044488 | tf_op jit(solution)/shard_map/ppermute | solution.py:291
  29.8 8.8 %collective-permute-start.3 = (f32[17,8,640]{2,1,0:T(8,128)S(1)}, f32[17,8,640]{2,1,0:T(8,128)}, u32[]{:S(2)}, u32[]{:S(2)}) collective-permute-start(f32[17,8,640]{2,1,0:T(8,128)S(1)} %get-tuple-element.64), channel_id=1, source_target_pairs={{0,12},{4,0},{8,4},{12,8},{1,13},{5,1},{9,5},{13,9},{2,14},{6,2},{... | collective-permute-start | bytes 1044488 | tf_op jit(solution)/shard_map/ppermute | solution.py:291
  41.2 11.8 %copy-start.6 = (f32[3,8192]{1,0:T(4,128)S(1)}, f32[3,8192]{1,0:T(4,128)}, u32[]{:S(2)}) copy-start(f32[3,8192]{1,0:T(4,128)} %param.32) | copy-start | bytes 294916
  41.2 13.0 %copy-start.9 = (s32[8192,1]{0,1:T(1,128)S(1)}, s32[8192,1]{0,1:T(1,128)}, u32[]{:S(2)}) copy-start(s32[8192,1]{0,1:T(1,128)} %param.29) | copy-start | bytes 98308
  41.2 14.3 %copy-start.10 = (s32[8192]{0:T(1024)S(1)}, s32[8192]{0:T(1024)}, u32[]{:S(2)}) copy-start(s32[8192]{0:T(1024)} %param.30) | copy-start | bytes 98308
  41.2 14.9 %copy-start.11 = (s32[8192]{0:T(1024)S(1)}, s32[8192]{0:T(1024)}, u32[]{:S(2)}) copy-start(s32[8192]{0:T(1024)} %param.31) | copy-start | bytes 98308
  41.2 15.5 %copy-start.12 = (f32[8192]{0:T(1024)S(1)}, f32[8192]{0:T(1024)}, u32[]{:S(2)}) copy-start(f32[8192]{0:T(1024)} %param.33) | copy-start | bytes 98308
  41.2 16.1 %copy-start.13 = (f32[8192]{0:T(1024)S(1)}, f32[8192]{0:T(1024)}, u32[]{:S(2)}) copy-start(f32[8192]{0:T(1024)} %param.34) | copy-start | bytes 98308
  58.6 38.3 %copy-start.3 = (f32[32,32,128]{2,1,0:T(8,128)S(1)}, f32[32,32,128]{2,1,0:T(8,128)}, u32[]{:S(2)}) copy-start(f32[32,32,128]{2,1,0:T(8,128)} %param.27) | copy-start | bytes 1572868
  58.6 38.3 %copy-start.4 = (f32[32,32,128]{2,1,0:T(8,128)S(1)}, f32[32,32,128]{2,1,0:T(8,128)}, u32[]{:S(2)}) copy-start(f32[32,32,128]{2,1,0:T(8,128)} %param.28) | copy-start | bytes 1572868
  69.5 29.4 %all-to-all-start = ((f32[32,24,128]{2,1,0:T(8,128)}), f32[32,24,128]{2,1,0:T(8,128)S(1)}, u32[]{:S(2)}, u32[]{:S(2)}) async-start(f32[32,24,128]{2,1,0:T(8,128)} %get-tuple-element.55), calls=%async_computation | async-start | bytes 786432 | tf_op jit(solution)/shard_map/all_to_all | solution.py:300
  78.1 124.6 %all-reduce.5.cloned.1.call-start = ((), (), s32[]{:S(2)}) async-start(), calls=%async_computation.3 | async-start | bytes 1048576 | tf_op jit(solution)/shard_map/psum | solution.py:309
  98.8 0.8 copy-start.5
  218.8 6.5 %copy-start.8 = (f32[32,4,128]{2,1,0:T(4,128)S(1)}, f32[32,4,128]{2,1,0:T(4,128)}, u32[]{:S(2)}) copy-start(f32[32,4,128]{2,1,0:T(4,128)} %get-tuple-element.58) | copy-start | bytes 196612
  220.0 38.3 %collective-permute-start.4 = (f32[5,48,640]{2,1,0:T(8,128)S(1)}, f32[5,48,640]{2,1,0:T(8,128)S(1)}, u32[]{:S(2)}, u32[]{:S(2)}) collective-permute-start(f32[5,48,640]{2,1,0:T(8,128)S(1)} %slice.146), channel_id=1, source_target_pairs={{0,16},{16,32},{32,48},{48,64},{64,80},{80,96},{96,112},{112,0},{1... | collective-permute-start | bytes 1843208 | tf_op jit(solution)/shard_map/ppermute | solution.py:291
  221.7 36.7 %collective-permute-start.5 = (f32[4,48,640]{2,1,0:T(8,128)S(1)}, f32[4,48,640]{2,1,0:T(8,128)S(1)}, u32[]{:S(2)}, u32[]{:S(2)}) collective-permute-start(f32[4,48,640]{2,1,0:T(8,128)S(1)} %slice.148), channel_id=1, source_target_pairs={{0,112},{16,0},{32,16},{48,32},{64,48},{80,64},{96,80},{112,96},{1... | collective-permute-start | bytes 1474568 | tf_op jit(solution)/shard_map/ppermute | solution.py:291
  253.4 4.9 %copy-start = (f32[17,48,640]{2,1,0:T(8,128)S(1)}, f32[17,48,640]{2,1,0:T(8,128)}, u32[]{:S(2)}) copy-start(f32[17,48,640]{2,1,0:T(8,128)} %backward.1) | copy-start | bytes 6266884
  256.8 1.5 slice-start
  258.3 1.0 copy-start.2
  258.5 6.6 %collective-permute-start.6 = (f32[8,5,640]{2,1,0:T(8,128)S(1)}, f32[8,5,640]{2,1,0:T(8,128)S(1)}, u32[]{:S(2)}, u32[]{:S(2)}) collective-permute-start(f32[8,5,640]{2,1,0:T(8,128)S(1)} %slice.151), channel_id=1, source_target_pairs={{0,4},{4,8},{8,12},{12,0},{1,5},{5,9},{9,13},{13,1},{2,6},{6,10},{... | collective-permute-start | bytes 307208 | tf_op jit(solution)/shard_map/ppermute | solution.py:291
  260.4 5.1 %collective-permute-start.7 = (f32[8,4,640]{2,1,0:T(4,128)S(1)}, f32[8,4,640]{2,1,0:T(4,128)S(1)}, u32[]{:S(2)}, u32[]{:S(2)}) collective-permute-start(f32[8,4,640]{2,1,0:T(4,128)S(1)} %slice.153), channel_id=1, source_target_pairs={{0,12},{4,0},{8,4},{12,8},{1,13},{5,1},{9,5},{13,9},{2,14},{6,2},{... | collective-permute-start | bytes 245768 | tf_op jit(solution)/shard_map/ppermute | solution.py:291
Sparse Core Ops, SparseCore 0:
  53.1 43.7 all-reduce.2
  161.2 41.5 all-reduce.4

commit v2 on v1

v2 whole, which is shorter than its diff:
```python
import functools
import numpy as np
import jax
import jax.numpy as jnp
from jax import lax
from jax.experimental import pallas as pl
from jax.experimental.pallas import tpu as pltpu
from jax.sharding import PartitionSpec as P

F32 = jnp.float32
BF16 = jnp.bfloat16
NU = 0.2
RATIO = 4
VMEM_LIMIT = 56 * 1024 * 1024
NN = (((1,), (0,)), ((), ()))
NT = (((1,), (1,)), ((), ()))
TN = (((0,), (0,)), ((), ()))


def mm(a, b, dims=NN):
    return lax.dot_general(a, b, dims, preferred_element_type=F32)


def split(v):
    hi = v.astype(BF16)
    return hi, (v - hi.astype(F32)).astype(BF16)


def iota(shape, dim):
    return lax.broadcasted_iota(jnp.int32, shape, dim)


def tent(position, count):
    return jnp.maximum(1.0 - jnp.abs(position - iota((count, 128), 0).astype(F32)), 0.0)


def stencil_kernel(inc_ref, obs_ref, dep_ref, adj_ref, table_ref, acc_ref, ahi_ref, alo_ref):
    turned = inc_ref[...].T
    hi, lo = split(turned)
    table_ref[0:128] = hi
    table_ref[128:256] = lo
    acc_ref[...] = jnp.zeros_like(acc_ref)

    def one_source(s, carry):
        cols = []
        for q in range(4):
            get = lambda ch: obs_ref[s, ch * 4 + q:ch * 4 + q + 1, :]
            base = get(5).astype(jnp.int32)
            pos_l = (base // 4096).astype(F32) + get(2)
            pos_x = ((base // 128) % 32).astype(F32) + get(0)
            pos_y = (base % 128).astype(F32) + get(1)
            in_l, in_x = tent(pos_l, 32), tent(pos_x, 32)
            cols.append(tent(pos_y, 128))
            for l in range(32):
                hi, lo = split(in_l[l:l + 1] * in_x)
                ahi_ref[l * 32:(l + 1) * 32, q * 128:(q + 1) * 128] = hi
                alo_ref[l * 32:(l + 1) * 32, q * 128:(q + 1) * 128] = lo
        both = mm(table_ref[...], ahi_ref[...])
        picked = both[:128] + both[128:] + mm(table_ref[0:128], alo_ref[...])
        shi, slo = [], []
        for q in range(4):
            dep = jnp.sum(picked[:, q * 128:(q + 1) * 128] * cols[q], 0, keepdims=True) - obs_ref[s, 12 + q:13 + q, :]
            dep_ref[s, q:q + 1, :] = dep
            hi, lo = split(cols[q] * (dep * obs_ref[s, 16 + q:17 + q, :]))
            shi.append(hi)
            slo.append(lo)
        shi = jnp.concatenate(shi, 1)
        slo = jnp.concatenate(slo, 1)
        acc_ref[...] += mm(ahi_ref[...], shi, NT) + mm(ahi_ref[...], slo, NT) + mm(alo_ref[...], shi, NT)
        return carry

    lax.fori_loop(0, obs_ref.shape[0], one_source, 0)
    adj_ref[...] = acc_ref[...]


def stencil(inc, obs):
    return pl.pallas_call(
        stencil_kernel,
        out_shape=(jax.ShapeDtypeStruct((32, 4, 128), F32), jax.ShapeDtypeStruct((1024, 128), F32)),
        in_specs=[pl.BlockSpec(memory_space=pltpu.VMEM)] * 2,
        out_specs=(pl.BlockSpec(memory_space=pltpu.VMEM),) * 2,
        scratch_shapes=[
            pltpu.VMEM((256, 1024), BF16),
            pltpu.VMEM((1024, 128), F32),
            pltpu.VMEM((1024, 512), BF16),
            pltpu.VMEM((1024, 512), BF16),
        ],
        compiler_params=pltpu.CompilerParams(vmem_limit_bytes=VMEM_LIMIT),
        name="stencil",
    )(inc, obs)


def line_weights(fine, coarse):
    out = np.zeros((fine, coarse), np.float32)
    for f in range(fine):
        out[f, f // RATIO] += 1.0 - (f % RATIO) / RATIO
        out[f, f // RATIO + 1] += (f % RATIO) / RATIO
    return out


def tables():
    along = line_weights(128, 40)
    across = line_weights(32, 16)
    spread_y = np.concatenate([along.T, along.T], 0)
    gather_y = np.concatenate([along.T, along.T], 1)
    eye = np.eye(8, dtype=np.float32)
    block = np.kron(eye, across)
    spread_x = np.concatenate([block, block], 1)
    gather_x = np.concatenate([block.T, block.T], 1)
    return [jnp.asarray(t, BF16) for t in (spread_y, gather_y, spread_x, gather_x)]


def diffuse_rows(field, first, last):
    near = field[first - 1:last - 1] + field[first + 1:last + 1]
    mid = field[first:last]
    near = near + pltpu.roll(mid, 1, 1) + pltpu.roll(mid, 47, 1)
    return mid + NU * (near - 4.0 * mid)


def three(a, b_ref):
    hi, lo = split(a)
    return mm(jnp.concatenate([hi, lo, hi], 1), b_ref[...])

MESH = pl.DeviceIdType.MESH
GROUPS = 32
CHUNKS = 5
BLOCKS = 4


def tile_id(index, mem):
    return (index // 4, index % 4, mem)


def remote(src, dst, send, recv, device):
    return pltpu.make_async_remote_copy(src_ref=src, dst_ref=dst, send_sem=send, recv_sem=recv, device_id=device, device_id_type=MESH)


class Place:
    def __init__(self):
        self.tx, self.ty, self.mem = lax.axis_index("tx"), lax.axis_index("ty"), lax.axis_index("mem")
        self.tile = self.tx * 4 + self.ty
        self.core = self.mem % 2
        self.below = (lax.rem(self.tx + 1, 8), self.ty, self.mem)
        self.above = (lax.rem(self.tx + 7, 8), self.ty, self.mem)
        self.right = (self.tx, lax.rem(self.ty + 1, 4), self.mem)
        self.left = (self.tx, lax.rem(self.ty + 3, 4), self.mem)
        self.twin = (self.tx, self.ty, self.mem + 1 - 2 * self.core)
        self.across = (self.tx, self.ty, lax.rem(self.mem + 2, 4))

    def greet(self):
        barrier = pltpu.get_barrier_semaphore()

        def one(d, carry):
            other = lax.rem(self.tile + d, GROUPS)
            pl.semaphore_signal(barrier, inc=1, device_id=tile_id(other, self.mem), device_id_type=MESH)
            return carry

        lax.fori_loop(1, GROUPS, one, 0)
        for other in (self.twin, self.across):
            pl.semaphore_signal(barrier, inc=1, device_id=other, device_id_type=MESH)
        pl.semaphore_wait(barrier, GROUPS + 1)


class Exchange:
    def __init__(self, place, src, dst, send, recv, own):
        self.place, self.src, self.dst, self.send, self.recv = place, src, dst, send, recv
        self.own = pltpu.make_async_copy(src.at[place.tile], dst.at[place.tile], own)

    def copy(self, d):
        other = lax.rem(self.place.tile + d, GROUPS)
        return remote(self.src.at[other], self.dst.at[self.place.tile], self.send.at[d], self.recv.at[d], tile_id(other, self.place.mem))

    def start(self):
        self.own.start()

        def one(d, carry):
            self.copy(d).start()
            return carry

        lax.fori_loop(1, GROUPS, one, 0)

    def wait(self):
        self.own.wait()

        def one(d, carry):
            self.copy(d).wait()
            return carry

        lax.fori_loop(1, GROUPS, one, 0)


class MemSum:
    def __init__(self, place, part, total, half, got, far, send, recv):
        self.place, self.part, self.total = place, part, total
        self.half, self.got, self.far, self.send, self.recv = half, got, far, send, recv

    def mine(self, b):
        return pl.ds(8 * b + 4 * self.place.core, 4)

    def near(self, b):
        return remote(self.part.at[pl.ds(8 * b + 4 - 4 * self.place.core, 4)], self.got.at[b], self.send.at[0, b], self.recv.at[0, b], self.place.twin)

    def over(self, b):
        return remote(self.half.at[b], self.far.at[b], self.send.at[1, b], self.recv.at[1, b], self.place.across)

    def back(self, b):
        return remote(self.total.at[self.mine(b)], self.total.at[self.mine(b)], self.send.at[2, b], self.recv.at[2, b], self.place.twin)

    def second(self, b):
        self.near(b).wait()
        self.half[b] = self.part[self.mine(b)] + self.got[b]
        self.over(b).start()

    def third(self, b, extra):
        self.over(b).wait()
        self.total[self.mine(b)] = self.half[b] + self.far[b] + extra(self.mine(b))
        self.back(b).start()

    def last(self, b):
        self.back(b).wait()


MEM_SCRATCH = [pltpu.VMEM((BLOCKS, 4, 32, 128), F32)] * 3 + [pltpu.SemaphoreType.DMA((3, BLOCKS))] * 2


def route_ranks(cnt_ref, owner_ref, col_ref, lev_ref, frac_ref, inn_ref, rinv_ref, tgt_ref, high_ref, low_ref, term_ref):
    rows, wide = owner_ref.shape
    place = iota((rows, wide), 0) * wide + iota((rows, wide), 1)
    live = place < cnt_ref[0]
    owner = jnp.where(live, owner_ref[...], GROUPS)
    same = iota((rows, GROUPS, wide), 1) == owner[:, None, :]
    onehot = jnp.where(same, 1.0, 0.0).astype(BF16).reshape(rows * GROUPS, wide)
    lower = iota((wide, 2 * wide), 0) < iota((wide, 2 * wide), 1)
    both = mm(onehot, jnp.where(lower, 1.0, 0.0).astype(BF16))
    inside, totals = both[:, :wide].reshape(rows, GROUPS, wide), both[:, wide:].reshape(rows, GROUPS, wide)
    running = jnp.zeros((GROUPS, wide), F32)
    ranks = []
    for c in range(rows):
        ranks.append(jnp.sum(jnp.where(same[c], inside[c] + running, 0.0), 0, keepdims=True))
        running = running + totals[c]
    rank = jnp.concatenate(ranks, 0).astype(jnp.int32)
    tgt_ref[...] = jnp.where(live, owner * 512 + rank, -1)
    high_ref[...] = jnp.where(live, rank // 128 * GROUPS + owner, -1)
    low_ref[...] = rank % 128
    base = (lev_ref[...] * 4096 + col_ref[...]).astype(F32)
    for at, v in ((3, inn_ref[...]), (4, rinv_ref[...]), (5, base)):
        hi, lo = split(v)
        term_ref[2 * at] = hi.astype(F32)
        term_ref[2 * at + 1] = lo.astype(F32)
    for at in range(3):
        for r in range(rows):
            hi, lo = split(frac_ref[at:at + 1, wide * r:wide * (r + 1)])
            term_ref[2 * at, r:r + 1] = hi.astype(F32)
            term_ref[2 * at + 1, r:r + 1] = lo.astype(F32)


def route_slots(high_ref, low_ref, term_ref, acc_ref, out_ref):
    acc_ref[...] = jnp.zeros_like(acc_ref)

    def one(c, carry):
        def pair(ref, *at):
            r = 2 * c
            return jnp.concatenate([ref[(*at, pl.ds(r, 1), slice(None))], ref[(*at, pl.ds(r + 1, 1), slice(None))]], 1)

        hit = jnp.where(iota((128, 256), 0) == pair(high_ref), 1.0, 0.0).astype(BF16)
        lane = jnp.where(iota((128, 256), 0) == pair(low_ref), 1.0, 0.0).astype(BF16)
        stack = jnp.concatenate([lane * pair(term_ref, t).astype(BF16) for t in range(12)], 0)
        acc_ref[...] += mm(hit, stack, NT)
        return carry

    lax.fori_loop(0, 32, one, 0, unroll=2)
    for ch in range(6):
        full = acc_ref[:, 256 * ch:256 * ch + 128] + acc_ref[:, 256 * ch + 128:256 * ch + 256]
        for q in range(4):
            out_ref[:, ch * 4 + q, :] = full[q * GROUPS:(q + 1) * GROUPS]


def unroute(tgt_ref, ret, out_ref):
    rows = tgt_ref.shape[0]
    hi, lo = split(ret.T)
    table = jnp.concatenate([hi, lo], 0)
    for c in range(0, rows, 2):
        tgt = jnp.concatenate([tgt_ref[c:c + 1], tgt_ref[c + 1:c + 2]], 1)
        hit = jnp.where(iota((128, 256), 0) == tgt // 128, 1.0, 0.0).astype(BF16)
        picked = mm(table, hit)
        picked = picked[:128] + picked[128:]
        row = jnp.sum(jnp.where((iota((128, 256), 0) == tgt % 128) & (tgt >= 0), picked, 0.0), 0, keepdims=True)
        out_ref[c:c + 1] = row[:, :128]
        out_ref[c + 1:c + 2] = row[:, 128:]


def diffuse_rows(field):
    near = field[:-2] + field[2:]
    mid = field[1:-1]
    near = near + pltpu.roll(mid, 1, 1) + pltpu.roll(mid, 47, 1)
    return mid + NU * (near - 4.0 * mid)


def three(a, b):
    hi, lo = split(a)
    bhi, blo = split(b)
    return mm(jnp.concatenate([hi, lo, hi], 1), jnp.concatenate([bhi, bhi, blo], 0))


def forward_kernel(
    cnt_ref, owner_ref, col_ref, lev_ref, frac_ref, inn_ref, rinv_ref, alpha_ref, pert_hbm, bg_ref, static_ref, mix_ref, sy_ref, sx_ref,
    inc_ref, obs_ref, tgt_ref,
    ext_ref, pert_ref, turn_ref, part_ref, out_ref, high_ref, low_ref, term_ref, acc_ref,
    half_ref, got_ref, far_ref, msend, mrecv,
    xsend, xrecv, ysend, yrecv, osend, orecv, own,
):
    place = Place()

    def x_copies(g):
        lanes = pl.ds(pl.multiple_of(g * 128, 128), 128)
        return (
            remote(alpha_ref.at[4:8, :, lanes], ext_ref.at[g, 0:4, 8:40], xsend.at[0, g], xrecv.at[0, g], place.below),
            remote(alpha_ref.at[0:5, :, lanes], ext_ref.at[g, 12:17, 8:40], xsend.at[1, g], xrecv.at[1, g], place.above),
        )

    def y_copies(g):
        return (
            remote(ext_ref.at[g, :, 32:40], ext_ref.at[g, :, 0:8], ysend.at[0, g], yrecv.at[0, g], place.right),
            remote(ext_ref.at[g, :, 8:16], ext_ref.at[g, :, 40:48], ysend.at[1, g], yrecv.at[1, g], place.left),
        )

    def own_copy(g):
        lanes = pl.ds(pl.multiple_of(g * 128, 128), 128)
        return pltpu.make_async_copy(alpha_ref.at[:, :, lanes], ext_ref.at[g, 4:12, 8:40], own.at[g])

    pert_copy = pltpu.make_async_copy(pert_hbm, pert_ref, own.at[CHUNKS])
    exchange = Exchange(place, out_ref, obs_ref, osend, orecv, own.at[CHUNKS + 1])
    total = MemSum(place, part_ref, inc_ref, half_ref, got_ref, far_ref, msend, mrecv)

    place.greet()

    def begin(g, carry):
        for copy in x_copies(g):
            copy.start()
        own_copy(g).start()
        return carry

    lax.fori_loop(0, CHUNKS, begin, 0)
    pert_copy.start()
    turn_ref[...] = jnp.zeros_like(turn_ref)
    route_ranks(cnt_ref, owner_ref, col_ref, lev_ref, frac_ref, inn_ref, rinv_ref, tgt_ref, high_ref, low_ref, term_ref)
    route_slots(high_ref, low_ref, term_ref, acc_ref, out_ref)

    def sideways(g, carry):
        for copy in x_copies(g):
            copy.wait()
        own_copy(g).wait()
        for copy in y_copies(g):
            copy.start()
        return carry

    lax.fori_loop(0, CHUNKS, sideways, 0)
    exchange.start()

    def smooth(g, carry):
        for copy in y_copies(g):
            copy.wait()
        field = ext_ref[g]
        for step in range(4):
            field = diffuse_rows(field)
        field = three(field[:, 8:48].reshape(9 * 40, 128), mix_ref[...]).reshape(9, 40, 128)
        for a in range(9):
            hi, lo = split(field[a])
            turn_ref[pl.ds(pl.multiple_of(g * 128, 128), 128), a, :] = mm(jnp.concatenate([hi, lo], 0), sy_ref[...], TN)
        return carry

    lax.fori_loop(0, CHUNKS, smooth, 0)
    pert_copy.wait()

    def block(b):
        def member(k, carry):
            hi, lo = split(turn_ref[pl.ds(k * 32 + 8 * b, 8)].reshape(128, 128))
            fine = mm(sx_ref[...], jnp.concatenate([hi, lo], 0)).reshape(8, 32, 128)
            return carry + fine * pert_ref[k, 8 * b:8 * b + 8].astype(F32)

        part_ref[8 * b:8 * b + 8] = lax.fori_loop(0, 20, member, jnp.zeros((8, 32, 128), F32), unroll=4)

    extra = lambda at: bg_ref[at] * static_ref[at]
    for s in range(BLOCKS + 3):
        if s < BLOCKS:
            block(s)
            total.near(s).start()
        if 0 <= s - 1 < BLOCKS:
            total.second(s - 1)
        if 0 <= s - 2 < BLOCKS:
            total.third(s - 2, extra)
        if 0 <= s - 3 < BLOCKS:
            total.last(s - 3)
    exchange.wait()


VMEM = pl.BlockSpec(memory_space=pltpu.VMEM)
SMEM = pl.BlockSpec(memory_space=pltpu.SMEM)
ANY = pl.BlockSpec(memory_space=pl.ANY)
DMA = pltpu.SemaphoreType.DMA


def forward(cnt, owner, col, lev, frac, inn, rinv, alpha, pert, bg, static, mix, sy, sx):
    return pl.pallas_call(
        forward_kernel,
        out_shape=(
            jax.ShapeDtypeStruct((32, 32, 128), F32),
            jax.ShapeDtypeStruct((GROUPS, 24, 128), F32),
            jax.ShapeDtypeStruct((64, 128), jnp.int32),
        ),
        in_specs=[SMEM] + [VMEM] * 6 + [ANY] * 2 + [VMEM] * 5,
        out_specs=(VMEM, VMEM, VMEM),
        scratch_shapes=[
            pltpu.VMEM((CHUNKS, 17, 48, 128), F32),
            pltpu.VMEM(pert.shape, BF16),
            pltpu.VMEM((640, 16, 128), F32),
            pltpu.VMEM((32, 32, 128), F32),
            pltpu.VMEM((GROUPS, 24, 128), F32),
            pltpu.VMEM((64, 128), jnp.int32),
            pltpu.VMEM((64, 128), jnp.int32),
            pltpu.VMEM((12, 64, 128), F32),
            pltpu.VMEM((128, 1536), F32),
        ] + MEM_SCRATCH + [DMA((2, CHUNKS))] * 4 + [DMA((GROUPS,))] * 2 + [DMA((CHUNKS + 2,))],
        compiler_params=pltpu.CompilerParams(vmem_limit_bytes=VMEM_LIMIT, collective_id=0, has_side_effects=True),
        name="forward",
    )(cnt, owner, col, lev, frac, inn, rinv, alpha, pert, bg, static, mix, sy, sx)


def backward_kernel(
    adj_ref, dep_ref, tgt_ref, alpha_ref, pert_hbm, bg_ref, static_ref, mix_ref, gy_ref, gx_ref,
    grad_ref, gstat_ref, depout_ref,
    full_ref, pert_ref, turn_ref, wide_ref, fromleft_ref, fromright_ref, fromabove_ref, frombelow_ref, ret_ref,
    half_ref, got_ref, far_ref, msend, mrecv,
    xsend, xrecv, ysend, yrecv, osend, orecv, own,
):
    place = Place()

    def y_copies(g):
        return (
            remote(wide_ref.at[g, :, 40:48], fromleft_ref.at[g], ysend.at[0, g], yrecv.at[0, g], place.right),
            remote(wide_ref.at[g, :, 0:8], fromright_ref.at[g], ysend.at[1, g], yrecv.at[1, g], place.left),
        )

    def x_copies(g):
        return (
            remote(wide_ref.at[g, 12:17, 8:40], fromabove_ref.at[g], xsend.at[0, g], xrecv.at[0, g], place.below),
            remote(wide_ref.at[g, 0:4, 8:40], frombelow_ref.at[g], xsend.at[1, g], xrecv.at[1, g], place.above),
        )

    pert_copy = pltpu.make_async_copy(pert_hbm, pert_ref, own.at[0])
    exchange = Exchange(place, dep_ref, ret_ref, osend, orecv, own.at[1])
    total = MemSum(place, adj_ref, full_ref, half_ref, got_ref, far_ref, msend, mrecv)

    place.greet()
    for b in range(BLOCKS):
        total.near(b).start()
    pert_copy.start()
    for b in range(BLOCKS):
        total.second(b)
    exchange.start()
    pert_copy.wait()

    def block(b):
        fine_adj = full_ref[8 * b:8 * b + 8]

        def member(k, carry):
            fine = fine_adj * pert_ref[k, 8 * b:8 * b + 8].astype(F32)
            hi, lo = split(fine.reshape(256, 128))
            turn_ref[pl.ds(k * 32 + 8 * b, 8)] = mm(gx_ref[...], jnp.concatenate([hi, lo], 0)).reshape(8, 16, 128)
            return carry

        lax.fori_loop(0, 20, member, 0, unroll=4)
        gstat_ref[8 * b:8 * b + 8] = static_ref[8 * b:8 * b + 8] + bg_ref[8 * b:8 * b + 8] * fine_adj

    for s in range(BLOCKS + 1):
        if s < BLOCKS:
            total.third(s, lambda at: 0.0)
        if s >= 1:
            total.last(s - 1)
            block(s - 1)

    def smooth(g, carry):
        rows = []
        for a in range(9):
            hi, lo = split(turn_ref[pl.ds(pl.multiple_of(g * 128, 128), 128), a, :])
            rows.append(mm(gy_ref[...], jnp.concatenate([hi, lo], 1), NT))
        field = three(jnp.concatenate(rows, 0), mix_ref[...]).reshape(9, 40, 128)
        field = jnp.concatenate([jnp.zeros((9, 8, 128), F32), field], 1)
        for step in range(4):
            two = jnp.zeros((2, 48, 128), F32)
            field = diffuse_rows(jnp.concatenate([two, field, two], 0))
        wide_ref[g] = field
        for copy in y_copies(g):
            copy.start()
        return carry

    def lengthways(g, carry):
        for copy in y_copies(g):
            copy.wait()
        wide_ref[g, :, 8:16] += fromleft_ref[g]
        wide_ref[g, :, 32:40] += fromright_ref[g]
        for copy in x_copies(g):
            copy.start()
        return carry

    def both(g, carry):
        smooth(g, carry)
        return lengthways(g - 1, carry)

    smooth(0, 0)
    lax.fori_loop(1, CHUNKS, both, 0)
    lengthways(CHUNKS - 1, 0)

    exchange.wait()
    unroute(tgt_ref, ret_ref[...].reshape(128, 128), depout_ref)
    for g in range(CHUNKS):
        for copy in x_copies(g):
            copy.wait()
        lanes = slice(128 * g, 128 * g + 128)
        grad_ref[:, :, lanes] = alpha_ref[:, :, lanes] + wide_ref[g, 4:12, 8:40]
        grad_ref[0:5, :, lanes] += fromabove_ref[g]
        grad_ref[4:8, :, lanes] += frombelow_ref[g]


def backward(adj, dep, tgt, alpha, pert, bg, static, mix, gy, gx):
    return pl.pallas_call(
        backward_kernel,
        out_shape=(
            jax.ShapeDtypeStruct(alpha.shape, F32),
            jax.ShapeDtypeStruct(static.shape, F32),
            jax.ShapeDtypeStruct(tgt.shape, F32),
        ),
        in_specs=[VMEM] * 4 + [ANY] + [VMEM] * 5,
        out_specs=(VMEM,) * 3,
        scratch_shapes=[
            pltpu.VMEM((32, 32, 128), F32),
            pltpu.VMEM(pert.shape, BF16),
            pltpu.VMEM((640, 16, 128), F32),
            pltpu.VMEM((CHUNKS, 17, 48, 128), F32),
            pltpu.VMEM((CHUNKS, 17, 8, 128), F32),
            pltpu.VMEM((CHUNKS, 17, 8, 128), F32),
            pltpu.VMEM((CHUNKS, 5, 32, 128), F32),
            pltpu.VMEM((CHUNKS, 4, 32, 128), F32),
            pltpu.VMEM((GROUPS, 4, 128), F32),
        ] + MEM_SCRATCH + [DMA((2, CHUNKS))] * 4 + [DMA((GROUPS,))] * 2 + [DMA((2,))],
        compiler_params=pltpu.CompilerParams(vmem_limit_bytes=VMEM_LIMIT, collective_id=1, has_side_effects=True),
        name="backward",
    )(adj, dep, tgt, alpha, pert, bg, static, mix, gy, gx)


def per_device(alpha, lv_sqrt, ens_pert, bg_sigma, static_ctrl, obs_owner, obs_column, obs_level, obs_frac, innovation, obs_rinv, obs_count):
    four = jnp.eye(4, dtype=F32)
    mix_forward, mix_backward = jnp.kron(four, lv_sqrt.T), jnp.kron(four, lv_sqrt)
    spread_y, gather_y, spread_x, gather_x = tables()
    shape = (64, 128)
    increment, incoming, target = forward(
        obs_count, obs_owner.reshape(shape), obs_column.reshape(shape), obs_level.reshape(shape), obs_frac,
        innovation.reshape(shape), obs_rinv.reshape(shape), alpha, ens_pert, bg_sigma, static_ctrl, mix_forward, spread_y, spread_x,
    )
    departure, adjoint = stencil(increment.reshape(1024, 128), incoming)
    grad_alpha, grad_static, departures = backward(
        adjoint.reshape(32, 32, 128), departure, target, alpha, ens_pert, bg_sigma, static_ctrl, mix_backward, gather_y, gather_x,
    )
    return grad_alpha, grad_static, departures.reshape(-1)


def solution(mesh):
    placed = (
        P("tx", "ty", "mem"),
        P(),
        P("mem", None, "tx", "ty"),
        P(None, "tx", "ty"),
        P(None, "tx", "ty"),
        P(("tx", "ty", "mem"), None),
        P(("tx", "ty", "mem")),
        P(("tx", "ty", "mem")),
        P(None, ("tx", "ty", "mem")),
        P(("tx", "ty", "mem")),
        P(("tx", "ty", "mem")),
        P(("tx", "ty", "mem")),
    )
    return jax.shard_map(
        per_device,
        mesh=mesh,
        in_specs=placed,
        out_specs=(P("tx", "ty", "mem"), P(None, "tx", "ty"), P(("tx", "ty", "mem"))),
        check_vma=False,
    )
```

time: 274 us -> 168 us (0.61)
  waiting for transfers between devices: 81.1 us -> 0 us
  Pallas kernels: 104 us -> 158 us
  blocking collectives: 28.1 us -> 0 us
  starting transfers between devices: 25 us -> 0 us
  between operations: 14.9 us -> 1.31 us
  other arithmetic: 8.82 us -> 0.86 us
  local copies, waits for them, and re-layouts: 11.8 us -> 7.57 us
    psum x2 -> x0, waiting for transfers between devices: 59.3 us -> none  [the longest x1 40.8 us: per_device(): adjoint = lax.psum(adjoint, 'mem').reshape(32, 32, 128)]
    pallas_call x4 -> x2, Pallas kernels: 42.1 us -> 96.2 us  [the longest x1 51.5 us: forward(): pl.pallas_call(forward_kernel, out_shape=(jax.ShapeDtypeStruct((32, 32, 1...]
    all_to_all x1 -> x0, blocking collectives: 28.1 us -> none  [per_device(): lax.all_to_all(departure, ('tx', 'ty'), split_axis=0, concat_axis=0, tile...]
    ppermute x8 -> x0, waiting for transfers between devices: 21.8 us -> none  [shifted(): lax.ppermute(value, axis, [(i, (i + by) % count) for i in range(count)])]
    ppermute x8 -> x0, starting transfers between devices: 16.1 us -> none  [shifted(): lax.ppermute(value, axis, [(i, (i + by) % count) for i in range(count)])]
    all_to_all x1 -> x0, starting transfers between devices: 8.63 us -> none  [per_device(): lax.all_to_all(outgoing, ('tx', 'ty'), split_axis=0, concat_axis=0, tiled...]
    slice x10 -> x0, local copies, waits for them, and re-layouts: 4.41 us -> none  [the longest x1 1.14 us: per_device(): above = shifted(back[12:], 'tx', 1)]
    concatenate x3 -> x0, other arithmetic: 3.86 us -> none  [the longest x1 2.56 us: per_device(): ext = jnp.concatenate([left, tall, right], 1)]
  transfers between devices with their start and end apart: 11 -> 0, of which waited for: 6 -> 0; matrix products, arithmetic and copies ran while one was open for 5% -> 0% of each run, Pallas kernels for 5% -> 0%
where the time goes in v2:
time: 168 us; the launch traced here: 167 us
  Pallas kernels  158 us (94%)
  local copies, waits for them, and re-layouts  7.57 us (5%)
    pallas_call x1, Pallas kernels, stencil(): pl.pallas_call(stencil_kernel, out_shape=(jax.ShapeDtypeStruct((32, 4, 12...  61.5 us
    pallas_call x1, Pallas kernels, forward(): pl.pallas_call(forward_kernel, out_shape=(jax.ShapeDtypeStruct((32, 32, 1...  51.5 us
    pallas_call x1, Pallas kernels, backward(): pl.pallas_call(backward_kernel, out_shape=(jax.ShapeDtypeStruct(alpha.sha...  44.7 us
    unnamed x3, local copies, waits for them, and re-layouts  5.21 us

profile of v2, /device:TPU:0, one launch (start us, length us, event | category | flops | bytes accessed | tf_op | source)
XLA Modules:
  0.0 167.4 jit_solution(15231629646524391411)
XLA Ops:
  1.3 0.8 copy.19
  2.1 0.9 broadcast_multiply_fusion
  2.9 0.8 mul.47.mix_ref
  3.7 0.8 mul.44.mix_ref
  4.5 51.5 %forward.1 = (f32[32,32,128]{2,1,0:T(8,128)}, f32[32,24,128]{2,1,0:T(8,128)}, s32[64,128]{1,0:T(8,128)}) custom-call(s32[1]{0:T(128)S(6)} %copy.23.cnt_ref, s32[64,128]{1,0:T(8,128)} %bitcast.12, s32[64,128]{1,0:T(8,128)} %bitcast.13, s32[64,128]{1,0:T(8,128)} %bitcast.14, f32[3,8192]{1,0:T(4,128)} %frac_ref.1, f32[64,128]{1,0:T(8,128)} %bitcast.15, ...), custom_call_target="tpu_custom_call" | custom-call | tf_op jit(solution)/shard_map/forward/pallas_call | solution.py:404
  56.0 61.5 %stencil.1 = (f32[32,4,128]{2,1,0:T(4,128)}, f32[1024,128]{1,0:T(8,128)}) custom-call(f32[1024,128]{1,0:T(8,128)} %bitcast.10, f32[32,24,128]{2,1,0:T(8,128)} %get-tuple-element.12.obs_ref), custom_call_target="tpu_custom_call" | custom-call | tf_op jit(solution)/shard_map/stencil/pallas_call | solution.py:77
  117.4 44.7 %backward.1 = (f32[8,32,640]{2,1,0:T(8,128)}, f32[32,32,128]{2,1,0:T(8,128)}, f32[64,128]{1,0:T(8,128)}) custom-call(f32[32,32,128]{2,1,0:T(8,128)} %bitcast.9, f32[32,4,128]{2,1,0:T(4,128)} %get-tuple-element.14.dep_ref, s32[64,128]{1,0:T(8,128)} %get-tuple-element.15.tgt_ref, f32[8,32,640]{2,1,0:T(8,128)} %alpha_ref.3, bf16[20,32,32,128]{3,2,1,0:T(8,128)(2,1)} %pert_hbm.3, ...), custom_call_target="tpu_custom_call" | custom-call | tf_op jit(solution)/shard_map/backward/pallas_call | solution.py:526
  162.1 2.0 %copy.24 = f32[8,32,640]{2,1,0:T(8,128)} copy(f32[8,32,640]{2,1,0:T(8,128)} %get-tuple-element.24) | data formatting | bytes 1310720
  164.1 1.9 %copy.25 = f32[32,32,128]{2,1,0:T(8,128)} copy(f32[32,32,128]{2,1,0:T(8,128)} %get-tuple-element.25) | data formatting | bytes 1048576
  166.0 1.4 copy.26
  (1 shorter events, 0.0 us)

commit v3 on v2

--- a/solution.py
+++ b/solution.py
@@ -34,60 +34,132 @@
     return jnp.maximum(1.0 - jnp.abs(position - iota((count, 128), 0).astype(F32)), 0.0)
 
 
-def stencil_kernel(inc_ref, obs_ref, dep_ref, adj_ref, table_ref, acc_ref, ahi_ref, alo_ref):
-    turned = inc_ref[...].T
-    hi, lo = split(turned)
-    table_ref[0:128] = hi
-    table_ref[128:256] = lo
+def chunk_order(obs_ref):
+    base = obs_ref[:, 20:24, :].astype(jnp.int32)
+    live = obs_ref[:, 16:20, :] > 0.0
+    level = base // 4096
+    first = jnp.min(jnp.where(live, level, 99), 2, keepdims=True).astype(F32)
+    last = jnp.max(jnp.where(live, level + 1, -1), 2, keepdims=True).astype(F32)
+    spread = lambda v: jnp.broadcast_to(v, (32, 4, 128)).reshape(128, 128)
+    first, last = spread(first), spread(last)
+    down, along = iota((128, 128), 0), iota((128, 128), 1)
+    key = first * 16384.0 + last * 128.0 + down.astype(F32)
+    other = key.T
+    rank = jnp.sum(jnp.where(other > key, 1.0, 0.0), 0, keepdims=True)
+    hit = along == jnp.broadcast_to(rank, (128, 128)).T.astype(jnp.int32)
+    pick = lambda v: jnp.sum(jnp.where(hit, v, 0.0), 0, keepdims=True)
+    live_count = jnp.sum(jnp.where(other < 99.0 * 16384.0, 1.0, 0.0), 1, keepdims=True)
+    count = jnp.broadcast_to(live_count, (128, 128))[0:1]
+    rows = [pick(down.astype(F32)), pick(first), pick(last), count]
+    return jnp.concatenate(rows + [jnp.zeros((4, 128), F32)], 0).astype(jnp.int32)
+
+
+def stencil_kernel(order_ref, table_ref, obs_ref, dep_ref, adj_ref, acc_ref, ahi_ref, alo_ref, in_l_ref, in_x_ref, in_y_ref, sum_ref, spread_ref):
     acc_ref[...] = jnp.zeros_like(acc_ref)
-
-    def one_source(s, carry):
-        cols = []
-        for q in range(4):
-            get = lambda ch: obs_ref[s, ch * 4 + q:ch * 4 + q + 1, :]
+    dep_ref[...] = jnp.zeros_like(dep_ref)
+
+    def blocks_of(n):
+        first = jnp.int32(99)
+        last = jnp.int32(-1)
+        for j in range(4):
+            first = jnp.minimum(first, order_ref[1, 4 * n + j])
+            last = jnp.maximum(last, order_ref[2, 4 * n + j])
+        return jnp.where(last < 0, 0, first // 8), jnp.where(last < 0, 0, last // 8 + 1)
+
+    def adjoint(slot, g):
+        acc_ref[g, 0:256] += mm(spread_ref[...], ahi_ref[slot, g], NT)
+        acc_ref[g, 256:384] += mm(spread_ref[0:128], alo_ref[slot, g], NT)
+
+    def one_group(n, before):
+        slot = lax.rem(n, 2)
+        old_from, old_to = before
+        new_from, new_to = blocks_of(n)
+        sources, parts = [], []
+        for j in range(4):
+            chunk = order_ref[0, 4 * n + j]
+            s, q = chunk // 4, lax.rem(chunk, 4)
+            sources.append(s)
+            parts.append(q)
+            get = lambda ch: obs_ref[s, pl.ds(ch * 4 + q, 1), :]
             base = get(5).astype(jnp.int32)
-            pos_l = (base // 4096).astype(F32) + get(2)
-            pos_x = ((base // 128) % 32).astype(F32) + get(0)
-            pos_y = (base % 128).astype(F32) + get(1)
-            in_l, in_x = tent(pos_l, 32), tent(pos_x, 32)
-            cols.append(tent(pos_y, 128))
-            for l in range(32):
-                hi, lo = split(in_l[l:l + 1] * in_x)
-                ahi_ref[l * 32:(l + 1) * 32, q * 128:(q + 1) * 128] = hi
-                alo_ref[l * 32:(l + 1) * 32, q * 128:(q + 1) * 128] = lo
-        both = mm(table_ref[...], ahi_ref[...])
-        picked = both[:128] + both[128:] + mm(table_ref[0:128], alo_ref[...])
-        shi, slo = [], []
-        for q in range(4):
-            dep = jnp.sum(picked[:, q * 128:(q + 1) * 128] * cols[q], 0, keepdims=True) - obs_ref[s, 12 + q:13 + q, :]
-            dep_ref[s, q:q + 1, :] = dep
-            hi, lo = split(cols[q] * (dep * obs_ref[s, 16 + q:17 + q, :]))
-            shi.append(hi)
-            slo.append(lo)
-        shi = jnp.concatenate(shi, 1)
-        slo = jnp.concatenate(slo, 1)
-        acc_ref[...] += mm(ahi_ref[...], shi, NT) + mm(ahi_ref[...], slo, NT) + mm(alo_ref[...], shi, NT)
+            at = slice(128 * j, 128 * j + 128)
+            in_l_ref[:, at] = tent((base // 4096).astype(F32) + get(2), 32)
+            in_x_ref[:, at] = tent(((base // 128) % 32).astype(F32) + get(0), 32)
+            in_y_ref[:, at] = tent((base % 128).astype(F32) + get(1), 128)
+        sum_ref[...] = jnp.zeros_like(sum_ref)
+
+        def gather(g):
+            in_l = in_l_ref[pl.ds(pl.multiple_of(8 * g, 8), 8), :]
+            for l in range(8):
+                hi, lo = split(in_l[l:l + 1] * in_x_ref[...])
+                ahi_ref[slot, g, 32 * l:32 * l + 32] = hi
+                alo_ref[slot, g, 32 * l:32 * l + 32] = lo
+            both = mm(table_ref[g], ahi_ref[slot, g])
+            sum_ref[...] += both[:128] + both[128:] + mm(table_ref[g, 0:128], alo_ref[slot, g])
+
+        shared_from = jnp.maximum(old_from, new_from)
+        shared_to = jnp.maximum(jnp.minimum(old_to, new_to), shared_from)
+
+        def together(g, carry):
+            adjoint(1 - slot, g)
+            gather(g)
+            return carry
+
+        def only_old(g, carry):
+            adjoint(1 - slot, g)
+            return carry
+
+        def only_new(g, carry):
+            gather(g)
+            return carry
+
+        lax.fori_loop(old_from, jnp.minimum(old_to, shared_from), only_old, 0)
+        lax.fori_loop(shared_to, old_to, only_old, 0)
+        lax.fori_loop(shared_from, shared_to, together, 0)
+        lax.fori_loop(new_from, jnp.minimum(new_to, shared_from), only_new, 0)
+        lax.fori_loop(shared_to, new_to, only_new, 0)
+
+        for j in range(4):
+            at = slice(128 * j, 128 * j + 128)
+            get = lambda ch: obs_ref[sources[j], pl.ds(ch * 4 + parts[j], 1), :]
+            dep = jnp.sum(sum_ref[:, at] * in_y_ref[:, at], 0, keepdims=True) - get(3)
+            dep_ref[sources[j], pl.ds(parts[j], 1), :] = dep
+            hi, lo = split(in_y_ref[:, at] * (dep * get(4)))
+            spread_ref[0:128, at] = hi
+            spread_ref[128:256, at] = lo
+        return new_from, new_to
+
+    groups = (order_ref[3, 0] + 3) // 4
+    old_from, old_to = lax.fori_loop(0, groups, one_group, (jnp.int32(0), jnp.int32(0)))
+
+    def finish(g, carry):
+        adjoint(lax.rem(groups + 1, 2), g)
         return carry
 
-    lax.fori_loop(0, obs_ref.shape[0], one_source, 0)
-    adj_ref[...] = acc_ref[...]
-
-
-def stencil(inc, obs):
+    lax.fori_loop(old_from, old_to, finish, 0)
+    for g in range(4):
+        adj_ref[256 * g:256 * g + 256] = (acc_ref[g, 0:128] + acc_ref[g, 128:256] + acc_ref[g, 256:384]).T
+
+
+def stencil(order, table, obs):
     return pl.pallas_call(
         stencil_kernel,
         out_shape=(jax.ShapeDtypeStruct((32, 4, 128), F32), jax.ShapeDtypeStruct((1024, 128), F32)),
-        in_specs=[pl.BlockSpec(memory_space=pltpu.VMEM)] * 2,
+        in_specs=[pl.BlockSpec(memory_space=pltpu.SMEM)] + [pl.BlockSpec(memory_space=pltpu.VMEM)] * 2,
         out_specs=(pl.BlockSpec(memory_space=pltpu.VMEM),) * 2,
         scratch_shapes=[
-            pltpu.VMEM((256, 1024), BF16),
-            pltpu.VMEM((1024, 128), F32),
-            pltpu.VMEM((1024, 512), BF16),
-            pltpu.VMEM((1024, 512), BF16),
+            pltpu.VMEM((4, 384, 256), F32),
+            pltpu.VMEM((2, 4, 256, 512), BF16),
+            pltpu.VMEM((2, 4, 256, 512), BF16),
+            pltpu.VMEM((32, 512), F32),
+            pltpu.VMEM((32, 512), F32),
+            pltpu.VMEM((128, 512), F32),
+            pltpu.VMEM((128, 512), F32),
+            pltpu.VMEM((256, 512), BF16),
         ],
         compiler_params=pltpu.CompilerParams(vmem_limit_bytes=VMEM_LIMIT),
         name="stencil",
-    )(inc, obs)
+    )(order, table, obs)
 
 
 def line_weights(fine, coarse):
@@ -228,17 +300,29 @@
     place = iota((rows, wide), 0) * wide + iota((rows, wide), 1)
     live = place < cnt_ref[0]
     owner = jnp.where(live, owner_ref[...], GROUPS)
-    same = iota((rows, GROUPS, wide), 1) == owner[:, None, :]
-    onehot = jnp.where(same, 1.0, 0.0).astype(BF16).reshape(rows * GROUPS, wide)
-    lower = iota((wide, 2 * wide), 0) < iota((wide, 2 * wide), 1)
-    both = mm(onehot, jnp.where(lower, 1.0, 0.0).astype(BF16))
-    inside, totals = both[:, :wide].reshape(rows, GROUPS, wide), both[:, wide:].reshape(rows, GROUPS, wide)
-    running = jnp.zeros((GROUPS, wide), F32)
+    level = lev_ref[...]
+    key = (owner * 32 + level).astype(F32)
+    turned = jnp.concatenate([key, key], 0).T
+    earlier = iota((wide, wide), 0) < iota((wide, wide), 1)
+    one_if = lambda cond: jnp.where(cond, 1.0, 0.0).astype(BF16)
+    owners = [one_if(iota((GROUPS, wide), 0) == owner[c:c + 1]) for c in range(rows)]
+    levels = [one_if(iota((32, wide), 0) == level[c:c + 1]) for c in range(rows)]
+    running = jnp.zeros((GROUPS, 32), F32)
+    starts = []
+    for c in range(rows):
+        starts.append(running)
+        running = running + mm(owners[c], levels[c], NT)
+    lower = one_if(iota((32, 32), 0) < iota((32, 32), 1))
+    hi, lo = split(running)
+    offset = mm(hi, lower) + mm(lo, lower)
     ranks = []
     for c in range(rows):
-        ranks.append(jnp.sum(jnp.where(same[c], inside[c] + running, 0.0), 0, keepdims=True))
-        running = running + totals[c]
-    rank = jnp.concatenate(ranks, 0).astype(jnp.int32)
+        hi, lo = split(offset + starts[c])
+        both = mm(jnp.concatenate([hi, lo], 0), levels[c])
+        same = jnp.where((turned[:, c:c + 1] == key[c:c + 1]) & earlier, 1.0, 0.0)
+        at = (both[:GROUPS] + both[GROUPS:]) * owners[c].astype(F32)
+        ranks.append(jnp.sum(at, 0, keepdims=True) + jnp.sum(same, 0, keepdims=True))
+    rank = jnp.where(live, jnp.concatenate(ranks, 0).astype(jnp.int32), 0)
     tgt_ref[...] = jnp.where(live, owner * 512 + rank, -1)
     high_ref[...] = jnp.where(live, rank // 128 * GROUPS + owner, -1)
     low_ref[...] = rank % 128
@@ -296,6 +380,11 @@
     return mid + NU * (near - 4.0 * mid)
 
 
+def mixing(lv):
+    tiled = jnp.concatenate([jnp.concatenate([lv] * 4, 1)] * 4, 0)
+    return jnp.where(iota((128, 128), 0) // 32 == iota((128, 128), 1) // 32, tiled, 0.0)
+
+
 def three(a, b):
     hi, lo = split(a)
     bhi, blo = split(b)
@@ -303,9 +392,9 @@
 
 
 def forward_kernel(
-    cnt_ref, owner_ref, col_ref, lev_ref, frac_ref, inn_ref, rinv_ref, alpha_ref, pert_hbm, bg_ref, static_ref, mix_ref, sy_ref, sx_ref,
-    inc_ref, obs_ref, tgt_ref,
-    ext_ref, pert_ref, turn_ref, part_ref, out_ref, high_ref, low_ref, term_ref, acc_ref,
+    cnt_ref, owner_ref, col_ref, lev_ref, frac_ref, inn_ref, rinv_ref, alpha_ref, pert_hbm, bg_ref, static_ref, lv_ref, sy_ref, sx_ref,
+    table_ref, obs_ref, order_ref, tgt_ref,
+    inc_ref, ext_ref, pert_ref, turn_ref, part_ref, out_ref, high_ref, low_ref, term_ref, acc_ref,
     half_ref, got_ref, far_ref, msend, mrecv,
     xsend, xrecv, ysend, yrecv, osend, orecv, own,
 ):
@@ -346,30 +435,35 @@
     route_ranks(cnt_ref, owner_ref, col_ref, lev_ref, frac_ref, inn_ref, rinv_ref, tgt_ref, high_ref, low_ref, term_ref)
     route_slots(high_ref, low_ref, term_ref, acc_ref, out_ref)
 
-    def sideways(g, carry):
+    exchange.start()
+    mix = mixing(lv_ref[...]).T
+
+    def sideways(g):
         for copy in x_copies(g):
             copy.wait()
         own_copy(g).wait()
         for copy in y_copies(g):
             copy.start()
-        return carry
-
-    lax.fori_loop(0, CHUNKS, sideways, 0)
-    exchange.start()
-
-    def smooth(g, carry):
+
+    def smooth(g):
         for copy in y_copies(g):
             copy.wait()
         field = ext_ref[g]
         for step in range(4):
             field = diffuse_rows(field)
-        field = three(field[:, 8:48].reshape(9 * 40, 128), mix_ref[...]).reshape(9, 40, 128)
+        field = three(field[:, 8:48].reshape(9 * 40, 128), mix).reshape(9, 40, 128)
         for a in range(9):
             hi, lo = split(field[a])
             turn_ref[pl.ds(pl.multiple_of(g * 128, 128), 128), a, :] = mm(jnp.concatenate([hi, lo], 0), sy_ref[...], TN)
+
+    def both(g, carry):
+        sideways(g)
+        smooth(g - 1)
         return carry
 
-    lax.fori_loop(0, CHUNKS, smooth, 0)
+    sideways(0)
+    lax.fori_loop(1, CHUNKS, both, 0)
+    smooth(CHUNKS - 1)
     pert_copy.wait()
 
     def block(b):
@@ -387,11 +481,17 @@
             total.near(s).start()
         if 0 <= s - 1 < BLOCKS:
             total.second(s - 1)
+        if s == BLOCKS:
+            exchange.wait()
+            order_ref[...] = chunk_order(obs_ref)
         if 0 <= s - 2 < BLOCKS:
             total.third(s - 2, extra)
         if 0 <= s - 3 < BLOCKS:
-            total.last(s - 3)
-    exchange.wait()
+            b = s - 3
+            total.last(b)
+            hi, lo = split(inc_ref[8 * b:8 * b + 8].reshape(256, 128).T)
+            table_ref[b, 0:128] = hi
+            table_ref[b, 128:256] = lo
 
 
 VMEM = pl.BlockSpec(memory_space=pltpu.VMEM)
@@ -400,17 +500,19 @@
 DMA = pltpu.SemaphoreType.DMA
 
 
-def forward(cnt, owner, col, lev, frac, inn, rinv, alpha, pert, bg, static, mix, sy, sx):
+def forward(cnt, owner, col, lev, frac, inn, rinv, alpha, pert, bg, static, lv, sy, sx):
     return pl.pallas_call(
         forward_kernel,
         out_shape=(
-            jax.ShapeDtypeStruct((32, 32, 128), F32),
+            jax.ShapeDtypeStruct((BLOCKS, 256, 256), BF16),
             jax.ShapeDtypeStruct((GROUPS, 24, 128), F32),
+            jax.ShapeDtypeStruct((8, 128), jnp.int32),
             jax.ShapeDtypeStruct((64, 128), jnp.int32),
         ),
         in_specs=[SMEM] + [VMEM] * 6 + [ANY] * 2 + [VMEM] * 5,
-        out_specs=(VMEM, VMEM, VMEM),
+        out_specs=(VMEM,) * 4,
         scratch_shapes=[
+            pltpu.VMEM((32, 32, 128), F32),
             pltpu.VMEM((CHUNKS, 17, 48, 128), F32),
             pltpu.VMEM(pert.shape, BF16),
             pltpu.VMEM((640, 16, 128), F32),
@@ -423,13 +525,13 @@
         ] + MEM_SCRATCH + [DMA((2, CHUNKS))] * 4 + [DMA((GROUPS,))] * 2 + [DMA((CHUNKS + 2,))],
         compiler_params=pltpu.CompilerParams(vmem_limit_bytes=VMEM_LIMIT, collective_id=0, has_side_effects=True),
         name="forward",
-    )(cnt, owner, col, lev, frac, inn, rinv, alpha, pert, bg, static, mix, sy, sx)
+    )(cnt, owner, col, lev, frac, inn, rinv, alpha, pert, bg, static, lv, sy, sx)
 
 
 def backward_kernel(
-    adj_ref, dep_ref, tgt_ref, alpha_ref, pert_hbm, bg_ref, static_ref, mix_ref, gy_ref, gx_ref,
-    grad_ref, gstat_ref, depout_ref,
-    full_ref, pert_ref, turn_ref, wide_ref, fromleft_ref, fromright_ref, fromabove_ref, frombelow_ref, ret_ref,
+    adj_ref, dep_ref, tgt_ref, pert_hbm, lv_ref, gy_ref, gx_ref,
+    grad_ref, full_ref, depout_ref,
+    pert_ref, turn_ref, wide_ref, fromleft_ref, fromright_ref, fromabove_ref, frombelow_ref, ret_ref,
     half_ref, got_ref, far_ref, msend, mrecv,
     xsend, xrecv, ysend, yrecv, osend, orecv, own,
 ):
@@ -470,7 +572,6 @@
             return carry
 
         lax.fori_loop(0, 20, member, 0, unroll=4)
-        gstat_ref[8 * b:8 * b + 8] = static_ref[8 * b:8 * b + 8] + bg_ref[8 * b:8 * b + 8] * fine_adj
 
     for s in range(BLOCKS + 1):
         if s < BLOCKS:
@@ -479,12 +580,14 @@
             total.last(s - 1)
             block(s - 1)
 
+    mix = mixing(lv_ref[...])
+
     def smooth(g, carry):
         rows = []
         for a in range(9):
             hi, lo = split(turn_ref[pl.ds(pl.multiple_of(g * 128, 128), 128), a, :])
             rows.append(mm(gy_ref[...], jnp.concatenate([hi, lo], 1), NT))
-        field = three(jnp.concatenate(rows, 0), mix_ref[...]).reshape(9, 40, 128)
+        field = three(jnp.concatenate(rows, 0), mix).reshape(9, 40, 128)
         field = jnp.concatenate([jnp.zeros((9, 8, 128), F32), field], 1)
         for step in range(4):
             two = jnp.zeros((2, 48, 128), F32)
@@ -517,23 +620,22 @@
         for copy in x_copies(g):
             copy.wait()
         lanes = slice(128 * g, 128 * g + 128)
-        grad_ref[:, :, lanes] = alpha_ref[:, :, lanes] + wide_ref[g, 4:12, 8:40]
+        grad_ref[:, :, lanes] = wide_ref[g, 4:12, 8:40]
         grad_ref[0:5, :, lanes] += fromabove_ref[g]
         grad_ref[4:8, :, lanes] += frombelow_ref[g]
 
 
-def backward(adj, dep, tgt, alpha, pert, bg, static, mix, gy, gx):
+def backward(adj, dep, tgt, pert, lv, gy, gx):
     return pl.pallas_call(
         backward_kernel,
         out_shape=(
-            jax.ShapeDtypeStruct(alpha.shape, F32),
-            jax.ShapeDtypeStruct(static.shape, F32),
+            jax.ShapeDtypeStruct((8, 32, 640), F32),
+            jax.ShapeDtypeStruct((32, 32, 128), F32),
             jax.ShapeDtypeStruct(tgt.shape, F32),
         ),
-        in_specs=[VMEM] * 4 + [ANY] + [VMEM] * 5,
+        in_specs=[VMEM] * 3 + [ANY] + [VMEM] * 3,
         out_specs=(VMEM,) * 3,
         scratch_shapes=[
-            pltpu.VMEM((32, 32, 128), F32),
             pltpu.VMEM(pert.shape, BF16),
             pltpu.VMEM((640, 16, 128), F32),
             pltpu.VMEM((CHUNKS, 17, 48, 128), F32),
@@ -545,22 +647,36 @@
         ] + MEM_SCRATCH + [DMA((2, CHUNKS))] * 4 + [DMA((GROUPS,))] * 2 + [DMA((2,))],
         compiler_params=pltpu.CompilerParams(vmem_limit_bytes=VMEM_LIMIT, collective_id=1, has_side_effects=True),
         name="backward",
-    )(adj, dep, tgt, alpha, pert, bg, static, mix, gy, gx)
+    )(adj, dep, tgt, pert, lv, gy, gx)
+
+
+def finish_kernel(alpha_ref, back_ref, bg_ref, static_ref, adj_ref, dep_ref, grad_ref, gstat_ref, out_ref):
+    grad_ref[...] = alpha_ref[...] + back_ref[...]
+    gstat_ref[...] = static_ref[...] + bg_ref[...] * adj_ref[...]
+    out_ref[...] = dep_ref[...]
+
+
+def finish(alpha, back, bg, static, adj, dep):
+    return pl.pallas_call(
+        finish_kernel,
+        out_shape=tuple(jax.ShapeDtypeStruct(a.shape, F32) for a in (alpha, static, dep)),
+        in_specs=[VMEM] * 6,
+        out_specs=(VMEM,) * 3,
+        compiler_params=pltpu.CompilerParams(vmem_limit_bytes=VMEM_LIMIT),
+        name="finish",
+    )(alpha, back, bg, static, adj, dep)
 
 
 def per_device(alpha, lv_sqrt, ens_pert, bg_sigma, static_ctrl, obs_owner, obs_column, obs_level, obs_frac, innovation, obs_rinv, obs_count):
-    four = jnp.eye(4, dtype=F32)
-    mix_forward, mix_backward = jnp.kron(four, lv_sqrt.T), jnp.kron(four, lv_sqrt)
     spread_y, gather_y, spread_x, gather_x = tables()
     shape = (64, 128)
-    increment, incoming, target = forward(
+    table, incoming, order, target = forward(
         obs_count, obs_owner.reshape(shape), obs_column.reshape(shape), obs_level.reshape(shape), obs_frac,
-        innovation.reshape(shape), obs_rinv.reshape(shape), alpha, ens_pert, bg_sigma, static_ctrl, mix_forward, spread_y, spread_x,
+        innovation.reshape(shape), obs_rinv.reshape(shape), alpha, ens_pert, bg_sigma, static_ctrl, lv_sqrt, spread_y, spread_x,
     )
-    departure, adjoint = stencil(increment.reshape(1024, 128), incoming)
-    grad_alpha, grad_static, departures = backward(
-        adjoint.reshape(32, 32, 128), departure, target, alpha, ens_pert, bg_sigma, static_ctrl, mix_backward, gather_y, gather_x,
-    )
+    departure, adjoint = stencil(order, table, incoming)
+    back, adjoint, departures = backward(adjoint.reshape(32, 32, 128), departure, target, ens_pert, lv_sqrt, gather_y, gather_x)
+    grad_alpha, grad_static, departures = finish(alpha, back, bg_sigma, static_ctrl, adjoint, departures)
     return grad_alpha, grad_static, departures.reshape(-1)
 
 

time: 168 us -> 140 us (0.83)
  Pallas kernels: 158 us -> 138 us
  local copies, waits for them, and re-layouts: 7.57 us -> 0 us
    pallas_call x1, Pallas kernels: 61.5 us -> 35 us  [stencil(): pl.pallas_call(stencil_kernel, out_shape=(jax.ShapeDtypeStruct((32, 4, 12...]
    pallas_call x2 -> x3, Pallas kernels: 96.2 us -> 103 us  [the longest x1 58.4 us: forward(): pl.pallas_call(forward_kernel, out_shape=(jax.ShapeDtypeStruct((BLOCKS, 2...]
    unnamed x3 -> x0, local copies, waits for them, and re-layouts: 5.21 us -> none
where the time goes in v3:
time: 140 us
  Pallas kernels  138 us (99%)
    pallas_call x1, Pallas kernels, forward(): pl.pallas_call(forward_kernel, out_shape=(jax.ShapeDtypeStruct((BLOCKS, 2...  58.4 us
    pallas_call x1, Pallas kernels, backward(): pl.pallas_call(backward_kernel, out_shape=(jax.ShapeDtypeStruct((8, 32, 6...  42.2 us
    pallas_call x1, Pallas kernels, stencil(): pl.pallas_call(stencil_kernel, out_shape=(jax.ShapeDtypeStruct((32, 4, 12...  35 us
    pallas_call x1, Pallas kernels, finish(): pl.pallas_call(finish_kernel, out_shape=tuple((jax.ShapeDtypeStruct(a.sha...  2.84 us

profile of v3, /device:TPU:0, one launch (start us, length us, event | category | flops | bytes accessed | tf_op | source)
XLA Modules:
  0.0 139.7 jit_solution(1590579711477075258)
XLA Ops:
  1.3 58.4 %forward.1 = (bf16[4,256,256]{2,1,0:T(8,128)(2,1)}, f32[32,24,128]{2,1,0:T(8,128)}, s32[8,128]{1,0:T(8,128)}, s32[64,128]{1,0:T(8,128)}) custom-call(s32[1]{0:T(128)S(6)} %copy.19.cnt_ref, s32[64,128]{1,0:T(8,128)} %bitcast.8, s32[64,128]{1,0:T(8,128)} %bitcast.9, s32[64,128]{1,0:T(8,128)} %bitcast.10, f32[3,8192]{1,0:T(4,128)} %frac_ref.1, ...), custom_call_target="tpu_custom_call" | custom-call | tf_op jit(solution)/shard_map/forward/pallas_call | solution.py:504
  59.7 35.0 %stencil.1 = (f32[32,4,128]{2,1,0:T(4,128)}, f32[1024,128]{1,0:T(8,128)}) custom-call(s32[8,128]{1,0:T(8,128)} %get-tuple-element.15.order_ref, bf16[4,256,256]{2,1,0:T(8,128)(2,1)} %get-tuple-element.16.table_ref, f32[32,24,128]{2,1,0:T(8,128)} %get-tuple-element.17.obs_ref), custom_call_target="tpu_custom_call" | custom-call | tf_op jit(solution)/shard_map/stencil/pallas_call | solution.py:145
  94.7 42.2 %backward.1 = (f32[8,32,640]{2,1,0:T(8,128)}, f32[32,32,128]{2,1,0:T(8,128)}, f32[64,128]{1,0:T(8,128)}) custom-call(f32[32,32,128]{2,1,0:T(8,128)} %bitcast.7, f32[32,4,128]{2,1,0:T(4,128)} %get-tuple-element.19.dep_ref, s32[64,128]{1,0:T(8,128)} %get-tuple-element.20.tgt_ref, bf16[20,32,32,128]{3,2,1,0:T(8,128)(2,1)} %pert_hbm.3, f32[32,32]{1,0:T(8,128)} %lv_ref.3, ...), custom_call_target="tpu_custom_call" | custom-call | tf_op jit(solution)/shard_map/backward/pallas_call | solution.py:629
  136.9 2.8 %finish.1 = (f32[8,32,640]{2,1,0:T(8,128)}, f32[32,32,128]{2,1,0:T(8,128)}, f32[64,128]{1,0:T(8,128)}) custom-call(f32[8,32,640]{2,1,0:T(8,128)} %alpha_ref.3, f32[8,32,640]{2,1,0:T(8,128)} %get-tuple-element.21.back_ref, f32[32,32,128]{2,1,0:T(8,128)} %bg_ref.3, f32[32,32,128]{2,1,0:T(8,128)} %static_ref.3, f32[32,32,128]{2,1,0:T(8,128)} %get-tuple-element.22.adj_ref, ...), custom_call_target="tpu_custom_call" | custom-call | tf_op jit(solution)/shard_map/finish/pallas_call | solution.py:660

commit v4 on v3

--- a/solution.py
+++ b/solution.py
@@ -48,76 +48,88 @@
     rank = jnp.sum(jnp.where(other > key, 1.0, 0.0), 0, keepdims=True)
     hit = along == jnp.broadcast_to(rank, (128, 128)).T.astype(jnp.int32)
     pick = lambda v: jnp.sum(jnp.where(hit, v, 0.0), 0, keepdims=True)
-    live_count = jnp.sum(jnp.where(other < 99.0 * 16384.0, 1.0, 0.0), 1, keepdims=True)
+    live_count = jnp.sum(jnp.where(other < 98.0 * 16384.0, 1.0, 0.0), 1, keepdims=True)
     count = jnp.broadcast_to(live_count, (128, 128))[0:1]
     rows = [pick(down.astype(F32)), pick(first), pick(last), count]
     return jnp.concatenate(rows + [jnp.zeros((4, 128), F32)], 0).astype(jnp.int32)
 
 
-def stencil_kernel(order_ref, table_ref, obs_ref, dep_ref, adj_ref, acc_ref, ahi_ref, alo_ref, in_l_ref, in_x_ref, in_y_ref, sum_ref, spread_ref):
+def stencil_kernel(order_ref, table_ref, obs_ref, dep_ref, adj_ref, acc_ref, ahi0, alo0, ahi1, alo1, place_ref, in_x_ref, in_y_ref, sum_ref, spread_ref, where_ref):
+    slots = ((ahi0, alo0), (ahi1, alo1))
     acc_ref[...] = jnp.zeros_like(acc_ref)
     dep_ref[...] = jnp.zeros_like(dep_ref)
-
-    def blocks_of(n):
-        first = jnp.int32(99)
-        last = jnp.int32(-1)
-        for j in range(4):
-            first = jnp.minimum(first, order_ref[1, 4 * n + j])
-            last = jnp.maximum(last, order_ref[2, 4 * n + j])
-        return jnp.where(last < 0, 0, first // 8), jnp.where(last < 0, 0, last // 8 + 1)
-
-    def adjoint(slot, g):
-        acc_ref[g, 0:256] += mm(spread_ref[...], ahi_ref[slot, g], NT)
-        acc_ref[g, 256:384] += mm(spread_ref[0:128], alo_ref[slot, g], NT)
-
-    def one_group(n, before):
-        slot = lax.rem(n, 2)
-        old_from, old_to = before
-        new_from, new_to = blocks_of(n)
+    ahi1[0:512] = jnp.zeros((512, 512), BF16)
+    alo1[0:512] = jnp.zeros((512, 512), BF16)
+    base = obs_ref[:, 20:24, :].astype(jnp.int32)
+    where_ref[:, 0:4] = (base >> 12).astype(F32) + obs_ref[:, 8:12, :]
+    where_ref[:, 4:8] = ((base >> 7) & 31).astype(F32) + obs_ref[:, 0:4, :]
+    where_ref[:, 8:12] = (base & 127).astype(F32) + obs_ref[:, 4:8, :]
+    spread_ref[...] = jnp.zeros_like(spread_ref)
+    groups = (order_ref[3, 0] + 3) // 4
+
+    def lanes(start, step, wide):
+        return pl.ds(pl.multiple_of((start + step) * 128, 128), wide)
+
+    def adjoint(slot, at, rows):
+        acc_ref[0:256, at] += mm(spread_ref[...], slots[slot][0][rows], NT)
+        acc_ref[256:384, at] += mm(spread_ref[0:128], slots[slot][1][rows], NT)
+
+    def more(start, rest, what):
+        def one(g, carry):
+            what(lanes(start, 4 + 2 * g, 256), pl.ds(pl.multiple_of(512 + 256 * g, 256), 256), 16 + 8 * g)
+            return carry
+
+        lax.fori_loop(0, rest, one, 0)
+
+    def one_group(n, slot, before):
+        ahi_ref, alo_ref = slots[slot]
+        old_start, old_rest = before
+        first_of = jnp.minimum(4 * n, 124)
+        first = order_ref[1, first_of]
+        last = order_ref[2, first_of]
+        for j in range(1, 4):
+            first = jnp.minimum(first, order_ref[1, first_of + j])
+            last = jnp.maximum(last, order_ref[2, first_of + j])
+        start = jnp.minimum(first // 4, 4)
+        rest = jnp.maximum(last - 4 * start - 16 + 8, 0) // 8
+        rest = jnp.where(n < groups, rest, 0)
+
+        adjoint(1 - slot, lanes(old_start, 0, 512), slice(0, 512))
         sources, parts = [], []
         for j in range(4):
-            chunk = order_ref[0, 4 * n + j]
+            chunk = order_ref[0, first_of + j]
             s, q = chunk // 4, lax.rem(chunk, 4)
             sources.append(s)
             parts.append(q)
-            get = lambda ch: obs_ref[s, pl.ds(ch * 4 + q, 1), :]
-            base = get(5).astype(jnp.int32)
+            get = lambda ch: where_ref[s, pl.ds(ch * 4 + q, 1), :]
             at = slice(128 * j, 128 * j + 128)
-            in_l_ref[:, at] = tent((base // 4096).astype(F32) + get(2), 32)
-            in_x_ref[:, at] = tent(((base // 128) % 32).astype(F32) + get(0), 32)
-            in_y_ref[:, at] = tent((base % 128).astype(F32) + get(1), 128)
-        sum_ref[...] = jnp.zeros_like(sum_ref)
-
-        def gather(g):
-            in_l = in_l_ref[pl.ds(pl.multiple_of(8 * g, 8), 8), :]
+            place_ref[:, at] = jnp.broadcast_to(get(0) - (4 * start).astype(F32), (8, 128))
+            in_x_ref[:, at] = tent(get(1), 32)
+            in_y_ref[:, at] = tent(get(2), 128)
+
+        def build(row, level):
+            far = place_ref[...] - (iota((8, 512), 0) + level).astype(F32)
+            in_l = jnp.maximum(1.0 - jnp.abs(far), 0.0)
             for l in range(8):
                 hi, lo = split(in_l[l:l + 1] * in_x_ref[...])
-                ahi_ref[slot, g, 32 * l:32 * l + 32] = hi
-                alo_ref[slot, g, 32 * l:32 * l + 32] = lo
-            both = mm(table_ref[g], ahi_ref[slot, g])
-            sum_ref[...] += both[:128] + both[128:] + mm(table_ref[g, 0:128], alo_ref[slot, g])
-
-        shared_from = jnp.maximum(old_from, new_from)
-        shared_to = jnp.maximum(jnp.minimum(old_to, new_to), shared_from)
-
-        def together(g, carry):
-            adjoint(1 - slot, g)
-            gather(g)
-            return carry
-
-        def only_old(g, carry):
-            adjoint(1 - slot, g)
-            return carry
-
-        def only_new(g, carry):
-            gather(g)
-            return carry
-
-        lax.fori_loop(old_from, jnp.minimum(old_to, shared_from), only_old, 0)
-        lax.fori_loop(shared_to, old_to, only_old, 0)
-        lax.fori_loop(shared_from, shared_to, together, 0)
-        lax.fori_loop(new_from, jnp.minimum(new_to, shared_from), only_new, 0)
-        lax.fori_loop(shared_to, new_to, only_new, 0)
+                at = pl.ds(row + 32 * l, 32)
+                ahi_ref[at] = hi
+                alo_ref[at] = lo
+
+        build(0, 0)
+        build(256, 8)
+        table = table_ref[:, lanes(start, 0, 512)]
+        both = mm(table, ahi_ref[0:512])
+        sum_ref[...] = both[:128] + both[128:] + mm(table[:128], alo_ref[0:512])
+
+        def gather(at, rows, level):
+            build(pl.multiple_of(32 * level, 256), level)
+            table = table_ref[:, at]
+            both = mm(table, ahi_ref[rows])
+            sum_ref[...] += both[:128] + both[128:] + mm(table[:128], alo_ref[rows])
+
+        more(old_start, old_rest, lambda at, rows, level: adjoint(1 - slot, at, rows))
+        more(start, rest, gather)
 
         for j in range(4):
             at = slice(128 * j, 128 * j + 128)
@@ -127,18 +139,15 @@
             hi, lo = split(in_y_ref[:, at] * (dep * get(4)))
             spread_ref[0:128, at] = hi
             spread_ref[128:256, at] = lo
-        return new_from, new_to
-
-    groups = (order_ref[3, 0] + 3) // 4
-    old_from, old_to = lax.fori_loop(0, groups, one_group, (jnp.int32(0), jnp.int32(0)))
-
-    def finish(g, carry):
-        adjoint(lax.rem(groups + 1, 2), g)
-        return carry
-
-    lax.fori_loop(old_from, old_to, finish, 0)
-    for g in range(4):
-        adj_ref[256 * g:256 * g + 256] = (acc_ref[g, 0:128] + acc_ref[g, 128:256] + acc_ref[g, 256:384]).T
+        return start, rest
+
+    def two_groups(i, before):
+        return one_group(2 * i + 1, 1, one_group(2 * i, 0, before))
+
+    start, rest = lax.fori_loop(0, (groups + 1) // 2, two_groups, (jnp.int32(0), jnp.int32(0)))
+    adjoint(1, lanes(start, 0, 512), slice(0, 512))
+    more(start, rest, lambda at, rows, level: adjoint(1, at, rows))
+    adj_ref[...] = (acc_ref[0:128, 0:1024] + acc_ref[128:256, 0:1024] + acc_ref[256:384, 0:1024]).T
 
 
 def stencil(order, table, obs):
@@ -148,14 +157,17 @@
         in_specs=[pl.BlockSpec(memory_space=pltpu.SMEM)] + [pl.BlockSpec(memory_space=pltpu.VMEM)] * 2,
         out_specs=(pl.BlockSpec(memory_space=pltpu.VMEM),) * 2,
         scratch_shapes=[
-            pltpu.VMEM((4, 384, 256), F32),
-            pltpu.VMEM((2, 4, 256, 512), BF16),
-            pltpu.VMEM((2, 4, 256, 512), BF16),
-            pltpu.VMEM((32, 512), F32),
+            pltpu.VMEM((384, 1280), F32),
+            pltpu.VMEM((1280, 512), BF16),
+            pltpu.VMEM((1280, 512), BF16),
+            pltpu.VMEM((1280, 512), BF16),
+            pltpu.VMEM((1280, 512), BF16),
+            pltpu.VMEM((8, 512), F32),
             pltpu.VMEM((32, 512), F32),
             pltpu.VMEM((128, 512), F32),
             pltpu.VMEM((128, 512), F32),
             pltpu.VMEM((256, 512), BF16),
+            pltpu.VMEM((32, 16, 128), F32),
         ],
         compiler_params=pltpu.CompilerParams(vmem_limit_bytes=VMEM_LIMIT),
         name="stencil",
@@ -408,9 +420,18 @@
         )
 
     def y_copies(g):
+        lanes = pl.ds(pl.multiple_of(g * 128, 128), 128)
         return (
-            remote(ext_ref.at[g, :, 32:40], ext_ref.at[g, :, 0:8], ysend.at[0, g], yrecv.at[0, g], place.right),
-            remote(ext_ref.at[g, :, 8:16], ext_ref.at[g, :, 40:48], ysend.at[1, g], yrecv.at[1, g], place.left),
+            remote(alpha_ref.at[:, 24:32, lanes], ext_ref.at[g, 4:12, 0:8], ysend.at[0, g], yrecv.at[0, g], place.right),
+            remote(alpha_ref.at[:, 0:8, lanes], ext_ref.at[g, 4:12, 40:48], ysend.at[1, g], yrecv.at[1, g], place.left),
+        )
+
+    def corner_copies(g):
+        return (
+            remote(ext_ref.at[g, 0:4, 32:40], ext_ref.at[g, 0:4, 0:8], ysend.at[2, g], yrecv.at[2, g], place.right),
+            remote(ext_ref.at[g, 0:4, 8:16], ext_ref.at[g, 0:4, 40:48], ysend.at[3, g], yrecv.at[3, g], place.left),
+            remote(ext_ref.at[g, 12:17, 32:40], ext_ref.at[g, 12:17, 0:8], ysend.at[4, g], yrecv.at[4, g], place.right),
+            remote(ext_ref.at[g, 12:17, 8:16], ext_ref.at[g, 12:17, 40:48], ysend.at[5, g], yrecv.at[5, g], place.left),
         )
 
     def own_copy(g):
@@ -424,7 +445,7 @@
     place.greet()
 
     def begin(g, carry):
-        for copy in x_copies(g):
+        for copy in x_copies(g) + y_copies(g):
             copy.start()
         own_copy(g).start()
         return carry
@@ -435,18 +456,19 @@
     route_ranks(cnt_ref, owner_ref, col_ref, lev_ref, frac_ref, inn_ref, rinv_ref, tgt_ref, high_ref, low_ref, term_ref)
     route_slots(high_ref, low_ref, term_ref, acc_ref, out_ref)
 
-    exchange.start()
     mix = mixing(lv_ref[...]).T
+    part_ref[...] = jnp.zeros_like(part_ref)
+    pert_copy.wait()
 
     def sideways(g):
         for copy in x_copies(g):
             copy.wait()
+        for copy in corner_copies(g):
+            copy.start()
+
+    def smooth(g):
         own_copy(g).wait()
-        for copy in y_copies(g):
-            copy.start()
-
-    def smooth(g):
-        for copy in y_copies(g):
+        for copy in y_copies(g) + corner_copies(g):
             copy.wait()
         field = ext_ref[g]
         for step in range(4):
@@ -454,44 +476,42 @@
         field = three(field[:, 8:48].reshape(9 * 40, 128), mix).reshape(9, 40, 128)
         for a in range(9):
             hi, lo = split(field[a])
-            turn_ref[pl.ds(pl.multiple_of(g * 128, 128), 128), a, :] = mm(jnp.concatenate([hi, lo], 0), sy_ref[...], TN)
+            turn_ref[:, a, :] = mm(jnp.concatenate([hi, lo], 0), sy_ref[...], TN)
+        for i in range(16):
+            hi, lo = split(turn_ref[8 * i:8 * i + 8].reshape(128, 128))
+            fine = mm(sx_ref[...], jnp.concatenate([hi, lo], 0)).reshape(8, 32, 128)
+            l0 = i % 4 * 8
+            part_ref[l0:l0 + 8] += fine * pert_ref[4 * g + i // 4, l0:l0 + 8].astype(F32)
 
     def both(g, carry):
         sideways(g)
+
+        @pl.when(g == CHUNKS - 1)
+        def _():
+            exchange.start()
+
         smooth(g - 1)
         return carry
 
     sideways(0)
     lax.fori_loop(1, CHUNKS, both, 0)
     smooth(CHUNKS - 1)
-    pert_copy.wait()
-
-    def block(b):
-        def member(k, carry):
-            hi, lo = split(turn_ref[pl.ds(k * 32 + 8 * b, 8)].reshape(128, 128))
-            fine = mm(sx_ref[...], jnp.concatenate([hi, lo], 0)).reshape(8, 32, 128)
-            return carry + fine * pert_ref[k, 8 * b:8 * b + 8].astype(F32)
-
-        part_ref[8 * b:8 * b + 8] = lax.fori_loop(0, 20, member, jnp.zeros((8, 32, 128), F32), unroll=4)
 
     extra = lambda at: bg_ref[at] * static_ref[at]
-    for s in range(BLOCKS + 3):
-        if s < BLOCKS:
-            block(s)
-            total.near(s).start()
-        if 0 <= s - 1 < BLOCKS:
-            total.second(s - 1)
-        if s == BLOCKS:
-            exchange.wait()
-            order_ref[...] = chunk_order(obs_ref)
-        if 0 <= s - 2 < BLOCKS:
-            total.third(s - 2, extra)
-        if 0 <= s - 3 < BLOCKS:
-            b = s - 3
-            total.last(b)
-            hi, lo = split(inc_ref[8 * b:8 * b + 8].reshape(256, 128).T)
-            table_ref[b, 0:128] = hi
-            table_ref[b, 128:256] = lo
+    for b in range(BLOCKS):
+        total.near(b).start()
+    for b in range(BLOCKS):
+        total.second(b)
+    exchange.wait()
+    order_ref[...] = chunk_order(obs_ref)
+    for b in range(BLOCKS):
+        total.third(b, extra)
+    for b in range(BLOCKS):
+        total.last(b)
+        hi, lo = split(inc_ref[8 * b:8 * b + 8].reshape(256, 128).T)
+        table_ref[0:128, 256 * b:256 * b + 256] = hi
+        table_ref[128:256, 256 * b:256 * b + 256] = lo
+    table_ref[:, 1024:1280] = jnp.zeros((256, 256), BF16)
 
 
 VMEM = pl.BlockSpec(memory_space=pltpu.VMEM)
@@ -504,7 +524,7 @@
     return pl.pallas_call(
         forward_kernel,
         out_shape=(
-            jax.ShapeDtypeStruct((BLOCKS, 256, 256), BF16),
+            jax.ShapeDtypeStruct((256, 1280), BF16),
             jax.ShapeDtypeStruct((GROUPS, 24, 128), F32),
             jax.ShapeDtypeStruct((8, 128), jnp.int32),
             jax.ShapeDtypeStruct((64, 128), jnp.int32),
@@ -515,14 +535,14 @@
             pltpu.VMEM((32, 32, 128), F32),
             pltpu.VMEM((CHUNKS, 17, 48, 128), F32),
             pltpu.VMEM(pert.shape, BF16),
-            pltpu.VMEM((640, 16, 128), F32),
+            pltpu.VMEM((128, 16, 128), F32),
             pltpu.VMEM((32, 32, 128), F32),
             pltpu.VMEM((GROUPS, 24, 128), F32),
             pltpu.VMEM((64, 128), jnp.int32),
             pltpu.VMEM((64, 128), jnp.int32),
             pltpu.VMEM((12, 64, 128), F32),
             pltpu.VMEM((128, 1536), F32),
-        ] + MEM_SCRATCH + [DMA((2, CHUNKS))] * 4 + [DMA((GROUPS,))] * 2 + [DMA((CHUNKS + 2,))],
+        ] + MEM_SCRATCH + [DMA((2, CHUNKS))] * 2 + [DMA((6, CHUNKS))] * 2 + [DMA((GROUPS,))] * 2 + [DMA((CHUNKS + 2,))],
         compiler_params=pltpu.CompilerParams(vmem_limit_bytes=VMEM_LIMIT, collective_id=0, has_side_effects=True),
         name="forward",
     )(cnt, owner, col, lev, frac, inn, rinv, alpha, pert, bg, static, lv, sy, sx)
@@ -562,7 +582,7 @@
     exchange.start()
     pert_copy.wait()
 
-    def block(b):
+    def block(b, start, count):
         fine_adj = full_ref[8 * b:8 * b + 8]
 
         def member(k, carry):
@@ -571,18 +591,24 @@
             turn_ref[pl.ds(k * 32 + 8 * b, 8)] = mm(gx_ref[...], jnp.concatenate([hi, lo], 0)).reshape(8, 16, 128)
             return carry
 
-        lax.fori_loop(0, 20, member, 0, unroll=4)
+        if count == 4:
+            for k in range(4):
+                member(start + k, 0)
+        else:
+            lax.fori_loop(start, start + count, member, 0, unroll=4)
 
     for s in range(BLOCKS + 1):
         if s < BLOCKS:
             total.third(s, lambda at: 0.0)
         if s >= 1:
             total.last(s - 1)
-            block(s - 1)
+            if s < BLOCKS:
+                block(s - 1, 0, 20)
 
     mix = mixing(lv_ref[...])
 
     def smooth(g, carry):
+        block(BLOCKS - 1, 4 * g, 4)
         rows = []
         for a in range(9):
             hi, lo = split(turn_ref[pl.ds(pl.multiple_of(g * 128, 128), 128), a, :])

time: 140 us -> 128 us (0.914)
  Pallas kernels: 138 us -> 126 us
    pallas_call x1, Pallas kernels: 35 us -> 26.2 us  [stencil(): pl.pallas_call(stencil_kernel, out_shape=(jax.ShapeDtypeStruct((32, 4, 12...]
    pallas_call x1, Pallas kernels: 58.4 us -> 52.1 us  [forward(): pl.pallas_call(forward_kernel, out_shape=(jax.ShapeDtypeStruct((256, 1280...]
    pallas_call x1, Pallas kernels: 42.2 us -> 45.3 us  [backward(): pl.pallas_call(backward_kernel, out_shape=(jax.ShapeDtypeStruct((8, 32, 6...]
where the time goes in v4:
time: 128 us
  Pallas kernels  126 us (98%)
  between operations  1.3 us (1%)
    pallas_call x1, Pallas kernels, forward(): pl.pallas_call(forward_kernel, out_shape=(jax.ShapeDtypeStruct((256, 1280...  52.1 us
    pallas_call x1, Pallas kernels, backward(): pl.pallas_call(backward_kernel, out_shape=(jax.ShapeDtypeStruct((8, 32, 6...  45.3 us
    pallas_call x1, Pallas kernels, stencil(): pl.pallas_call(stencil_kernel, out_shape=(jax.ShapeDtypeStruct((32, 4, 12...  26.2 us
    pallas_call x1, Pallas kernels, finish(): pl.pallas_call(finish_kernel, out_shape=tuple((jax.ShapeDtypeStruct(a.sha...  2.84 us

profile of v4, /device:TPU:0, one launch (start us, length us, event | category | flops | bytes accessed | tf_op | source)
XLA Modules:
  0.0 127.8 jit_solution(4207686837531303426)
XLA Ops:
  1.3 52.1 %forward.1 = (bf16[256,1280]{1,0:T(8,128)(2,1)}, f32[32,24,128]{2,1,0:T(8,128)}, s32[8,128]{1,0:T(8,128)}, s32[64,128]{1,0:T(8,128)}) custom-call(s32[1]{0:T(128)S(6)} %copy.19.cnt_ref, s32[64,128]{1,0:T(8,128)} %bitcast.8, s32[64,128]{1,0:T(8,128)} %bitcast.9, s32[64,128]{1,0:T(8,128)} %bitcast.10, f32[3,8192]{1,0:T(4,128)} %frac_ref.1, ...), custom_call_target="tpu_custom_call" | custom-call | tf_op jit(solution)/shard_map/forward/pallas_call | solution.py:524
  53.4 26.2 %stencil.1 = (f32[32,4,128]{2,1,0:T(4,128)}, f32[1024,128]{1,0:T(8,128)}) custom-call(s32[8,128]{1,0:T(8,128)} %get-tuple-element.15.order_ref, bf16[256,1280]{1,0:T(8,128)(2,1)} %get-tuple-element.16.table_ref, f32[32,24,128]{2,1,0:T(8,128)} %get-tuple-element.17.obs_ref), custom_call_target="tpu_custom_call" | custom-call | tf_op jit(solution)/shard_map/stencil/pallas_call | solution.py:154
  79.6 45.3 %backward.1 = (f32[8,32,640]{2,1,0:T(8,128)}, f32[32,32,128]{2,1,0:T(8,128)}, f32[64,128]{1,0:T(8,128)}) custom-call(f32[32,32,128]{2,1,0:T(8,128)} %bitcast.7, f32[32,4,128]{2,1,0:T(4,128)} %get-tuple-element.19.dep_ref, s32[64,128]{1,0:T(8,128)} %get-tuple-element.20.tgt_ref, bf16[20,32,32,128]{3,2,1,0:T(8,128)(2,1)} %pert_hbm.3, f32[32,32]{1,0:T(8,128)} %lv_ref.3, ...), custom_call_target="tpu_custom_call" | custom-call | tf_op jit(solution)/shard_map/backward/pallas_call | solution.py:655
  124.9 2.8 %finish.1 = (f32[8,32,640]{2,1,0:T(8,128)}, f32[32,32,128]{2,1,0:T(8,128)}, f32[64,128]{1,0:T(8,128)}) custom-call(f32[8,32,640]{2,1,0:T(8,128)} %alpha_ref.3, f32[8,32,640]{2,1,0:T(8,128)} %get-tuple-element.21.back_ref, f32[32,32,128]{2,1,0:T(8,128)} %bg_ref.3, f32[32,32,128]{2,1,0:T(8,128)} %static_ref.3, f32[32,32,128]{2,1,0:T(8,128)} %get-tuple-element.22.adj_ref, ...), custom_call_target="tpu_custom_call" | custom-call | tf_op jit(solution)/shard_map/finish/pallas_call | solution.py:686

commit v5 on v4

--- a/solution.py
+++ b/solution.py
@@ -222,7 +222,6 @@
 class Place:
     def __init__(self):
         self.tx, self.ty, self.mem = lax.axis_index("tx"), lax.axis_index("ty"), lax.axis_index("mem")
-        self.tile = self.tx * 4 + self.ty
         self.core = self.mem % 2
         self.below = (lax.rem(self.tx + 1, 8), self.ty, self.mem)
         self.above = (lax.rem(self.tx + 7, 8), self.ty, self.mem)
@@ -231,46 +230,54 @@
         self.twin = (self.tx, self.ty, self.mem + 1 - 2 * self.core)
         self.across = (self.tx, self.ty, lax.rem(self.mem + 2, 4))
 
+    def along_ty(self, d):
+        return (self.tx, lax.rem(self.ty + d, 4), self.mem)
+
+    def along_tx(self, d):
+        return (lax.rem(self.tx + d, 8), self.ty, self.mem)
+
     def greet(self):
         barrier = pltpu.get_barrier_semaphore()
-
-        def one(d, carry):
-            other = lax.rem(self.tile + d, GROUPS)
-            pl.semaphore_signal(barrier, inc=1, device_id=tile_id(other, self.mem), device_id_type=MESH)
-            return carry
-
-        lax.fori_loop(1, GROUPS, one, 0)
-        for other in (self.twin, self.across):
+        others = [self.along_tx(d) for d in range(1, 8)] + [self.along_ty(d) for d in range(1, 4)] + [self.twin, self.across]
+        for other in others:
             pl.semaphore_signal(barrier, inc=1, device_id=other, device_id_type=MESH)
-        pl.semaphore_wait(barrier, GROUPS + 1)
+        pl.semaphore_wait(barrier, len(others))
 
 
 class Exchange:
-    def __init__(self, place, src, dst, send, recv, own):
-        self.place, self.src, self.dst, self.send, self.recv = place, src, dst, send, recv
-        self.own = pltpu.make_async_copy(src.at[place.tile], dst.at[place.tile], own)
-
-    def copy(self, d):
-        other = lax.rem(self.place.tile + d, GROUPS)
-        return remote(self.src.at[other], self.dst.at[self.place.tile], self.send.at[d], self.recv.at[d], tile_id(other, self.place.mem))
+    def __init__(self, place, src, mid, dst, send, recv, own):
+        self.place, self.src, self.mid, self.dst, self.send, self.recv, self.own = place, src, mid, dst, send, recv, own
+
+    def first(self, d):
+        other = self.place.along_ty(d)
+        return remote(self.src.at[:, other[1]], self.mid.at[self.place.ty], self.send.at[d - 1], self.recv.at[d - 1], other)
+
+    def second(self, d):
+        other = self.place.along_tx(d)
+        return remote(self.mid.at[:, other[0]], self.dst.at[self.place.tx], self.send.at[d + 2], self.recv.at[d + 2], other)
+
+    def keep(self, at):
+        if at == 0:
+            return pltpu.make_async_copy(self.src.at[:, self.place.ty], self.mid.at[self.place.ty], self.own.at[0])
+        return pltpu.make_async_copy(self.mid.at[:, self.place.tx], self.dst.at[self.place.tx], self.own.at[1])
 
     def start(self):
-        self.own.start()
-
-        def one(d, carry):
-            self.copy(d).start()
-            return carry
-
-        lax.fori_loop(1, GROUPS, one, 0)
+        self.keep(0).start()
+        for d in range(1, 4):
+            self.first(d).start()
+
+    def turn(self):
+        self.keep(0).wait()
+        for d in range(1, 4):
+            self.first(d).wait()
+        self.keep(1).start()
+        for d in range(1, 8):
+            self.second(d).start()
 
     def wait(self):
-        self.own.wait()
-
-        def one(d, carry):
-            self.copy(d).wait()
-            return carry
-
-        lax.fori_loop(1, GROUPS, one, 0)
+        self.keep(1).wait()
+        for d in range(1, 8):
+            self.second(d).wait()
 
 
 class MemSum:
@@ -350,25 +357,28 @@
             term_ref[2 * at + 1, r:r + 1] = lo.astype(F32)
 
 
-def route_slots(high_ref, low_ref, term_ref, acc_ref, out_ref):
-    acc_ref[...] = jnp.zeros_like(acc_ref)
-
+def route_slots(start, count, high_ref, low_ref, term_ref, acc_ref):
     def one(c, carry):
-        def pair(ref, *at):
-            r = 2 * c
-            return jnp.concatenate([ref[(*at, pl.ds(r, 1), slice(None))], ref[(*at, pl.ds(r + 1, 1), slice(None))]], 1)
-
-        hit = jnp.where(iota((128, 256), 0) == pair(high_ref), 1.0, 0.0).astype(BF16)
-        lane = jnp.where(iota((128, 256), 0) == pair(low_ref), 1.0, 0.0).astype(BF16)
-        stack = jnp.concatenate([lane * pair(term_ref, t).astype(BF16) for t in range(12)], 0)
-        acc_ref[...] += mm(hit, stack, NT)
+        def line(ref, *at):
+            rows = ref[(*at, pl.ds(pl.multiple_of(8 * c, 8), 8), slice(None))]
+            return jnp.concatenate([rows[r:r + 1] for r in range(8)], 1)
+
+        hit = jnp.where(iota((128, 1024), 0) == line(high_ref), 1.0, 0.0).astype(BF16)
+        lane = jnp.where(iota((128, 1024), 0) == line(low_ref), 1.0, 0.0).astype(BF16)
+        for ch in range(6):
+            stack = jnp.concatenate([lane * line(term_ref, 2 * ch + t).astype(BF16) for t in range(2)], 0)
+            acc_ref[:, 256 * ch:256 * ch + 256] += mm(hit, stack, NT)
         return carry
 
-    lax.fori_loop(0, 32, one, 0, unroll=2)
+    lax.fori_loop(start, start + count, one, 0)
+
+
+def route_out(acc_ref, out_ref):
     for ch in range(6):
         full = acc_ref[:, 256 * ch:256 * ch + 128] + acc_ref[:, 256 * ch + 128:256 * ch + 256]
         for q in range(4):
-            out_ref[:, ch * 4 + q, :] = full[q * GROUPS:(q + 1) * GROUPS]
+            rows = full[q * GROUPS:(q + 1) * GROUPS].reshape(8, 4, 128)
+            out_ref[:, :, ch * 4 + q, :] = rows
 
 
 def unroute(tgt_ref, ret, out_ref):
@@ -406,59 +416,56 @@
 def forward_kernel(
     cnt_ref, owner_ref, col_ref, lev_ref, frac_ref, inn_ref, rinv_ref, alpha_ref, pert_hbm, bg_ref, static_ref, lv_ref, sy_ref, sx_ref,
     table_ref, obs_ref, order_ref, tgt_ref,
-    inc_ref, ext_ref, pert_ref, turn_ref, part_ref, out_ref, high_ref, low_ref, term_ref, acc_ref,
+    inc_ref, halo_ref, fromleft_ref, fromright_ref, mine_ref, pert_ref, turn_ref, part_ref, out_ref, mid_ref, high_ref, low_ref, term_ref, acc_ref,
     half_ref, got_ref, far_ref, msend, mrecv,
-    xsend, xrecv, ysend, yrecv, osend, orecv, own,
+    xsend, xrecv, ysend, yrecv, osend, orecv, around, own,
 ):
     place = Place()
 
     def x_copies(g):
         lanes = pl.ds(pl.multiple_of(g * 128, 128), 128)
         return (
-            remote(alpha_ref.at[4:8, :, lanes], ext_ref.at[g, 0:4, 8:40], xsend.at[0, g], xrecv.at[0, g], place.below),
-            remote(alpha_ref.at[0:5, :, lanes], ext_ref.at[g, 12:17, 8:40], xsend.at[1, g], xrecv.at[1, g], place.above),
+            remote(alpha_ref.at[4:8, :, lanes], halo_ref.at[g, 0:4, 8:40], xsend.at[0, g], xrecv.at[0, g], place.below),
+            remote(alpha_ref.at[0:5, :, lanes], halo_ref.at[g, 4:9, 8:40], xsend.at[1, g], xrecv.at[1, g], place.above),
         )
 
-    def y_copies(g):
-        lanes = pl.ds(pl.multiple_of(g * 128, 128), 128)
-        return (
-            remote(alpha_ref.at[:, 24:32, lanes], ext_ref.at[g, 4:12, 0:8], ysend.at[0, g], yrecv.at[0, g], place.right),
-            remote(alpha_ref.at[:, 0:8, lanes], ext_ref.at[g, 4:12, 40:48], ysend.at[1, g], yrecv.at[1, g], place.left),
-        )
+    y_copies = (
+        remote(alpha_ref.at[:, 24:32], fromleft_ref, ysend.at[0, CHUNKS], yrecv.at[0, CHUNKS], place.right),
+        remote(alpha_ref.at[:, 0:8], fromright_ref, ysend.at[1, CHUNKS], yrecv.at[1, CHUNKS], place.left),
+    )
 
     def corner_copies(g):
         return (
-            remote(ext_ref.at[g, 0:4, 32:40], ext_ref.at[g, 0:4, 0:8], ysend.at[2, g], yrecv.at[2, g], place.right),
-            remote(ext_ref.at[g, 0:4, 8:16], ext_ref.at[g, 0:4, 40:48], ysend.at[3, g], yrecv.at[3, g], place.left),
-            remote(ext_ref.at[g, 12:17, 32:40], ext_ref.at[g, 12:17, 0:8], ysend.at[4, g], yrecv.at[4, g], place.right),
-            remote(ext_ref.at[g, 12:17, 8:16], ext_ref.at[g, 12:17, 40:48], ysend.at[5, g], yrecv.at[5, g], place.left),
+            remote(halo_ref.at[g, :, 32:40], halo_ref.at[g, :, 0:8], ysend.at[0, g], yrecv.at[0, g], place.right),
+            remote(halo_ref.at[g, :, 8:16], halo_ref.at[g, :, 40:48], ysend.at[1, g], yrecv.at[1, g], place.left),
         )
 
-    def own_copy(g):
-        lanes = pl.ds(pl.multiple_of(g * 128, 128), 128)
-        return pltpu.make_async_copy(alpha_ref.at[:, :, lanes], ext_ref.at[g, 4:12, 8:40], own.at[g])
-
-    pert_copy = pltpu.make_async_copy(pert_hbm, pert_ref, own.at[CHUNKS])
-    exchange = Exchange(place, out_ref, obs_ref, osend, orecv, own.at[CHUNKS + 1])
+    own_copy = pltpu.make_async_copy(alpha_ref, mine_ref, own.at[0])
+    pert_copy = pltpu.make_async_copy(pert_hbm, pert_ref, own.at[1])
+    exchange = Exchange(place, out_ref, mid_ref, obs_ref, osend, orecv, around)
     total = MemSum(place, part_ref, inc_ref, half_ref, got_ref, far_ref, msend, mrecv)
 
     place.greet()
 
     def begin(g, carry):
-        for copy in x_copies(g) + y_copies(g):
+        for copy in x_copies(g):
             copy.start()
-        own_copy(g).start()
         return carry
 
     lax.fori_loop(0, CHUNKS, begin, 0)
+    for copy in y_copies:
+        copy.start()
+    own_copy.start()
     pert_copy.start()
     turn_ref[...] = jnp.zeros_like(turn_ref)
     route_ranks(cnt_ref, owner_ref, col_ref, lev_ref, frac_ref, inn_ref, rinv_ref, tgt_ref, high_ref, low_ref, term_ref)
-    route_slots(high_ref, low_ref, term_ref, acc_ref, out_ref)
-
+    acc_ref[...] = jnp.zeros_like(acc_ref)
     mix = mixing(lv_ref[...]).T
     part_ref[...] = jnp.zeros_like(part_ref)
+    own_copy.wait()
     pert_copy.wait()
+    for copy in y_copies:
+        copy.wait()
 
     def sideways(g):
         for copy in x_copies(g):
@@ -467,35 +474,48 @@
             copy.start()
 
     def smooth(g):
-        own_copy(g).wait()
-        for copy in y_copies(g) + corner_copies(g):
+        for copy in corner_copies(g):
             copy.wait()
-        field = ext_ref[g]
+        lanes = pl.ds(pl.multiple_of(g * 128, 128), 128)
+        center = jnp.concatenate([fromleft_ref[:, :, lanes], mine_ref[:, :, lanes], fromright_ref[:, :, lanes]], 1)
+        field = jnp.concatenate([halo_ref[g, 0:4], center, halo_ref[g, 4:9]], 0)
         for step in range(4):
             field = diffuse_rows(field)
         field = three(field[:, 8:48].reshape(9 * 40, 128), mix).reshape(9, 40, 128)
         for a in range(9):
             hi, lo = split(field[a])
             turn_ref[:, a, :] = mm(jnp.concatenate([hi, lo], 0), sy_ref[...], TN)
-        for i in range(16):
-            hi, lo = split(turn_ref[8 * i:8 * i + 8].reshape(128, 128))
-            fine = mm(sx_ref[...], jnp.concatenate([hi, lo], 0)).reshape(8, 32, 128)
-            l0 = i % 4 * 8
-            part_ref[l0:l0 + 8] += fine * pert_ref[4 * g + i // 4, l0:l0 + 8].astype(F32)
+        for b in range(BLOCKS):
+            at = slice(8 * b, 8 * b + 8)
+            sums = part_ref[at]
+            for k in range(4):
+                hi, lo = split(turn_ref[32 * k + 8 * b:32 * k + 8 * b + 8].reshape(128, 128))
+                fine = mm(sx_ref[...], jnp.concatenate([hi, lo], 0)).reshape(8, 32, 128)
+                sums = sums + fine * pert_ref[4 * g + k, at].astype(F32)
+            part_ref[at] = sums
+
+    sideways(0)
+    route_slots(0, 4, high_ref, low_ref, term_ref, acc_ref)
+    sideways(1)
+    route_slots(4, 4, high_ref, low_ref, term_ref, acc_ref)
+    sideways(2)
+    route_out(acc_ref, out_ref)
+    exchange.start()
 
     def both(g, carry):
-        sideways(g)
-
-        @pl.when(g == CHUNKS - 1)
+        @pl.when(g == 2)
         def _():
-            exchange.start()
-
-        smooth(g - 1)
+            exchange.turn()
+
+        smooth(g)
+
+        @pl.when(g < CHUNKS - 3)
+        def _():
+            sideways(g + 3)
+
         return carry
 
-    sideways(0)
-    lax.fori_loop(1, CHUNKS, both, 0)
-    smooth(CHUNKS - 1)
+    lax.fori_loop(0, CHUNKS, both, 0)
 
     extra = lambda at: bg_ref[at] * static_ref[at]
     for b in range(BLOCKS):
@@ -503,7 +523,7 @@
     for b in range(BLOCKS):
         total.second(b)
     exchange.wait()
-    order_ref[...] = chunk_order(obs_ref)
+    order_ref[...] = chunk_order(obs_ref[...].reshape(GROUPS, 24, 128))
     for b in range(BLOCKS):
         total.third(b, extra)
     for b in range(BLOCKS):
@@ -525,7 +545,7 @@
         forward_kernel,
         out_shape=(
             jax.ShapeDtypeStruct((256, 1280), BF16),
-            jax.ShapeDtypeStruct((GROUPS, 24, 128), F32),
+            jax.ShapeDtypeStruct((8, 4, 24, 128), F32),
             jax.ShapeDtypeStruct((8, 128), jnp.int32),
             jax.ShapeDtypeStruct((64, 128), jnp.int32),
         ),
@@ -533,16 +553,20 @@
         out_specs=(VMEM,) * 4,
         scratch_shapes=[
             pltpu.VMEM((32, 32, 128), F32),
-            pltpu.VMEM((CHUNKS, 17, 48, 128), F32),
+            pltpu.VMEM((CHUNKS, 9, 48, 128), F32),
+            pltpu.VMEM((8, 8, 640), F32),
+            pltpu.VMEM((8, 8, 640), F32),
+            pltpu.VMEM((8, 32, 640), F32),
             pltpu.VMEM(pert.shape, BF16),
             pltpu.VMEM((128, 16, 128), F32),
             pltpu.VMEM((32, 32, 128), F32),
-            pltpu.VMEM((GROUPS, 24, 128), F32),
+            pltpu.VMEM((8, 4, 24, 128), F32),
+            pltpu.VMEM((4, 8, 24, 128), F32),
             pltpu.VMEM((64, 128), jnp.int32),
             pltpu.VMEM((64, 128), jnp.int32),
             pltpu.VMEM((12, 64, 128), F32),
             pltpu.VMEM((128, 1536), F32),
-        ] + MEM_SCRATCH + [DMA((2, CHUNKS))] * 2 + [DMA((6, CHUNKS))] * 2 + [DMA((GROUPS,))] * 2 + [DMA((CHUNKS + 2,))],
+        ] + MEM_SCRATCH + [DMA((2, CHUNKS))] * 2 + [DMA((2, CHUNKS + 1))] * 2 + [DMA((10,))] * 2 + [DMA((2,)), DMA((2,))],
         compiler_params=pltpu.CompilerParams(vmem_limit_bytes=VMEM_LIMIT, collective_id=0, has_side_effects=True),
         name="forward",
     )(cnt, owner, col, lev, frac, inn, rinv, alpha, pert, bg, static, lv, sy, sx)
@@ -551,9 +575,9 @@
 def backward_kernel(
     adj_ref, dep_ref, tgt_ref, pert_hbm, lv_ref, gy_ref, gx_ref,
     grad_ref, full_ref, depout_ref,
-    pert_ref, turn_ref, wide_ref, fromleft_ref, fromright_ref, fromabove_ref, frombelow_ref, ret_ref,
+    pert_ref, turn_ref, wide_ref, fromleft_ref, fromright_ref, fromabove_ref, frombelow_ref, mid_ref, ret_ref,
     half_ref, got_ref, far_ref, msend, mrecv,
-    xsend, xrecv, ysend, yrecv, osend, orecv, own,
+    xsend, xrecv, ysend, yrecv, osend, orecv, around, own,
 ):
     place = Place()
 
@@ -570,7 +594,7 @@
         )
 
     pert_copy = pltpu.make_async_copy(pert_hbm, pert_ref, own.at[0])
-    exchange = Exchange(place, dep_ref, ret_ref, osend, orecv, own.at[1])
+    exchange = Exchange(place, dep_ref, mid_ref, ret_ref, osend, orecv, around)
     total = MemSum(place, adj_ref, full_ref, half_ref, got_ref, far_ref, msend, mrecv)
 
     place.greet()
@@ -605,6 +629,7 @@
             if s < BLOCKS:
                 block(s - 1, 0, 20)
 
+    exchange.turn()
     mix = mixing(lv_ref[...])
 
     def smooth(g, carry):
@@ -669,8 +694,9 @@
             pltpu.VMEM((CHUNKS, 17, 8, 128), F32),
             pltpu.VMEM((CHUNKS, 5, 32, 128), F32),
             pltpu.VMEM((CHUNKS, 4, 32, 128), F32),
-            pltpu.VMEM((GROUPS, 4, 128), F32),
-        ] + MEM_SCRATCH + [DMA((2, CHUNKS))] * 4 + [DMA((GROUPS,))] * 2 + [DMA((2,))],
+            pltpu.VMEM((4, 8, 4, 128), F32),
+            pltpu.VMEM((8, 4, 4, 128), F32),
+        ] + MEM_SCRATCH + [DMA((2, CHUNKS))] * 4 + [DMA((10,))] * 2 + [DMA((2,)), DMA((1,))],
         compiler_params=pltpu.CompilerParams(vmem_limit_bytes=VMEM_LIMIT, collective_id=1, has_side_effects=True),
         name="backward",
     )(adj, dep, tgt, pert, lv, gy, gx)
@@ -700,8 +726,8 @@
         obs_count, obs_owner.reshape(shape), obs_column.reshape(shape), obs_level.reshape(shape), obs_frac,
         innovation.reshape(shape), obs_rinv.reshape(shape), alpha, ens_pert, bg_sigma, static_ctrl, lv_sqrt, spread_y, spread_x,
     )
-    departure, adjoint = stencil(order, table, incoming)
-    back, adjoint, departures = backward(adjoint.reshape(32, 32, 128), departure, target, ens_pert, lv_sqrt, gather_y, gather_x)
+    departure, adjoint = stencil(order, table, incoming.reshape(GROUPS, 24, 128))
+    back, adjoint, departures = backward(adjoint.reshape(32, 32, 128), departure.reshape(8, 4, 4, 128), target, ens_pert, lv_sqrt, gather_y, gather_x)
     grad_alpha, grad_static, departures = finish(alpha, back, bg_sigma, static_ctrl, adjoint, departures)
     return grad_alpha, grad_static, departures.reshape(-1)
 

time: 128 us -> 123 us (0.961)
  Pallas kernels: 126 us -> 121 us
    pallas_call x1, Pallas kernels: 52.1 us -> 49.1 us  [forward(): pl.pallas_call(forward_kernel, out_shape=(jax.ShapeDtypeStruct((256, 1280...]
    pallas_call x1, Pallas kernels: 45.3 us -> 43.3 us  [backward(): pl.pallas_call(backward_kernel, out_shape=(jax.ShapeDtypeStruct((8, 32, 6...]
where the time goes in v5:
time: 123 us
  Pallas kernels  121 us (98%)
  between operations  1.3 us (1%)
    pallas_call x1, Pallas kernels, forward(): pl.pallas_call(forward_kernel, out_shape=(jax.ShapeDtypeStruct((256, 1280...  49.1 us
    pallas_call x1, Pallas kernels, backward(): pl.pallas_call(backward_kernel, out_shape=(jax.ShapeDtypeStruct((8, 32, 6...  43.3 us
    pallas_call x1, Pallas kernels, stencil(): pl.pallas_call(stencil_kernel, out_shape=(jax.ShapeDtypeStruct((32, 4, 12...  26 us
    pallas_call x1, Pallas kernels, finish(): pl.pallas_call(finish_kernel, out_shape=tuple((jax.ShapeDtypeStruct(a.sha...  2.84 us

profile of v5, /device:TPU:0, one launch (start us, length us, event | category | flops | bytes accessed | tf_op | source)
XLA Modules:
  0.0 122.6 jit_solution(18283094750272210097)
XLA Ops:
  1.3 49.1 %forward.1 = (bf16[256,1280]{1,0:T(8,128)(2,1)}, f32[8,4,24,128]{3,2,1,0:T(8,128)}, s32[8,128]{1,0:T(8,128)}, s32[64,128]{1,0:T(8,128)}) custom-call(s32[1]{0:T(128)S(6)} %copy.19.cnt_ref, s32[64,128]{1,0:T(8,128)} %bitcast.12, s32[64,128]{1,0:T(8,128)} %bitcast.13, s32[64,128]{1,0:T(8,128)} %bitcast.14, f32[3,8192]{1,0:T(4,128)} %frac_ref.1, ...), custom_call_target="tpu_custom_call" | custom-call | tf_op jit(solution)/shard_map/forward/pallas_call | solution.py:544
  50.4 26.0 %stencil.1 = (f32[32,4,128]{2,1,0:T(4,128)}, f32[1024,128]{1,0:T(8,128)}) custom-call(s32[8,128]{1,0:T(8,128)} %get-tuple-element.15.order_ref, bf16[256,1280]{1,0:T(8,128)(2,1)} %get-tuple-element.16.table_ref, f32[32,24,128]{2,1,0:T(8,128)} %bitcast.10), custom_call_target="tpu_custom_call" | custom-call | tf_op jit(solution)/shard_map/stencil/pallas_call | solution.py:154
  76.4 43.3 %backward.1 = (f32[8,32,640]{2,1,0:T(8,128)}, f32[32,32,128]{2,1,0:T(8,128)}, f32[64,128]{1,0:T(8,128)}) custom-call(f32[32,32,128]{2,1,0:T(8,128)} %bitcast.9, f32[8,4,4,128]{3,2,1,0:T(4,128)} %bitcast.11, s32[64,128]{1,0:T(8,128)} %get-tuple-element.20.tgt_ref, bf16[20,32,32,128]{3,2,1,0:T(8,128)(2,1)} %pert_hbm.3, f32[32,32]{1,0:T(8,128)} %lv_ref.3, ...), custom_call_target="tpu_custom_call" | custom-call | tf_op jit(solution)/shard_map/backward/pallas_call | solution.py:680
  119.7 2.8 %finish.1 = (f32[8,32,640]{2,1,0:T(8,128)}, f32[32,32,128]{2,1,0:T(8,128)}, f32[64,128]{1,0:T(8,128)}) custom-call(f32[8,32,640]{2,1,0:T(8,128)} %alpha_ref.3, f32[8,32,640]{2,1,0:T(8,128)} %get-tuple-element.21.back_ref, f32[32,32,128]{2,1,0:T(8,128)} %bg_ref.3, f32[32,32,128]{2,1,0:T(8,128)} %static_ref.3, f32[32,32,128]{2,1,0:T(8,128)} %get-tuple-element.22.adj_ref, ...), custom_call_target="tpu_custom_call" | custom-call | tf_op jit(solution)/shard_map/finish/pallas_call | solution.py:712

commit v6 on v5

--- a/solution.py
+++ b/solution.py
@@ -236,11 +236,12 @@
     def along_tx(self, d):
         return (lax.rem(self.tx + d, 8), self.ty, self.mem)
 
-    def greet(self):
+    def greet(self, meanwhile):
         barrier = pltpu.get_barrier_semaphore()
         others = [self.along_tx(d) for d in range(1, 8)] + [self.along_ty(d) for d in range(1, 4)] + [self.twin, self.across]
         for other in others:
             pl.semaphore_signal(barrier, inc=1, device_id=other, device_id_type=MESH)
+        meanwhile()
         pl.semaphore_wait(barrier, len(others))
 
 
@@ -445,7 +446,14 @@
     exchange = Exchange(place, out_ref, mid_ref, obs_ref, osend, orecv, around)
     total = MemSum(place, part_ref, inc_ref, half_ref, got_ref, far_ref, msend, mrecv)
 
-    place.greet()
+    def meanwhile():
+        own_copy.start()
+        pert_copy.start()
+        turn_ref[...] = jnp.zeros_like(turn_ref)
+        acc_ref[...] = jnp.zeros_like(acc_ref)
+        part_ref[...] = jnp.zeros_like(part_ref)
+
+    place.greet(meanwhile)
 
     def begin(g, carry):
         for copy in x_copies(g):
@@ -455,13 +463,8 @@
     lax.fori_loop(0, CHUNKS, begin, 0)
     for copy in y_copies:
         copy.start()
-    own_copy.start()
-    pert_copy.start()
-    turn_ref[...] = jnp.zeros_like(turn_ref)
     route_ranks(cnt_ref, owner_ref, col_ref, lev_ref, frac_ref, inn_ref, rinv_ref, tgt_ref, high_ref, low_ref, term_ref)
-    acc_ref[...] = jnp.zeros_like(acc_ref)
     mix = mixing(lv_ref[...]).T
-    part_ref[...] = jnp.zeros_like(part_ref)
     own_copy.wait()
     pert_copy.wait()
     for copy in y_copies:
@@ -597,10 +600,9 @@
     exchange = Exchange(place, dep_ref, mid_ref, ret_ref, osend, orecv, around)
     total = MemSum(place, adj_ref, full_ref, half_ref, got_ref, far_ref, msend, mrecv)
 
-    place.greet()
+    place.greet(pert_copy.start)
     for b in range(BLOCKS):
         total.near(b).start()
-    pert_copy.start()
     for b in range(BLOCKS):
         total.second(b)
     exchange.start()

time: 123 us -> 123 us (level)
    pallas_call x1, Pallas kernels: 43.3 us -> 40.3 us  [backward(): pl.pallas_call(backward_kernel, out_shape=(jax.ShapeDtypeStruct((8, 32, 6...]
    pallas_call x1, Pallas kernels: 26 us -> 28.7 us  [stencil(): pl.pallas_call(stencil_kernel, out_shape=(jax.ShapeDtypeStruct((32, 4, 12...]
where the time goes in v6:
time: 123 us; the launch traced here: 122 us
  Pallas kernels  121 us (98%)
  between operations  1.3 us (1%)
    pallas_call x1, Pallas kernels, forward(): pl.pallas_call(forward_kernel, out_shape=(jax.ShapeDtypeStruct((256, 1280...  49.1 us
    pallas_call x1, Pallas kernels, backward(): pl.pallas_call(backward_kernel, out_shape=(jax.ShapeDtypeStruct((8, 32, 6...  40.3 us
    pallas_call x1, Pallas kernels, stencil(): pl.pallas_call(stencil_kernel, out_shape=(jax.ShapeDtypeStruct((32, 4, 12...  28.7 us
    pallas_call x1, Pallas kernels, finish(): pl.pallas_call(finish_kernel, out_shape=tuple((jax.ShapeDtypeStruct(a.sha...  2.84 us

profile of v6, /device:TPU:0, one launch (start us, length us, event | category | flops | bytes accessed | tf_op | source)
XLA Modules:
  0.0 122.3 jit_solution(13736492313524938755)
XLA Ops:
  1.3 49.1 %forward.1 = (bf16[256,1280]{1,0:T(8,128)(2,1)}, f32[8,4,24,128]{3,2,1,0:T(8,128)}, s32[8,128]{1,0:T(8,128)}, s32[64,128]{1,0:T(8,128)}) custom-call(s32[1]{0:T(128)S(6)} %copy.19.cnt_ref, s32[64,128]{1,0:T(8,128)} %bitcast.12, s32[64,128]{1,0:T(8,128)} %bitcast.13, s32[64,128]{1,0:T(8,128)} %bitcast.14, f32[3,8192]{1,0:T(4,128)} %frac_ref.1, ...), custom_call_target="tpu_custom_call" | custom-call | tf_op jit(solution)/shard_map/forward/pallas_call | solution.py:547
  50.4 28.7 %stencil.1 = (f32[32,4,128]{2,1,0:T(4,128)}, f32[1024,128]{1,0:T(8,128)}) custom-call(s32[8,128]{1,0:T(8,128)} %get-tuple-element.15.order_ref, bf16[256,1280]{1,0:T(8,128)(2,1)} %get-tuple-element.16.table_ref, f32[32,24,128]{2,1,0:T(8,128)} %bitcast.10), custom_call_target="tpu_custom_call" | custom-call | tf_op jit(solution)/shard_map/stencil/pallas_call | solution.py:154
  79.1 40.3 %backward.1 = (f32[8,32,640]{2,1,0:T(8,128)}, f32[32,32,128]{2,1,0:T(8,128)}, f32[64,128]{1,0:T(8,128)}) custom-call(f32[32,32,128]{2,1,0:T(8,128)} %bitcast.9, f32[8,4,4,128]{3,2,1,0:T(4,128)} %bitcast.11, s32[64,128]{1,0:T(8,128)} %get-tuple-element.20.tgt_ref, bf16[20,32,32,128]{3,2,1,0:T(8,128)(2,1)} %pert_hbm.3, f32[32,32]{1,0:T(8,128)} %lv_ref.3, ...), custom_call_target="tpu_custom_call" | custom-call | tf_op jit(solution)/shard_map/backward/pallas_call | solution.py:682
  119.4 2.8 %finish.1 = (f32[8,32,640]{2,1,0:T(8,128)}, f32[32,32,128]{2,1,0:T(8,128)}, f32[64,128]{1,0:T(8,128)}) custom-call(f32[8,32,640]{2,1,0:T(8,128)} %alpha_ref.3, f32[8,32,640]{2,1,0:T(8,128)} %get-tuple-element.21.back_ref, f32[32,32,128]{2,1,0:T(8,128)} %bg_ref.3, f32[32,32,128]{2,1,0:T(8,128)} %static_ref.3, f32[32,32,128]{2,1,0:T(8,128)} %get-tuple-element.22.adj_ref, ...), custom_call_target="tpu_custom_call" | custom-call | tf_op jit(solution)/shard_map/finish/pallas_call | solution.py:714
